TPU v7x, 128 devices: a whole 4x4x4 slice. The times are simulated.
128 devices in a mesh: row: 32 (over x, y, core), col: 4 (over z).
Axes of the slice: x: 4, y: 4, z: 4, core: 2. Of those that a mesh axis runs over, the one named last changes fastest.
Arguments:
- coeffs: bfloat16 [4096, 1024], P('row', 'col'), may hold values from -0.09375 to 0.09375
- coef_pattern: int32 [32, 8], replicated, may hold values 0 or 1
- keep_density: int32 [2, 32, 32], replicated, may hold values 0 or 1
- keep_square: int32 [2, 32, 32], replicated, may hold values 0 or 1
Outputs:
- density: float32 [4096, 4096], P('row', 'col')
All inputs are finite; a program needn't handle non-finite values.
Results may differ from a plain program's by a relative error of at most 0.0042.
Values may be sent and summed in bfloat16 or wider, within the bound.
No kernel may reach another device: no remote copies, remote signals or barrier semaphores. Data moves between devices by JAX's collectives and lax.ppermute only.
A program may use at most 64 MiB of HBM per device.

v0:
```python
import jax
import jax.numpy as jnp
from jax import lax
from jax.sharding import PartitionSpec as P

B = 128


def widen(blocks):
    return jnp.repeat(jnp.repeat(blocks, B, 0), B, 1)


def local_blocks(table, row_width, col_width):
    row_start = lax.axis_index("row") * (row_width // B)
    col_start = lax.axis_index("col") * (col_width // B)
    part = lax.dynamic_slice(table, (row_start, col_start), (row_width // B, col_width // B))
    return widen(part).astype(jnp.float32)


def body(coeffs, coef_pattern, keep_density, keep_square):
    rows, width = coeffs.shape
    kept = coeffs * local_blocks(coef_pattern, rows, width).astype(jnp.bfloat16)
    terms = lax.dot_general(
        kept,
        lax.all_gather(kept, "row", axis=0, tiled=True),
        (((1,), (1,)), ((), ())),
        preferred_element_type=jnp.float32,
    )
    density = lax.psum_scatter(terms, "col", scatter_dimension=1, tiled=True)
    cols = density.shape[1]
    for step in range(keep_density.shape[0]):
        mask_density = local_blocks(keep_density[step], rows, cols)
        mask_square = local_blocks(keep_square[step], rows, cols)
        current = (density * mask_density).astype(jnp.bfloat16)
        full_rows = lax.all_gather(current, "col", axis=1, tiled=True)
        panel = lax.all_gather(current, "row", axis=0, tiled=True)
        square = jnp.dot(full_rows, panel, preferred_element_type=jnp.float32)
        square = square * mask_square
        square_low = square.astype(jnp.bfloat16)
        square_full = lax.all_gather(square_low, "col", axis=1, tiled=True)
        cube = jnp.dot(square_full, panel, preferred_element_type=jnp.float32)
        density = 3.0 * square - 2.0 * cube
    return density


def solution(mesh):
    placed = (P("row", "col"), P(), P(), P())
    return jax.shard_map(
        body, mesh=mesh, in_specs=placed, out_specs=P("row", "col"), check_vma=False
    )
```

profile of v0, /device:TPU:1, one launch (start us, length us, event | category | flops | bytes accessed | tf_op | source)
XLA Modules:
  0.0 328.3 jit_solution(4905271148094593431)
XLA Ops:
  6.5 0.0 all-gather.8.cloned.1.call-start
  6.5 0.9 fusion.12
  7.4 0.1 broadcast_bitcast_fusion.4
  7.5 1.5 broadcast_multiply_fusion
  9.0 0.0 all-gather.8.cloned.1.call-update
  9.0 0.0 reduce-scatter.2.cloned.1.call-start
  9.0 47.9 %all-gather.8.cloned.1.call-done = bf16[4096,256]{1,0:T(8,128)(2,1)} async-done(((bf16[128,256]{1,0:T(8,128)(2,1)}), bf16[4096,256]{1,0:T(8,128)(2,1)}) %all-gather.8.cloned.1.call-update) | async-done | bytes 2097168 | tf_op jit(solution)/shard_map/all_gather | solution.py:25
  57.0 3.8 %fusion.17 = f32[128,4096]{1,0:T(8,128)} fusion(bf16[128,256]{1,0:T(8,128)(2,1)} %broadcast_multiply_fusion, bf16[4096,256]{1,0:T(8,128)(2,1)} %all-gather.8.cloned.1.call-done), kind=kOutput, calls=%fused_computation.33 | convolution fusion | flops 268435456 | bytes 4259840 | tf_op jit(solution)/shard_map/dot_general | solution.py:23
  60.8 0.0 reduce-scatter.2.cloned.1.call-update
  60.8 0.0 all-gather.10.cloned.1.call-start
  60.8 0.7 fusion.14
  61.6 0.1 fusion.5
  61.7 0.1 broadcast_bitcast_fusion.3
  61.7 28.0 %reduce-scatter.2.cloned.1.call-done = f32[128,1024]{1,0:T(8,128)} async-done(((f32[128,4096]{1,0:T(8,128)}), f32[128,1024]{1,0:T(8,128)}) %reduce-scatter.2.cloned.1.call-update) | async-done | bytes 524304 | tf_op jit(solution)/shard_map/reduce_scatter | solution.py:29
  89.8 1.8 multiply_convert_fusion
  91.5 0.0 all-gather.10.cloned.1.call-update
  91.6 0.0 all-gather.12.cloned.1.call-start
  91.6 0.5 all-gather.12.cloned.1.call-update
  92.1 0.0 all-gather.14.cloned.1.call-start
  92.2 0.7 fusion.13
  92.9 0.1 fusion.7
  93.0 0.1 broadcast_bitcast_fusion.2
  93.1 21.4 %all-gather.10.cloned.1.call-done = bf16[128,4096]{1,0:T(8,128)(2,1)} async-done(((bf16[128,1024]{1,0:T(8,128)(2,1)}), bf16[128,4096]{1,0:T(8,128)(2,1)}) %all-gather.10.cloned.1.call-update) | async-done | bytes 1048592 | tf_op jit(solution)/shard_map/all_gather | solution.py:35
  114.5 56.9 %all-gather.12.cloned.1.call-done = bf16[4096,1024]{1,0:T(8,128)(2,1)} async-done(((bf16[128,1024]{1,0:T(8,128)(2,1)}), bf16[4096,1024]{1,0:T(8,128)(2,1)}) %all-gather.12.cloned.1.call-update) | async-done | bytes 8388624 | tf_op jit(solution)/shard_map/all_gather | solution.py:36
  171.4 5.7 %fusion.15 = (bf16[128,1024]{1,0:T(8,128)(2,1)}, f32[128,1024]{1,0:T(8,128)S(1)}) fusion(f32[1024]{0:T(1024)S(1)} %broadcast_bitcast_fusion.2, bf16[128,4096]{1,0:T(8,128)(2,1)} %all-gather.10.cloned.1.call-done, bf16[4096,1024]{1,0:T(8,128)(2,1)} %all-gather.12.cloned.1.call-done), kind=kOutput, calls=%fused_computation.31 | convolution fusion | flops 1074003968 | bytes 10227712 | tf_op jit(solution)/shard_map/dot_general | solution.py:37
  177.1 0.0 all-gather.14.cloned.1.call-update
  177.1 0.0 all-gather.16.cloned.1.call-start
  177.2 0.1 fusion.9
  177.2 0.1 broadcast_bitcast_fusion.1
  177.3 22.4 %all-gather.14.cloned.1.call-done = bf16[128,4096]{1,0:T(8,128)(2,1)} async-done(((bf16[128,1024]{1,0:T(8,128)(2,1)}), bf16[128,4096]{1,0:T(8,128)(2,1)}) %all-gather.14.cloned.1.call-update) | async-done | bytes 1048592 | tf_op jit(solution)/shard_map/all_gather | solution.py:40
  199.8 5.7 %fusion.3 = bf16[128,1024]{1,0:T(8,128)(2,1)} fusion(bf16[128,4096]{1,0:T(8,128)(2,1)} %all-gather.14.cloned.1.call-done, bf16[4096,1024]{1,0:T(8,128)(2,1)} %all-gather.12.cloned.1.call-done, f32[128,1024]{1,0:T(8,128)S(1)} %get-tuple-element.10, f32[1024]{0:T(1024)S(1)} %broadcast_bitcast_fusion.1), kind=kOutput, calls=%fused_computation.7 | convolution fusion | flops 1074397184 | bytes 10227712 | tf_op jit(solution)/shard_map/dot_general | solution.py:41
  205.5 0.0 all-gather.16.cloned.1.call-update
  205.5 0.0 all-gather.18.cloned.1.call-start
  205.6 0.7 all-gather.18.cloned.1.call-update
  206.3 0.0 all-gather.20.cloned.1.call-start
  206.3 0.1 fusion.11
  206.4 0.1 broadcast_bitcast_fusion
  206.5 23.8 %all-gather.16.cloned.1.call-done = bf16[128,4096]{1,0:T(8,128)(2,1)} async-done(((bf16[128,1024]{1,0:T(8,128)(2,1)}), bf16[128,4096]{1,0:T(8,128)(2,1)}) %all-gather.16.cloned.1.call-update) | async-done | bytes 1048592 | tf_op jit(solution)/shard_map/all_gather | solution.py:35
  230.3 57.0 %all-gather.18.cloned.1.call-done = bf16[4096,1024]{1,0:T(8,128)(2,1)} async-done(((bf16[128,1024]{1,0:T(8,128)(2,1)}), bf16[4096,1024]{1,0:T(8,128)(2,1)}) %all-gather.18.cloned.1.call-update) | async-done | bytes 8388624 | tf_op jit(solution)/shard_map/all_gather | solution.py:36
  287.3 5.7 %fusion.16 = (bf16[128,1024]{1,0:T(8,128)(2,1)}, f32[128,1024]{1,0:T(8,128)S(1)}) fusion(f32[1024]{0:T(1024)S(1)} %broadcast_bitcast_fusion, bf16[128,4096]{1,0:T(8,128)(2,1)} %all-gather.16.cloned.1.call-done, bf16[4096,1024]{1,0:T(8,128)(2,1)} %all-gather.18.cloned.1.call-done), kind=kOutput, calls=%fused_computation.32 | convolution fusion | flops 1074003968 | bytes 10227712 | tf_op jit(solution)/shard_map/dot_general | solution.py:37
  293.0 0.0 all-gather.20.cloned.1.call-update
  293.0 22.6 %all-gather.20.cloned.1.call-done = bf16[128,4096]{1,0:T(8,128)(2,1)} async-done(((bf16[128,1024]{1,0:T(8,128)(2,1)}), bf16[128,4096]{1,0:T(8,128)(2,1)}) %all-gather.20.cloned.1.call-update) | async-done | bytes 1048592 | tf_op jit(solution)/shard_map/all_gather | solution.py:40
  315.7 5.8 %fusion.2 = f32[128,1024]{1,0:T(8,128)} fusion(bf16[128,4096]{1,0:T(8,128)(2,1)} %all-gather.20.cloned.1.call-done, bf16[4096,1024]{1,0:T(8,128)(2,1)} %all-gather.18.cloned.1.call-done, f32[128,1024]{1,0:T(8,128)S(1)} %get-tuple-element.12), kind=kOutput, calls=%fused_computation.6 | convolution fusion | flops 1074135040 | bytes 10485760 | tf_op jit(solution)/shard_map/dot_general | solution.py:41
Async XLA Ops:
  6.5 50.5 %all-gather.8.cloned.1.call-start = ((), (), s32[]{:S(2)}) async-start(), calls=%async_computation.1 | async-start | bytes 2162688 | tf_op jit(solution)/shard_map/all_gather | solution.py:25
  9.0 80.8 %reduce-scatter.2.cloned.1.call-start = ((), (), s32[]{:S(2)}) async-start(), calls=%async_computation.2 | async-start | bytes 2621440 | tf_op jit(solution)/shard_map/reduce_scatter | solution.py:29
  60.8 53.7 %all-gather.10.cloned.1.call-start = ((), (), s32[]{:S(2)}) async-start(), calls=%async_computation.3 | async-start | bytes 1310720 | tf_op jit(solution)/shard_map/all_gather | solution.py:35
  91.6 79.8 %all-gather.12.cloned.1.call-start = ((), (), s32[]{:S(2)}) async-start(), calls=%async_computation.4 | async-start | bytes 8650752 | tf_op jit(solution)/shard_map/all_gather | solution.py:36
  92.1 107.6 %all-gather.14.cloned.1.call-start = ((), (), s32[]{:S(2)}) async-start(), calls=%async_computation.5 | async-start | bytes 1310720 | tf_op jit(solution)/shard_map/all_gather | solution.py:40
  177.1 53.2 %all-gather.16.cloned.1.call-start = ((), (), s32[]{:S(2)}) async-start(), calls=%async_computation.6 | async-start | bytes 1310720 | tf_op jit(solution)/shard_map/all_gather | solution.py:35
  205.5 81.8 %all-gather.18.cloned.1.call-start = ((), (), s32[]{:S(2)}) async-start(), calls=%async_computation.7 | async-start | bytes 8650752 | tf_op jit(solution)/shard_map/all_gather | solution.py:36
  206.3 109.4 %all-gather.20.cloned.1.call-start = ((), (), s32[]{:S(2)}) async-start(), calls=%async_computation.8 | async-start | bytes 1310720 | tf_op jit(solution)/shard_map/all_gather | solution.py:40
Sparse Core Ops, SparseCore 0:
  9.6 47.3 all-gather.7
  60.9 28.8 reduce-scatter.1
  91.7 22.7 all-gather.9
  116.9 54.4 all-gather.11
  177.2 22.4 all-gather.13
  205.6 24.6 all-gather.15
  232.8 54.4 all-gather.17
  293.1 22.4 all-gather.19
where the time goes:
time: 329 us; the launch traced here: 328 us
  waiting for transfers between devices  282 us (86%)
  matrix products  26.6 us (8%)
  between operations  13.5 us (4%)
  other arithmetic  4.45 us (1%)
    all_gather x2, waiting for transfers between devices, body(): panel = lax.all_gather(current, 'row', axis=0, tiled=True)  114 us
    all_gather x1, waiting for transfers between devices, body(): lax.all_gather(kept, 'row', axis=0, tiled=True)  47.9 us
    all_gather x2, waiting for transfers between devices, body(): full_rows = lax.all_gather(current, 'col', axis=1, tiled=True)  45.3 us
    all_gather x2, waiting for transfers between devices, body(): square_full = lax.all_gather(square_low, 'col', axis=1, tiled=True)  45.1 us
    reduce_scatter x1, waiting for transfers between devices, body(): density = lax.psum_scatter(terms, 'col', scatter_dimension=1, tiled=True)  28 us
    dot_general x2, matrix products, body(): cube = jnp.dot(square_full, panel, preferred_element_type=jnp.float32)  11.5 us
    dot_general x2, matrix products, body(): square = jnp.dot(full_rows, panel, preferred_element_type=jnp.float32)  11.4 us
  transfers between devices with their start and end apart: 8, of which 8 were waited for; matrix products, arithmetic and copies ran while one was open for 1% of the time, Pallas kernels for 0%

commit v1 on v0

v1 whole, which is shorter than its diff:
```python
import jax
import jax.numpy as jnp
from jax import lax
from jax.experimental import pallas as pl
from jax.experimental.pallas import tpu as pltpu
from jax.sharding import PartitionSpec as P

B = 128
N = 4096
K = 1024
ROWS = 256
COLS = 512
AXES = ("row", "col")
MIB = 1024 * 1024


def device(x, y, core, z):
    return (((x % 4) * 4 + y % 4) * 2 + core) * 4 + z % 4


def pairs(target):
    return [
        (device(x, y, core, z), device(*target(x, y, core, z)))
        for x in range(4) for y in range(4) for core in range(2) for z in range(4)
    ]


def other_core(a):
    return lax.ppermute(a, AXES, pairs(lambda x, y, core, z: (x, y, 1 - core, z)))


def from_z(a, d):
    return lax.ppermute(a, AXES, pairs(lambda x, y, core, z: (x, y, core, z - d)))


def from_first(a, d):
    return lax.ppermute(a, AXES, pairs(
        lambda x, y, core, z: (x - d, y, core, z) if core == 0 else (x, y - d, core, z)))


def from_second(a, d):
    return lax.ppermute(a, AXES, pairs(
        lambda x, y, core, z: (x, y - d, core, z) if core == 0 else (x - d, y, core, z)))


def gather_z(a):
    return [a] + [from_z(a, d) for d in (1, 3, 2)]


def by_offset(parts):
    own, one, three, two = parts
    return [own, one, two, three]


def gather_plane(a):
    line = jnp.concatenate(by_offset([a] + [from_first(a, d) for d in (1, 3, 2)]), axis=0)
    return by_offset([line] + [from_second(line, d) for d in (1, 3, 2)])


def place(x, y, kind, first, second):
    px = jnp.where(kind == 0, x + first, x + second) & 3
    py = jnp.where(kind == 0, y + second, y + first) & 3
    return px, py


def dot_t(a, b):
    return lax.dot_general(a, b, (((1,), (1,)), ((), ())), preferred_element_type=jnp.float32)


def dot(a, b):
    return jnp.dot(a, b, preferred_element_type=jnp.float32)


def first_square(where, keep_d, keep_s, *refs):
    parts, (panel, square, low), (kept, col_rows, row, sems) = refs[:8], refs[8:11], refs[11:]
    x, y, core, z = where[0], where[1], where[2], where[3]
    chip = x * 4 + y
    copies = [
        pltpu.make_async_copy(part, kept.at[pl.ds(i * 512, 512)], sems.at[i])
        for i, part in enumerate(parts)
    ]
    for copy in copies:
        copy.start()
    for copy in copies:
        copy.wait()

    def position(block):
        px, py, kind = block >> 3, (block >> 1) & 3, block & 1
        dx, dy = (px - x) & 3, (py - y) & 3
        first = jnp.where(kind == 0, dx, dy)
        second = jnp.where(kind == 0, dy, dx)
        return jnp.where(kind == core, 0, 16) + second * 4 + first

    col_block = z * 8 + core * 4
    for t in range(4):
        at = pl.multiple_of(position(col_block + t) * B, B)
        col_rows[pl.ds(t * B, B), :] = kept[pl.ds(at, B), :]
    for t in range(2):
        at = pl.multiple_of(position(chip * 2 + t) * B, B)
        col_rows[pl.ds(512 + t * B, B), :] = kept[pl.ds(at, B), :]

    @pl.loop(0, 8)
    def _(part):
        kind = jnp.where(part < 4, core, 1 - core)
        second = part & 3
        chunk = kept[pl.ds(pl.multiple_of(part * 512, 512), 512), :]
        blocks = []
        for first in range(4):
            px, py = place(x, y, kind, first, second)
            blocks.append(px * 8 + py * 2 + kind)
        down = dot_t(chunk, col_rows[0:512, :])
        for i in range(4):
            at = pl.multiple_of(blocks[i] * B, B)
            for t in range(4):
                keep = keep_d[0, blocks[i], col_block + t].astype(jnp.float32)
                piece = down[i * B:(i + 1) * B, t * B:(t + 1) * B] * keep
                panel[pl.ds(at, B), t * B:(t + 1) * B] = piece.astype(jnp.bfloat16)
        across = dot_t(col_rows[512:768, :], chunk)
        for i in range(4):
            at = pl.multiple_of(blocks[i] * B, B)
            for t in range(2):
                keep = keep_d[0, chip * 2 + t, blocks[i]].astype(jnp.float32)
                piece = across[t * B:(t + 1) * B, i * B:(i + 1) * B] * keep
                row[t * B:(t + 1) * B, pl.ds(at, B)] = piece.astype(jnp.bfloat16)

    finish_square(dot(row[...], panel[...]), keep_s, 0, chip * 2, col_block, square, low)


def finish_square(value, keep_s, step, row_block, col_block, square, low):
    for t in range(2):
        for u in range(4):
            keep = keep_s[step, row_block + t, col_block + u].astype(jnp.float32)
            piece = value[t * B:(t + 1) * B, u * B:(u + 1) * B] * keep
            square[t * B:(t + 1) * B, u * B:(u + 1) * B] = piece
            low[t * B:(t + 1) * B, u * B:(u + 1) * B] = piece.astype(jnp.bfloat16)


def row_times_panel(own, other, core, z, panel):
    total = None
    for d in range(4):
        for ref, half in ((own[d], core), (other[d], 1 - core)):
            at = pl.multiple_of((((z + d) & 3) * 2 + half) * COLS, COLS)
            term = dot(ref[...], panel[pl.ds(at, COLS), :])
            total = term if total is None else total + term
    return total


def first_density(where, keep_d, *refs):
    own, other, (square, panel), (out,) = refs[:4], refs[4:8], refs[8:10], refs[10:]
    x, y, core, z = where[0], where[1], where[2], where[3]
    cube = row_times_panel(own, other, core, z, panel)
    value = 3.0 * square[...] - 2.0 * cube
    for t in range(2):
        for u in range(4):
            keep = keep_d[1, (x * 4 + y) * 2 + t, z * 8 + core * 4 + u].astype(jnp.float32)
            piece = value[t * B:(t + 1) * B, u * B:(u + 1) * B] * keep
            out[t * B:(t + 1) * B, u * B:(u + 1) * B] = piece.astype(jnp.bfloat16)


def load_panel(parts, panel, sems, x, y, core):
    copies = []
    for second, part in enumerate(parts):
        for first in range(4):
            px, py = place(x, y, core, first, second)
            at = pl.multiple_of((px * 4 + py) * ROWS, ROWS)
            copies.append(pltpu.make_async_copy(
                part.at[pl.ds(first * ROWS, ROWS)], panel.at[pl.ds(at, ROWS)], sems.at[second * 4 + first]))
    for copy in copies:
        copy.start()
    for copy in copies:
        copy.wait()


def second_square(where, keep_s, *refs):
    own, other, parts, (square, low), (panel, sems) = refs[:4], refs[4:8], refs[8:12], refs[12:14], refs[14:]
    x, y, core, z = where[0], where[1], where[2], where[3]
    load_panel(parts, panel, sems, x, y, core)
    value = row_times_panel(own, other, core, z, panel)
    finish_square(value, keep_s, 1, (x * 4 + y) * 2, z * 8 + core * 4, square, low)


def second_density(where, *refs):
    own, other, (square,), parts, (stay, leave), (panel, sems) = (
        refs[:4], refs[4:8], refs[8:9], refs[9:13], refs[13:15], refs[15:])
    x, y, core, z = where[0], where[1], where[2], where[3]
    load_panel(parts, panel, sems, x, y, core)
    value = 3.0 * square[...] - 2.0 * row_times_panel(own, other, core, z, panel)
    first = core == 0
    stay[...] = jnp.where(first, value[:B], value[B:])
    leave[...] = jnp.where(first, value[B:], value[:B])


SMEM = pl.BlockSpec(memory_space=pltpu.SMEM)
VMEM = pl.BlockSpec(memory_space=pltpu.VMEM)
ANY = pl.BlockSpec(memory_space=pl.ANY)


def call(kernel, ins, outs, scratch, flops, moved):
    return pl.pallas_call(
        kernel,
        in_specs=ins,
        out_specs=[VMEM] * len(outs),
        out_shape=outs,
        scratch_shapes=scratch,
        cost_estimate=pl.CostEstimate(flops=flops, bytes_accessed=moved, transcendentals=0),
        compiler_params=pltpu.CompilerParams(vmem_limit_bytes=40 * MIB),
    )


def body(coeffs, coef_pattern, keep_density, keep_square):
    r, z = lax.axis_index("row"), lax.axis_index("col")
    x, y, core = r // 8, (r // 2) % 4, r % 2
    where = jnp.stack([x, y, core, z]).astype(jnp.int32)
    low_block = jax.ShapeDtypeStruct((ROWS, COLS), jnp.bfloat16)
    full_block = jax.ShapeDtypeStruct((ROWS, COLS), jnp.float32)
    panel_scratch = [pltpu.VMEM((N, COLS), jnp.bfloat16), pltpu.SemaphoreType.DMA((16,))]

    pattern = lax.dynamic_slice(coef_pattern, (r, z * 2), (1, 2))
    kept = coeffs * jnp.repeat(pattern, B, 1).astype(jnp.bfloat16)

    kept = jnp.concatenate(by_offset(gather_z(kept)), axis=1)
    parts = gather_plane(kept)
    parts = parts + [other_core(part) for part in parts]
    panel, square, low = call(
        first_square, [SMEM] * 3 + [ANY] * 8,
        [jax.ShapeDtypeStruct((N, COLS), jnp.bfloat16), full_block, low_block],
        [
            pltpu.VMEM((N, K), jnp.bfloat16),
            pltpu.VMEM((COLS + ROWS, K), jnp.bfloat16),
            pltpu.VMEM((ROWS, N), jnp.bfloat16),
            pltpu.SemaphoreType.DMA((8,)),
        ],
        2 * N * K * (COLS + ROWS) + 2 * ROWS * N * COLS, 13 * MIB,
    )(where, keep_density, keep_square, *parts)

    own = by_offset(gather_z(low))
    other = [other_core(part) for part in own]
    (current,) = call(
        first_density, [SMEM] * 2 + [VMEM] * 10, [low_block], [], 2 * ROWS * N * COLS, 7 * MIB,
    )(where, keep_density, *own, *other, square, panel)

    parts = gather_plane(current)
    own = by_offset(gather_z(current))
    other = [other_core(part) for part in own]
    square, low = call(
        second_square, [SMEM] * 2 + [VMEM] * 8 + [ANY] * 4, [full_block, low_block],
        panel_scratch, 2 * ROWS * N * COLS, 7 * MIB,
    )(where, keep_square, *own, *other, *parts)

    own = by_offset(gather_z(low))
    other = [other_core(part) for part in own]
    half = jax.ShapeDtypeStruct((B, COLS), jnp.float32)
    stay, leave = call(
        second_density, [SMEM] + [VMEM] * 9 + [ANY] * 4, [half, half],
        panel_scratch, 2 * ROWS * N * COLS, 8 * MIB,
    )(where, *own, *other, square, *parts)
    come = other_core(leave)
    left = core == 0
    return jnp.concatenate([jnp.where(left, stay, come), jnp.where(left, come, stay)], axis=1)


def solution(mesh):
    placed = (P("row", "col"), P(), P(), P())
    return jax.shard_map(
        body, mesh=mesh, in_specs=placed, out_specs=P("row", "col"), check_vma=False
    )
```

time: 329 us -> 155 us (0.47)
  waiting for transfers between devices: 282 us -> 58.6 us
  starting transfers between devices: 0.29 us -> 71.2 us
  matrix products: 26.6 us -> 0 us
  Pallas kernels: 0 us -> 21.7 us
  between operations: 13.5 us -> 0.13 us
    all_gather x7 -> x0, waiting for transfers between devices: 252 us -> none  [the longest x2 114 us: body(): panel = lax.all_gather(current, 'row', axis=0, tiled=True)]
    ppermute x0 -> x41, starting transfers between devices: none -> 71.2 us  [the longest x17 35.1 us: other_core(): lax.ppermute(a, AXES, pairs(lambda x, y, core, z: (x, y, 1 - core, z)))]
    ppermute x0 -> x41, waiting for transfers between devices: none -> 58.6 us  [the longest x12 20.8 us: from_z(): lax.ppermute(a, AXES, pairs(lambda x, y, core, z: (x, y, core, z - d)))]
    reduce_scatter x1 -> x0, waiting for transfers between devices: 28 us -> none  [body(): density = lax.psum_scatter(terms, 'col', scatter_dimension=1, tiled=True)]
    dot_general x5 -> x0, matrix products: 26.6 us -> none  [the longest x2 11.5 us: body(): cube = jnp.dot(square_full, panel, preferred_element_type=jnp.float32)]
    pallas_call x0 -> x4, Pallas kernels: none -> 21.7 us  [the longest x1 14.2 us: body(): call(first_square, [SMEM] * 3 + [ANY] * 8, [jax.ShapeDtypeStruct((N, COLS...]
  transfers between devices with their start and end apart: 8 -> 41, of which waited for: 8 -> 22; matrix products, arithmetic and copies ran while one was open for 1% -> 0% of each run, Pallas kernels for 0% -> 0%
where the time goes in v1:
time: 155 us
  starting transfers between devices  71.2 us (46%)
  waiting for transfers between devices  58.6 us (38%)
  Pallas kernels  21.7 us (14%)
  other arithmetic  2.84 us (2%)
    ppermute x17, starting transfers between devices, other_core(): lax.ppermute(a, AXES, pairs(lambda x, y, core, z: (x, y, 1 - core, z)))  35.1 us
    ppermute x12, waiting for transfers between devices, from_z(): lax.ppermute(a, AXES, pairs(lambda x, y, core, z: (x, y, core, z - d)))  20.8 us
    ppermute x6, waiting for transfers between devices, from_second(): lax.ppermute(a, AXES, pairs(lambda x, y, core, z: (x, y - d, core, z) if...  18.1 us
    ppermute x12, starting transfers between devices, from_z(): lax.ppermute(a, AXES, pairs(lambda x, y, core, z: (x, y, core, z - d)))  17.5 us
    pallas_call x1, Pallas kernels, body(): call(first_square, [SMEM] * 3 + [ANY] * 8, [jax.ShapeDtypeStruct((N, COLS...  14.2 us
    ppermute x6, waiting for transfers between devices, from_first(): lax.ppermute(a, AXES, pairs(lambda x, y, core, z: (x - d, y, core, z) if...  9.98 us
    ppermute x17, waiting for transfers between devices, other_core(): lax.ppermute(a, AXES, pairs(lambda x, y, core, z: (x, y, 1 - core, z)))  9.62 us
    ppermute x6, starting transfers between devices, from_second(): lax.ppermute(a, AXES, pairs(lambda x, y, core, z: (x, y - d, core, z) if...  9.39 us
  transfers between devices with their start and end apart: 41, of which 22 were waited for; matrix products, arithmetic and copies ran while one was open for 0% of the time, Pallas kernels for 0%

profile of v1, /device:TPU:1, one launch (start us, length us, event | category | flops | bytes accessed | tf_op | source)
XLA Modules:
  0.0 154.5 jit_solution(10906029421089156105)
XLA Ops:
  1.8 2.5 %collective-permute-start.2 = (bf16[128,256]{1,0:T(8,128)(2,1)S(1)}, bf16[128,256]{1,0:T(8,128)(2,1)S(1)}, u32[]{:S(2)}, u32[]{:S(2)}) collective-permute-start(bf16[128,256]{1,0:T(8,128)(2,1)S(1)} %broadcast_multiply_fusion), channel_id=1, source_target_pairs={{0,1},{1,2},{2,3},{3,0},{4,5},{5,6},{6,7},{7,4},{8,9},{9,10},{10,1... | collective-permute-start | bytes 196616 | tf_op jit(solution)/shard_map/ppermute | solution.py:33
  4.3 3.3 %collective-permute-start.1 = (bf16[128,256]{1,0:T(8,128)(2,1)S(1)}, bf16[128,256]{1,0:T(8,128)(2,1)S(1)}, u32[]{:S(2)}, u32[]{:S(2)}) collective-permute-start(bf16[128,256]{1,0:T(8,128)(2,1)S(1)} %broadcast_multiply_fusion), channel_id=1, source_target_pairs={{0,2},{1,3},{2,0},{3,1},{4,6},{5,7},{6,4},{7,5},{8,10},{9,11},{10,... | collective-permute-start | bytes 196616 | tf_op jit(solution)/shard_map/ppermute | solution.py:33
  8.3 1.9 %collective-permute-done.1 = bf16[128,256]{1,0:T(8,128)(2,1)S(1)} collective-permute-done((bf16[128,256]{1,0:T(8,128)(2,1)S(1)}, bf16[128,256]{1,0:T(8,128)(2,1)S(1)}, u32[]{:S(2)}, u32[]{:S(2)}) %collective-permute-start.1) | collective-permute-done | bytes 65568 | tf_op jit(solution)/shard_map/ppermute | solution.py:33
  11.0 1.4 collective-permute-start.5
  12.4 2.6 %collective-permute-start.4 = (bf16[128,1024]{1,0:T(8,128)(2,1)S(1)}, bf16[128,1024]{1,0:T(8,128)(2,1)S(1)}, u32[]{:S(2)}, u32[]{:S(2)}) collective-permute-start(bf16[128,1024]{1,0:T(8,128)(2,1)S(1)} %pad_maximum_fusion.3), channel_id=1, source_target_pairs={{0,64},{1,65},{2,66},{3,67},{4,20},{5,21},{6,22},{7,23},{8,72},{9,... | collective-permute-start | bytes 786440 | tf_op jit(solution)/shard_map/ppermute | solution.py:37
  15.0 1.1 collective-permute-start.3
  16.1 1.8 %collective-permute-done.5 = bf16[128,1024]{1,0:T(8,128)(2,1)S(1)} collective-permute-done((bf16[128,1024]{1,0:T(8,128)(2,1)S(1)}, bf16[128,1024]{1,0:T(8,128)(2,1)S(1)}, u32[]{:S(2)}, u32[]{:S(2)}) %collective-permute-start.5) | collective-permute-done | bytes 262176 | tf_op jit(solution)/shard_map/ppermute | solution.py:37
  17.9 4.0 %collective-permute-done.4 = bf16[128,1024]{1,0:T(8,128)(2,1)S(1)} collective-permute-done((bf16[128,1024]{1,0:T(8,128)(2,1)S(1)}, bf16[128,1024]{1,0:T(8,128)(2,1)S(1)}, u32[]{:S(2)}, u32[]{:S(2)}) %collective-permute-start.4) | collective-permute-done | bytes 262176 | tf_op jit(solution)/shard_map/ppermute | solution.py:37
  22.0 1.0 collective-permute-start.8
  22.9 2.5 %collective-permute-start.7 = (bf16[512,1024]{1,0:T(8,128)(2,1)S(1)}, bf16[512,1024]{1,0:T(8,128)(2,1)S(1)}, u32[]{:S(2)}, u32[]{:S(2)}) collective-permute-start(bf16[512,1024]{1,0:T(8,128)(2,1)S(1)} %pad_maximum_fusion.refs_0_), channel_id=1, source_target_pairs={{0,16},{1,17},{2,18},{3,19},{4,68},{5,69},{6,70},{7,71},{8,24},{9,... | collective-permute-start | bytes 3145736 | tf_op jit(solution)/shard_map/ppermute | solution.py:42
  25.4 1.2 collective-permute-start.6
  26.5 4.0 %collective-permute-start.9 = (bf16[512,1024]{1,0:T(8,128)(2,1)S(1)}, bf16[512,1024]{1,0:T(8,128)(2,1)}, u32[]{:S(2)}, u32[]{:S(2)}) collective-permute-start(bf16[512,1024]{1,0:T(8,128)(2,1)S(1)} %pad_maximum_fusion.refs_0_), channel_id=1, source_target_pairs={{0,4},{1,5},{2,6},{3,7},{4,0},{5,1},{6,2},{7,3},{8,12},{9,13},{10,... | collective-permute-start | bytes 3145736 | tf_op jit(solution)/shard_map/ppermute | solution.py:29
  30.5 6.6 %collective-permute-done.8.refs_3_ = bf16[512,1024]{1,0:T(8,128)(2,1)S(1)} collective-permute-done((bf16[512,1024]{1,0:T(8,128)(2,1)S(1)}, bf16[512,1024]{1,0:T(8,128)(2,1)S(1)}, u32[]{:S(2)}, u32[]{:S(2)}) %collective-permute-start.8) | collective-permute-done | bytes 1048608 | tf_op jit(solution)/shard_map/ppermute | solution.py:42
  37.2 3.5 %collective-permute-start.12 = (bf16[512,1024]{1,0:T(8,128)(2,1)S(1)}, bf16[512,1024]{1,0:T(8,128)(2,1)}, u32[]{:S(2)}, u32[]{:S(2)}) collective-permute-start(bf16[512,1024]{1,0:T(8,128)(2,1)S(1)} %collective-permute-done.8.refs_3_), channel_id=1, source_target_pairs={{0,4},{1,5},{2,6},{3,7},{4,0},{5,1},{6,2},{7,3},{8,12},{9,13},{10,... | collective-permute-start | bytes 3145736 | tf_op jit(solution)/shard_map/ppermute | solution.py:29
  40.7 8.4 %collective-permute-done.7.refs_2_ = bf16[512,1024]{1,0:T(8,128)(2,1)S(1)} collective-permute-done((bf16[512,1024]{1,0:T(8,128)(2,1)S(1)}, bf16[512,1024]{1,0:T(8,128)(2,1)S(1)}, u32[]{:S(2)}, u32[]{:S(2)}) %collective-permute-start.7) | collective-permute-done | bytes 1048608 | tf_op jit(solution)/shard_map/ppermute | solution.py:42
  49.1 4.1 %collective-permute-start.11 = (bf16[512,1024]{1,0:T(8,128)(2,1)S(1)}, bf16[512,1024]{1,0:T(8,128)(2,1)}, u32[]{:S(2)}, u32[]{:S(2)}) collective-permute-start(bf16[512,1024]{1,0:T(8,128)(2,1)S(1)} %collective-permute-done.7.refs_2_), channel_id=1, source_target_pairs={{0,4},{1,5},{2,6},{3,7},{4,0},{5,1},{6,2},{7,3},{8,12},{9,13},{10,... | collective-permute-start | bytes 3145736 | tf_op jit(solution)/shard_map/ppermute | solution.py:29
  53.3 3.7 %collective-permute-done.11.refs_6_ = bf16[512,1024]{1,0:T(8,128)(2,1)} collective-permute-done((bf16[512,1024]{1,0:T(8,128)(2,1)S(1)}, bf16[512,1024]{1,0:T(8,128)(2,1)}, u32[]{:S(2)}, u32[]{:S(2)}) %collective-permute-start.11) | collective-permute-done | bytes 1048608 | tf_op jit(solution)/shard_map/ppermute | solution.py:29
  57.3 14.2 %shard_map.46 = (bf16[4096,512]{1,0:T(8,128)(2,1)S(1)}, f32[256,512]{1,0:T(8,128)S(1)}, bf16[256,512]{1,0:T(8,128)(2,1)S(1)}) custom-call(s32[4]{0:T(128)S(1)} %pad_add_fusion.where, s32[2,32,32]{2,1,0:T(8,128)S(1)} %copy-done, s32[2,32,32]{2,1,0:T(8,128)S(1)} %copy-done.1, bf16[512,1024]{1,0:T(8,128)(2,1)S(1)} %pad_maximum_fusion.refs_0_, ...), custom_call_target="tpu_custom_call" | custom-call | flops 7516192768 | bytes 13631488 | tf_op jit(solution)/shard_map/pallas_call | solution.py:224
  71.6 3.1 %collective-permute-start.14 = (bf16[256,512]{1,0:T(8,128)(2,1)S(1)}, bf16[256,512]{1,0:T(8,128)(2,1)S(1)}, u32[]{:S(2)}, u32[]{:S(2)}) collective-permute-start(bf16[256,512]{1,0:T(8,128)(2,1)S(1)} %get-tuple-element.12.refs_0_), channel_id=1, source_target_pairs={{0,2},{1,3},{2,0},{3,1},{4,6},{5,7},{6,4},{7,5},{8,10},{9,11},{10,... | collective-permute-start | bytes 786440 | tf_op jit(solution)/shard_map/ppermute | solution.py:33
  74.9 1.2 collective-permute-start.16
  76.1 4.2 %collective-permute-done.15.refs_3_ = bf16[256,512]{1,0:T(8,128)(2,1)S(1)} collective-permute-done((bf16[256,512]{1,0:T(8,128)(2,1)S(1)}, bf16[256,512]{1,0:T(8,128)(2,1)S(1)}, u32[]{:S(2)}, u32[]{:S(2)}) %collective-permute-start.15) | collective-permute-done | bytes 262176 | tf_op jit(solution)/shard_map/ppermute | solution.py:33
  80.3 1.6 %collective-permute-start.19 = (bf16[256,512]{1,0:T(8,128)(2,1)S(1)}, bf16[256,512]{1,0:T(8,128)(2,1)S(1)}, u32[]{:S(2)}, u32[]{:S(2)}) collective-permute-start(bf16[256,512]{1,0:T(8,128)(2,1)S(1)} %collective-permute-done.15.refs_3_), channel_id=1, source_target_pairs={{0,4},{1,5},{2,6},{3,7},{4,0},{5,1},{6,2},{7,3},{8,12},{9,13},{10,... | collective-permute-start | bytes 786440 | tf_op jit(solution)/shard_map/ppermute | solution.py:29
  81.9 4.5 %collective-permute-done.14.refs_2_ = bf16[256,512]{1,0:T(8,128)(2,1)S(1)} collective-permute-done((bf16[256,512]{1,0:T(8,128)(2,1)S(1)}, bf16[256,512]{1,0:T(8,128)(2,1)S(1)}, u32[]{:S(2)}, u32[]{:S(2)}) %collective-permute-start.14) | collective-permute-done | bytes 262176 | tf_op jit(solution)/shard_map/ppermute | solution.py:33
  86.4 1.2 collective-permute-start.18
  87.8 1.0 collective-permute-done.18.refs_6_
  89.1 2.3 %shard_map.47.refs_0_ = bf16[256,512]{1,0:T(8,128)(2,1)S(1)} custom-call(s32[4]{0:T(128)S(1)} %pad_add_fusion.where, s32[2,32,32]{2,1,0:T(8,128)S(1)} %copy-done, bf16[256,512]{1,0:T(8,128)(2,1)S(1)} %get-tuple-element.12.refs_0_, bf16[256,512]{1,0:T(8,128)(2,1)S(1)} %collective-permute-done.13.refs_1_, ...), custom_call_target="tpu_custom_call" | custom-call | flops 1073741824 | bytes 7340032 | tf_op jit(solution)/shard_map/pallas_call | solution.py:238
  91.5 2.0 %collective-permute-start.28 = (bf16[256,512]{1,0:T(8,128)(2,1)S(1)}, bf16[256,512]{1,0:T(8,128)(2,1)S(1)}, u32[]{:S(2)}, u32[]{:S(2)}) collective-permute-start(bf16[256,512]{1,0:T(8,128)(2,1)S(1)} %shard_map.47.refs_0_), channel_id=1, source_target_pairs={{0,64},{1,65},{2,66},{3,67},{4,20},{5,21},{6,22},{7,23},{8,72},{9,... | collective-permute-start | bytes 786440 | tf_op jit(solution)/shard_map/ppermute | solution.py:37
  93.6 2.0 %collective-permute-start.27 = (bf16[256,512]{1,0:T(8,128)(2,1)S(1)}, bf16[256,512]{1,0:T(8,128)(2,1)S(1)}, u32[]{:S(2)}, u32[]{:S(2)}) collective-permute-start(bf16[256,512]{1,0:T(8,128)(2,1)S(1)} %shard_map.47.refs_0_), channel_id=1, source_target_pairs={{0,96},{1,97},{2,98},{3,99},{4,28},{5,29},{6,30},{7,31},{8,104},{9... | collective-permute-start | bytes 786440 | tf_op jit(solution)/shard_map/ppermute | solution.py:37
  95.6 1.9 %collective-permute-start.23 = (bf16[256,512]{1,0:T(8,128)(2,1)S(1)}, bf16[256,512]{1,0:T(8,128)(2,1)S(1)}, u32[]{:S(2)}, u32[]{:S(2)}) collective-permute-start(bf16[256,512]{1,0:T(8,128)(2,1)S(1)} %shard_map.47.refs_0_), channel_id=1, source_target_pairs={{0,4},{1,5},{2,6},{3,7},{4,0},{5,1},{6,2},{7,3},{8,12},{9,13},{10,... | collective-permute-start | bytes 786440 | tf_op jit(solution)/shard_map/ppermute | solution.py:29
  97.5 3.6 %collective-permute-done.29 = bf16[256,512]{1,0:T(8,128)(2,1)S(1)} collective-permute-done((bf16[256,512]{1,0:T(8,128)(2,1)S(1)}, bf16[256,512]{1,0:T(8,128)(2,1)S(1)}, u32[]{:S(2)}, u32[]{:S(2)}) %collective-permute-start.29) | collective-permute-done | bytes 262176 | tf_op jit(solution)/shard_map/ppermute | solution.py:37
  101.7 1.7 %collective-permute-start.32 = (bf16[1024,512]{1,0:T(8,128)(2,1)S(1)}, bf16[1024,512]{1,0:T(8,128)(2,1)S(1)}, u32[]{:S(2)}, u32[]{:S(2)}) collective-permute-start(bf16[1024,512]{1,0:T(8,128)(2,1)S(1)} %pad_maximum_fusion.1.refs_8_.refs_9_), channel_id=1, source_target_pairs={{0,8},{1,9},{2,10},{3,11},{4,36},{5,37},{6,38},{7,39},{8,16},{9,17... | collective-permute-start | bytes 3145736 | tf_op jit(solution)/shard_map/ppermute | solution.py:42
  103.4 1.8 %collective-permute-start.31 = (bf16[1024,512]{1,0:T(8,128)(2,1)S(1)}, bf16[1024,512]{1,0:T(8,128)(2,1)S(1)}, u32[]{:S(2)}, u32[]{:S(2)}) collective-permute-start(bf16[1024,512]{1,0:T(8,128)(2,1)S(1)} %pad_maximum_fusion.1.refs_8_.refs_9_), channel_id=1, source_target_pairs={{0,16},{1,17},{2,18},{3,19},{4,68},{5,69},{6,70},{7,71},{8,24},{9,... | collective-permute-start | bytes 3145736 | tf_op jit(solution)/shard_map/ppermute | solution.py:42
  105.3 1.3 collective-permute-start.30
  106.9 3.0 %collective-permute-start.21 = (bf16[256,512]{1,0:T(8,128)(2,1)S(1)}, bf16[256,512]{1,0:T(8,128)(2,1)S(1)}, u32[]{:S(2)}, u32[]{:S(2)}) collective-permute-start(bf16[256,512]{1,0:T(8,128)(2,1)S(1)} %shard_map.47.refs_0_), channel_id=1, source_target_pairs={{0,2},{1,3},{2,0},{3,1},{4,6},{5,7},{6,4},{7,5},{8,10},{9,11},{10,... | collective-permute-start | bytes 786440 | tf_op jit(solution)/shard_map/ppermute | solution.py:33
  109.9 4.1 %collective-permute-done.22.refs_3_ = bf16[256,512]{1,0:T(8,128)(2,1)S(1)} collective-permute-done((bf16[256,512]{1,0:T(8,128)(2,1)S(1)}, bf16[256,512]{1,0:T(8,128)(2,1)S(1)}, u32[]{:S(2)}, u32[]{:S(2)}) %collective-permute-start.22) | collective-permute-done | bytes 262176 | tf_op jit(solution)/shard_map/ppermute | solution.py:33
  114.9 5.3 %collective-permute-done.21.refs_2_ = bf16[256,512]{1,0:T(8,128)(2,1)S(1)} collective-permute-done((bf16[256,512]{1,0:T(8,128)(2,1)S(1)}, bf16[256,512]{1,0:T(8,128)(2,1)S(1)}, u32[]{:S(2)}, u32[]{:S(2)}) %collective-permute-start.21) | collective-permute-done | bytes 262176 | tf_op jit(solution)/shard_map/ppermute | solution.py:33
  120.2 2.5 %collective-permute-start.26 = (bf16[256,512]{1,0:T(8,128)(2,1)S(1)}, bf16[256,512]{1,0:T(8,128)(2,1)S(1)}, u32[]{:S(2)}, u32[]{:S(2)}) collective-permute-start(bf16[256,512]{1,0:T(8,128)(2,1)S(1)} %collective-permute-done.22.refs_3_), channel_id=1, source_target_pairs={{0,4},{1,5},{2,6},{3,7},{4,0},{5,1},{6,2},{7,3},{8,12},{9,13},{10,... | collective-permute-start | bytes 786440 | tf_op jit(solution)/shard_map/ppermute | solution.py:29
  122.8 1.6 %collective-permute-start.25 = (bf16[256,512]{1,0:T(8,128)(2,1)S(1)}, bf16[256,512]{1,0:T(8,128)(2,1)S(1)}, u32[]{:S(2)}, u32[]{:S(2)}) collective-permute-start(bf16[256,512]{1,0:T(8,128)(2,1)S(1)} %collective-permute-done.21.refs_2_), channel_id=1, source_target_pairs={{0,4},{1,5},{2,6},{3,7},{4,0},{5,1},{6,2},{7,3},{8,12},{9,13},{10,... | collective-permute-start | bytes 786440 | tf_op jit(solution)/shard_map/ppermute | solution.py:29
  124.4 1.2 collective-permute-done.25.refs_6_
  125.9 3.1 %collective-permute-done.31.refs_10_.refs_11_ = bf16[1024,512]{1,0:T(8,128)(2,1)S(1)} collective-permute-done((bf16[1024,512]{1,0:T(8,128)(2,1)S(1)}, bf16[1024,512]{1,0:T(8,128)(2,1)S(1)}, u32[]{:S(2)}, u32[]{:S(2)}) %collective-permute-start.31) | collective-permute-done | bytes 1048608 | tf_op jit(solution)/shard_map/ppermute | solution.py:42
  129.0 2.9 %shard_map.48 = (f32[256,512]{1,0:T(8,128)S(1)}, bf16[256,512]{1,0:T(8,128)(2,1)S(1)}) custom-call(s32[4]{0:T(128)S(1)} %pad_add_fusion.where, s32[2,32,32]{2,1,0:T(8,128)S(1)} %copy-done.1, bf16[256,512]{1,0:T(8,128)(2,1)S(1)} %shard_map.47.refs_0_, bf16[256,512]{1,0:T(8,128)(2,1)S(1)} %collective-permute-done.20.refs_1_, ...), custom_call_target="tpu_custom_call" | custom-call | flops 1073741824 | bytes 7340032 | tf_op jit(solution)/shard_map/pallas_call | solution.py:245
  132.3 3.0 %collective-permute-start.34 = (bf16[256,512]{1,0:T(8,128)(2,1)S(1)}, bf16[256,512]{1,0:T(8,128)(2,1)S(1)}, u32[]{:S(2)}, u32[]{:S(2)}) collective-permute-start(bf16[256,512]{1,0:T(8,128)(2,1)S(1)} %get-tuple-element.15.refs_0_), channel_id=1, source_target_pairs={{0,2},{1,3},{2,0},{3,1},{4,6},{5,7},{6,4},{7,5},{8,10},{9,11},{10,... | collective-permute-start | bytes 786440 | tf_op jit(solution)/shard_map/ppermute | solution.py:33
  135.3 3.1 %collective-permute-start.36 = (bf16[256,512]{1,0:T(8,128)(2,1)S(1)}, bf16[256,512]{1,0:T(8,128)(2,1)S(1)}, u32[]{:S(2)}, u32[]{:S(2)}) collective-permute-start(bf16[256,512]{1,0:T(8,128)(2,1)S(1)} %get-tuple-element.15.refs_0_), channel_id=1, source_target_pairs={{0,4},{1,5},{2,6},{3,7},{4,0},{5,1},{6,2},{7,3},{8,12},{9,13},{10,... | collective-permute-start | bytes 786440 | tf_op jit(solution)/shard_map/ppermute | solution.py:29
  138.4 6.1 %collective-permute-start.39 = (bf16[256,512]{1,0:T(8,128)(2,1)S(1)}, bf16[256,512]{1,0:T(8,128)(2,1)S(1)}, u32[]{:S(2)}, u32[]{:S(2)}) collective-permute-start(bf16[256,512]{1,0:T(8,128)(2,1)S(1)} %collective-permute-done.35.refs_3_), channel_id=1, source_target_pairs={{0,4},{1,5},{2,6},{3,7},{4,0},{5,1},{6,2},{7,3},{8,12},{9,13},{10,... | collective-permute-start | bytes 786440 | tf_op jit(solution)/shard_map/ppermute | solution.py:29
  144.4 3.7 %collective-permute-start.38 = (bf16[256,512]{1,0:T(8,128)(2,1)S(1)}, bf16[256,512]{1,0:T(8,128)(2,1)S(1)}, u32[]{:S(2)}, u32[]{:S(2)}) collective-permute-start(bf16[256,512]{1,0:T(8,128)(2,1)S(1)} %collective-permute-done.34.refs_2_), channel_id=1, source_target_pairs={{0,4},{1,5},{2,6},{3,7},{4,0},{5,1},{6,2},{7,3},{8,12},{9,13},{10,... | collective-permute-start | bytes 786440 | tf_op jit(solution)/shard_map/ppermute | solution.py:29
  148.2 1.1 collective-permute-done.38.refs_6_
  149.7 2.4 %shard_map.49 = (f32[128,512]{1,0:T(8,128)S(1)}, f32[128,512]{1,0:T(8,128)S(1)}) custom-call(s32[4]{0:T(128)S(1)} %pad_add_fusion.where, bf16[256,512]{1,0:T(8,128)(2,1)S(1)} %get-tuple-element.15.refs_0_, bf16[256,512]{1,0:T(8,128)(2,1)S(1)} %collective-permute-done.33.refs_1_, bf16[256,512]{1,0:T(8,128)(2,1)S(1)} %collective-permute-done.34.refs_2_, ...), custom_call_target="tpu_custom_call" | custom-call | flops 1073741824 | bytes 8388608 | tf_op jit(solution)/shard_map/pallas_call | solution.py:253
  152.5 1.2 collective-permute-done.40
  (51 shorter events, 9.3 us)
Async XLA Ops:
  0.0 57.3 %copy-start.1 = (s32[2,32,32]{2,1,0:T(8,128)S(1)}, s32[2,32,32]{2,1,0:T(8,128)}, u32[]{:S(2)}) copy-start(s32[2,32,32]{2,1,0:T(8,128)} %keep_s.3) | copy-start | bytes 24580
  0.0 57.3 %copy-start = (s32[2,32,32]{2,1,0:T(8,128)S(1)}, s32[2,32,32]{2,1,0:T(8,128)}, u32[]{:S(2)}) copy-start(s32[2,32,32]{2,1,0:T(8,128)} %keep_d.3) | copy-start | bytes 24580
  1.8 6.5 %collective-permute-start.2 = (bf16[128,256]{1,0:T(8,128)(2,1)S(1)}, bf16[128,256]{1,0:T(8,128)(2,1)S(1)}, u32[]{:S(2)}, u32[]{:S(2)}) collective-permute-start(bf16[128,256]{1,0:T(8,128)(2,1)S(1)} %broadcast_multiply_fusion), channel_id=1, source_target_pairs={{0,1},{1,2},{2,3},{3,0},{4,5},{5,6},{6,7},{7,4},{8,9},{9,10},{10,1... | collective-permute-start | bytes 196616 | tf_op jit(solution)/shard_map/ppermute | solution.py:33
  4.3 5.9 %collective-permute-start.1 = (bf16[128,256]{1,0:T(8,128)(2,1)S(1)}, bf16[128,256]{1,0:T(8,128)(2,1)S(1)}, u32[]{:S(2)}, u32[]{:S(2)}) collective-permute-start(bf16[128,256]{1,0:T(8,128)(2,1)S(1)} %broadcast_multiply_fusion), channel_id=1, source_target_pairs={{0,2},{1,3},{2,0},{3,1},{4,6},{5,7},{6,4},{7,5},{8,10},{9,11},{10,... | collective-permute-start | bytes 196616 | tf_op jit(solution)/shard_map/ppermute | solution.py:33
  7.6 3.4 %collective-permute-start = (bf16[128,256]{1,0:T(8,128)(2,1)S(1)}, bf16[128,256]{1,0:T(8,128)(2,1)S(1)}, u32[]{:S(2)}, u32[]{:S(2)}) collective-permute-start(bf16[128,256]{1,0:T(8,128)(2,1)S(1)} %broadcast_multiply_fusion), channel_id=1, source_target_pairs={{0,3},{1,0},{2,1},{3,2},{4,7},{5,4},{6,5},{7,6},{8,11},{9,8},{10,9... | collective-permute-start | bytes 196616 | tf_op jit(solution)/shard_map/ppermute | solution.py:33
  11.0 6.9 %collective-permute-start.5 = (bf16[128,1024]{1,0:T(8,128)(2,1)S(1)}, bf16[128,1024]{1,0:T(8,128)(2,1)S(1)}, u32[]{:S(2)}, u32[]{:S(2)}) collective-permute-start(bf16[128,1024]{1,0:T(8,128)(2,1)S(1)} %pad_maximum_fusion.3), channel_id=1, source_target_pairs={{0,32},{1,33},{2,34},{3,35},{4,12},{5,13},{6,14},{7,15},{8,40},{9,... | collective-permute-start | bytes 786440 | tf_op jit(solution)/shard_map/ppermute | solution.py:37
  12.4 9.5 %collective-permute-start.4 = (bf16[128,1024]{1,0:T(8,128)(2,1)S(1)}, bf16[128,1024]{1,0:T(8,128)(2,1)S(1)}, u32[]{:S(2)}, u32[]{:S(2)}) collective-permute-start(bf16[128,1024]{1,0:T(8,128)(2,1)S(1)} %pad_maximum_fusion.3), channel_id=1, source_target_pairs={{0,64},{1,65},{2,66},{3,67},{4,20},{5,21},{6,22},{7,23},{8,72},{9,... | collective-permute-start | bytes 786440 | tf_op jit(solution)/shard_map/ppermute | solution.py:37
  15.0 6.9 %collective-permute-start.3 = (bf16[128,1024]{1,0:T(8,128)(2,1)S(1)}, bf16[128,1024]{1,0:T(8,128)(2,1)S(1)}, u32[]{:S(2)}, u32[]{:S(2)}) collective-permute-start(bf16[128,1024]{1,0:T(8,128)(2,1)S(1)} %pad_maximum_fusion.3), channel_id=1, source_target_pairs={{0,96},{1,97},{2,98},{3,99},{4,28},{5,29},{6,30},{7,31},{8,104},{9... | collective-permute-start | bytes 786440 | tf_op jit(solution)/shard_map/ppermute | solution.py:37
  22.0 15.2 %collective-permute-start.8 = (bf16[512,1024]{1,0:T(8,128)(2,1)S(1)}, bf16[512,1024]{1,0:T(8,128)(2,1)S(1)}, u32[]{:S(2)}, u32[]{:S(2)}) collective-permute-start(bf16[512,1024]{1,0:T(8,128)(2,1)S(1)} %pad_maximum_fusion.refs_0_), channel_id=1, source_target_pairs={{0,8},{1,9},{2,10},{3,11},{4,36},{5,37},{6,38},{7,39},{8,16},{9,17... | collective-permute-start | bytes 3145736 | tf_op jit(solution)/shard_map/ppermute | solution.py:42
  22.9 26.2 %collective-permute-start.7 = (bf16[512,1024]{1,0:T(8,128)(2,1)S(1)}, bf16[512,1024]{1,0:T(8,128)(2,1)S(1)}, u32[]{:S(2)}, u32[]{:S(2)}) collective-permute-start(bf16[512,1024]{1,0:T(8,128)(2,1)S(1)} %pad_maximum_fusion.refs_0_), channel_id=1, source_target_pairs={{0,16},{1,17},{2,18},{3,19},{4,68},{5,69},{6,70},{7,71},{8,24},{9,... | collective-permute-start | bytes 3145736 | tf_op jit(solution)/shard_map/ppermute | solution.py:42
  25.4 27.8 %collective-permute-start.6 = (bf16[512,1024]{1,0:T(8,128)(2,1)S(1)}, bf16[512,1024]{1,0:T(8,128)(2,1)}, u32[]{:S(2)}, u32[]{:S(2)}) collective-permute-start(bf16[512,1024]{1,0:T(8,128)(2,1)S(1)} %pad_maximum_fusion.refs_0_), channel_id=1, source_target_pairs={{0,24},{1,25},{2,26},{3,27},{4,100},{5,101},{6,102},{7,103},{8,0},... | collective-permute-start | bytes 3145736 | tf_op jit(solution)/shard_map/ppermute | solution.py:42
  26.5 26.7 %collective-permute-start.9 = (bf16[512,1024]{1,0:T(8,128)(2,1)S(1)}, bf16[512,1024]{1,0:T(8,128)(2,1)}, u32[]{:S(2)}, u32[]{:S(2)}) collective-permute-start(bf16[512,1024]{1,0:T(8,128)(2,1)S(1)} %pad_maximum_fusion.refs_0_), channel_id=1, source_target_pairs={{0,4},{1,5},{2,6},{3,7},{4,0},{5,1},{6,2},{7,3},{8,12},{9,13},{10,... | collective-permute-start | bytes 3145736 | tf_op jit(solution)/shard_map/ppermute | solution.py:29
  37.2 16.1 %collective-permute-start.12 = (bf16[512,1024]{1,0:T(8,128)(2,1)S(1)}, bf16[512,1024]{1,0:T(8,128)(2,1)}, u32[]{:S(2)}, u32[]{:S(2)}) collective-permute-start(bf16[512,1024]{1,0:T(8,128)(2,1)S(1)} %collective-permute-done.8.refs_3_), channel_id=1, source_target_pairs={{0,4},{1,5},{2,6},{3,7},{4,0},{5,1},{6,2},{7,3},{8,12},{9,13},{10,... | collective-permute-start | bytes 3145736 | tf_op jit(solution)/shard_map/ppermute | solution.py:29
  49.1 7.9 %collective-permute-start.11 = (bf16[512,1024]{1,0:T(8,128)(2,1)S(1)}, bf16[512,1024]{1,0:T(8,128)(2,1)}, u32[]{:S(2)}, u32[]{:S(2)}) collective-permute-start(bf16[512,1024]{1,0:T(8,128)(2,1)S(1)} %collective-permute-done.7.refs_2_), channel_id=1, source_target_pairs={{0,4},{1,5},{2,6},{3,7},{4,0},{5,1},{6,2},{7,3},{8,12},{9,13},{10,... | collective-permute-start | bytes 3145736 | tf_op jit(solution)/shard_map/ppermute | solution.py:29
  53.2 4.1 %collective-permute-start.10 = (bf16[512,1024]{1,0:T(8,128)(2,1)}, bf16[512,1024]{1,0:T(8,128)(2,1)}, u32[]{:S(2)}, u32[]{:S(2)}) collective-permute-start(bf16[512,1024]{1,0:T(8,128)(2,1)} %collective-permute-done.6.refs_1_), channel_id=1, source_target_pairs={{0,4},{1,5},{2,6},{3,7},{4,0},{5,1},{6,2},{7,3},{8,12},{9,13},{10,... | collective-permute-start | bytes 3145736 | tf_op jit(solution)/shard_map/ppermute | solution.py:29
  71.5 8.8 %collective-permute-start.15 = (bf16[256,512]{1,0:T(8,128)(2,1)S(1)}, bf16[256,512]{1,0:T(8,128)(2,1)S(1)}, u32[]{:S(2)}, u32[]{:S(2)}) collective-permute-start(bf16[256,512]{1,0:T(8,128)(2,1)S(1)} %get-tuple-element.12.refs_0_), channel_id=1, source_target_pairs={{0,1},{1,2},{2,3},{3,0},{4,5},{5,6},{6,7},{7,4},{8,9},{9,10},{10,1... | collective-permute-start | bytes 786440 | tf_op jit(solution)/shard_map/ppermute | solution.py:33
  71.6 14.8 %collective-permute-start.14 = (bf16[256,512]{1,0:T(8,128)(2,1)S(1)}, bf16[256,512]{1,0:T(8,128)(2,1)S(1)}, u32[]{:S(2)}, u32[]{:S(2)}) collective-permute-start(bf16[256,512]{1,0:T(8,128)(2,1)S(1)} %get-tuple-element.12.refs_0_), channel_id=1, source_target_pairs={{0,2},{1,3},{2,0},{3,1},{4,6},{5,7},{6,4},{7,5},{8,10},{9,11},{10,... | collective-permute-start | bytes 786440 | tf_op jit(solution)/shard_map/ppermute | solution.py:33
  74.7 12.9 %collective-permute-start.13 = (bf16[256,512]{1,0:T(8,128)(2,1)S(1)}, bf16[256,512]{1,0:T(8,128)(2,1)S(1)}, u32[]{:S(2)}, u32[]{:S(2)}) collective-permute-start(bf16[256,512]{1,0:T(8,128)(2,1)S(1)} %get-tuple-element.12.refs_0_), channel_id=1, source_target_pairs={{0,3},{1,0},{2,1},{3,2},{4,7},{5,4},{6,5},{7,6},{8,11},{9,8},{10,9... | collective-permute-start | bytes 786440 | tf_op jit(solution)/shard_map/ppermute | solution.py:33
  74.9 12.9 %collective-permute-start.16 = (bf16[256,512]{1,0:T(8,128)(2,1)S(1)}, bf16[256,512]{1,0:T(8,128)(2,1)S(1)}, u32[]{:S(2)}, u32[]{:S(2)}) collective-permute-start(bf16[256,512]{1,0:T(8,128)(2,1)S(1)} %get-tuple-element.12.refs_0_), channel_id=1, source_target_pairs={{0,4},{1,5},{2,6},{3,7},{4,0},{5,1},{6,2},{7,3},{8,12},{9,13},{10,... | collective-permute-start | bytes 786440 | tf_op jit(solution)/shard_map/ppermute | solution.py:29
  80.3 7.4 %collective-permute-start.19 = (bf16[256,512]{1,0:T(8,128)(2,1)S(1)}, bf16[256,512]{1,0:T(8,128)(2,1)S(1)}, u32[]{:S(2)}, u32[]{:S(2)}) collective-permute-start(bf16[256,512]{1,0:T(8,128)(2,1)S(1)} %collective-permute-done.15.refs_3_), channel_id=1, source_target_pairs={{0,4},{1,5},{2,6},{3,7},{4,0},{5,1},{6,2},{7,3},{8,12},{9,13},{10,... | collective-permute-start | bytes 786440 | tf_op jit(solution)/shard_map/ppermute | solution.py:29
  86.4 2.4 %collective-permute-start.18 = (bf16[256,512]{1,0:T(8,128)(2,1)S(1)}, bf16[256,512]{1,0:T(8,128)(2,1)S(1)}, u32[]{:S(2)}, u32[]{:S(2)}) collective-permute-start(bf16[256,512]{1,0:T(8,128)(2,1)S(1)} %collective-permute-done.14.refs_2_), channel_id=1, source_target_pairs={{0,4},{1,5},{2,6},{3,7},{4,0},{5,1},{6,2},{7,3},{8,12},{9,13},{10,... | collective-permute-start | bytes 786440 | tf_op jit(solution)/shard_map/ppermute | solution.py:29
  87.6 1.5 collective-permute-start.17
  91.5 9.6 %collective-permute-start.29 = (bf16[256,512]{1,0:T(8,128)(2,1)S(1)}, bf16[256,512]{1,0:T(8,128)(2,1)S(1)}, u32[]{:S(2)}, u32[]{:S(2)}) collective-permute-start(bf16[256,512]{1,0:T(8,128)(2,1)S(1)} %shard_map.47.refs_0_), channel_id=1, source_target_pairs={{0,32},{1,33},{2,34},{3,35},{4,12},{5,13},{6,14},{7,15},{8,40},{9,... | collective-permute-start | bytes 786440 | tf_op jit(solution)/shard_map/ppermute | solution.py:37
  91.5 9.5 %collective-permute-start.28 = (bf16[256,512]{1,0:T(8,128)(2,1)S(1)}, bf16[256,512]{1,0:T(8,128)(2,1)S(1)}, u32[]{:S(2)}, u32[]{:S(2)}) collective-permute-start(bf16[256,512]{1,0:T(8,128)(2,1)S(1)} %shard_map.47.refs_0_), channel_id=1, source_target_pairs={{0,64},{1,65},{2,66},{3,67},{4,20},{5,21},{6,22},{7,23},{8,72},{9,... | collective-permute-start | bytes 786440 | tf_op jit(solution)/shard_map/ppermute | solution.py:37
  93.6 8.1 %collective-permute-start.27 = (bf16[256,512]{1,0:T(8,128)(2,1)S(1)}, bf16[256,512]{1,0:T(8,128)(2,1)S(1)}, u32[]{:S(2)}, u32[]{:S(2)}) collective-permute-start(bf16[256,512]{1,0:T(8,128)(2,1)S(1)} %shard_map.47.refs_0_), channel_id=1, source_target_pairs={{0,96},{1,97},{2,98},{3,99},{4,28},{5,29},{6,30},{7,31},{8,104},{9... | collective-permute-start | bytes 786440 | tf_op jit(solution)/shard_map/ppermute | solution.py:37
  95.6 11.4 %collective-permute-start.23 = (bf16[256,512]{1,0:T(8,128)(2,1)S(1)}, bf16[256,512]{1,0:T(8,128)(2,1)S(1)}, u32[]{:S(2)}, u32[]{:S(2)}) collective-permute-start(bf16[256,512]{1,0:T(8,128)(2,1)S(1)} %shard_map.47.refs_0_), channel_id=1, source_target_pairs={{0,4},{1,5},{2,6},{3,7},{4,0},{5,1},{6,2},{7,3},{8,12},{9,13},{10,... | collective-permute-start | bytes 786440 | tf_op jit(solution)/shard_map/ppermute | solution.py:29
  101.7 24.1 %collective-permute-start.32 = (bf16[1024,512]{1,0:T(8,128)(2,1)S(1)}, bf16[1024,512]{1,0:T(8,128)(2,1)S(1)}, u32[]{:S(2)}, u32[]{:S(2)}) collective-permute-start(bf16[1024,512]{1,0:T(8,128)(2,1)S(1)} %pad_maximum_fusion.1.refs_8_.refs_9_), channel_id=1, source_target_pairs={{0,8},{1,9},{2,10},{3,11},{4,36},{5,37},{6,38},{7,39},{8,16},{9,17... | collective-permute-start | bytes 3145736 | tf_op jit(solution)/shard_map/ppermute | solution.py:42
  103.4 25.5 %collective-permute-start.31 = (bf16[1024,512]{1,0:T(8,128)(2,1)S(1)}, bf16[1024,512]{1,0:T(8,128)(2,1)S(1)}, u32[]{:S(2)}, u32[]{:S(2)}) collective-permute-start(bf16[1024,512]{1,0:T(8,128)(2,1)S(1)} %pad_maximum_fusion.1.refs_8_.refs_9_), channel_id=1, source_target_pairs={{0,16},{1,17},{2,18},{3,19},{4,68},{5,69},{6,70},{7,71},{8,24},{9,... | collective-permute-start | bytes 3145736 | tf_op jit(solution)/shard_map/ppermute | solution.py:42
  105.3 23.7 %collective-permute-start.30 = (bf16[1024,512]{1,0:T(8,128)(2,1)S(1)}, bf16[1024,512]{1,0:T(8,128)(2,1)S(1)}, u32[]{:S(2)}, u32[]{:S(2)}) collective-permute-start(bf16[1024,512]{1,0:T(8,128)(2,1)S(1)} %pad_maximum_fusion.1.refs_8_.refs_9_), channel_id=1, source_target_pairs={{0,24},{1,25},{2,26},{3,27},{4,100},{5,101},{6,102},{7,103},{8,0},... | collective-permute-start | bytes 3145736 | tf_op jit(solution)/shard_map/ppermute | solution.py:42
  106.6 7.4 %collective-permute-start.22 = (bf16[256,512]{1,0:T(8,128)(2,1)S(1)}, bf16[256,512]{1,0:T(8,128)(2,1)S(1)}, u32[]{:S(2)}, u32[]{:S(2)}) collective-permute-start(bf16[256,512]{1,0:T(8,128)(2,1)S(1)} %shard_map.47.refs_0_), channel_id=1, source_target_pairs={{0,1},{1,2},{2,3},{3,0},{4,5},{5,6},{6,7},{7,4},{8,9},{9,10},{10,1... | collective-permute-start | bytes 786440 | tf_op jit(solution)/shard_map/ppermute | solution.py:33
  106.9 13.3 %collective-permute-start.21 = (bf16[256,512]{1,0:T(8,128)(2,1)S(1)}, bf16[256,512]{1,0:T(8,128)(2,1)S(1)}, u32[]{:S(2)}, u32[]{:S(2)}) collective-permute-start(bf16[256,512]{1,0:T(8,128)(2,1)S(1)} %shard_map.47.refs_0_), channel_id=1, source_target_pairs={{0,2},{1,3},{2,0},{3,1},{4,6},{5,7},{6,4},{7,5},{8,10},{9,11},{10,... | collective-permute-start | bytes 786440 | tf_op jit(solution)/shard_map/ppermute | solution.py:33
  113.9 8.8 %collective-permute-start.20 = (bf16[256,512]{1,0:T(8,128)(2,1)S(1)}, bf16[256,512]{1,0:T(8,128)(2,1)S(1)}, u32[]{:S(2)}, u32[]{:S(2)}) collective-permute-start(bf16[256,512]{1,0:T(8,128)(2,1)S(1)} %shard_map.47.refs_0_), channel_id=1, source_target_pairs={{0,3},{1,0},{2,1},{3,2},{4,7},{5,4},{6,5},{7,6},{8,11},{9,8},{10,9... | collective-permute-start | bytes 786440 | tf_op jit(solution)/shard_map/ppermute | solution.py:33
  120.2 4.1 %collective-permute-start.26 = (bf16[256,512]{1,0:T(8,128)(2,1)S(1)}, bf16[256,512]{1,0:T(8,128)(2,1)S(1)}, u32[]{:S(2)}, u32[]{:S(2)}) collective-permute-start(bf16[256,512]{1,0:T(8,128)(2,1)S(1)} %collective-permute-done.22.refs_3_), channel_id=1, source_target_pairs={{0,4},{1,5},{2,6},{3,7},{4,0},{5,1},{6,2},{7,3},{8,12},{9,13},{10,... | collective-permute-start | bytes 786440 | tf_op jit(solution)/shard_map/ppermute | solution.py:29
  122.8 2.7 %collective-permute-start.25 = (bf16[256,512]{1,0:T(8,128)(2,1)S(1)}, bf16[256,512]{1,0:T(8,128)(2,1)S(1)}, u32[]{:S(2)}, u32[]{:S(2)}) collective-permute-start(bf16[256,512]{1,0:T(8,128)(2,1)S(1)} %collective-permute-done.21.refs_2_), channel_id=1, source_target_pairs={{0,4},{1,5},{2,6},{3,7},{4,0},{5,1},{6,2},{7,3},{8,12},{9,13},{10,... | collective-permute-start | bytes 786440 | tf_op jit(solution)/shard_map/ppermute | solution.py:29
  124.4 1.5 collective-permute-start.24
  131.9 6.5 %collective-permute-start.35 = (bf16[256,512]{1,0:T(8,128)(2,1)S(1)}, bf16[256,512]{1,0:T(8,128)(2,1)S(1)}, u32[]{:S(2)}, u32[]{:S(2)}) collective-permute-start(bf16[256,512]{1,0:T(8,128)(2,1)S(1)} %get-tuple-element.15.refs_0_), channel_id=1, source_target_pairs={{0,1},{1,2},{2,3},{3,0},{4,5},{5,6},{6,7},{7,4},{8,9},{9,10},{10,1... | collective-permute-start | bytes 786440 | tf_op jit(solution)/shard_map/ppermute | solution.py:33
  132.3 12.1 %collective-permute-start.34 = (bf16[256,512]{1,0:T(8,128)(2,1)S(1)}, bf16[256,512]{1,0:T(8,128)(2,1)S(1)}, u32[]{:S(2)}, u32[]{:S(2)}) collective-permute-start(bf16[256,512]{1,0:T(8,128)(2,1)S(1)} %get-tuple-element.15.refs_0_), channel_id=1, source_target_pairs={{0,2},{1,3},{2,0},{3,1},{4,6},{5,7},{6,4},{7,5},{8,10},{9,11},{10,... | collective-permute-start | bytes 786440 | tf_op jit(solution)/shard_map/ppermute | solution.py:33
  135.3 12.9 %collective-permute-start.33 = (bf16[256,512]{1,0:T(8,128)(2,1)S(1)}, bf16[256,512]{1,0:T(8,128)(2,1)S(1)}, u32[]{:S(2)}, u32[]{:S(2)}) collective-permute-start(bf16[256,512]{1,0:T(8,128)(2,1)S(1)} %get-tuple-element.15.refs_0_), channel_id=1, source_target_pairs={{0,3},{1,0},{2,1},{3,2},{4,7},{5,4},{6,5},{7,6},{8,11},{9,8},{10,9... | collective-permute-start | bytes 786440 | tf_op jit(solution)/shard_map/ppermute | solution.py:33
  135.3 12.9 %collective-permute-start.36 = (bf16[256,512]{1,0:T(8,128)(2,1)S(1)}, bf16[256,512]{1,0:T(8,128)(2,1)S(1)}, u32[]{:S(2)}, u32[]{:S(2)}) collective-permute-start(bf16[256,512]{1,0:T(8,128)(2,1)S(1)} %get-tuple-element.15.refs_0_), channel_id=1, source_target_pairs={{0,4},{1,5},{2,6},{3,7},{4,0},{5,1},{6,2},{7,3},{8,12},{9,13},{10,... | collective-permute-start | bytes 786440 | tf_op jit(solution)/shard_map/ppermute | solution.py:29
  138.4 9.8 %collective-permute-start.39 = (bf16[256,512]{1,0:T(8,128)(2,1)S(1)}, bf16[256,512]{1,0:T(8,128)(2,1)S(1)}, u32[]{:S(2)}, u32[]{:S(2)}) collective-permute-start(bf16[256,512]{1,0:T(8,128)(2,1)S(1)} %collective-permute-done.35.refs_3_), channel_id=1, source_target_pairs={{0,4},{1,5},{2,6},{3,7},{4,0},{5,1},{6,2},{7,3},{8,12},{9,13},{10,... | collective-permute-start | bytes 786440 | tf_op jit(solution)/shard_map/ppermute | solution.py:29
  144.4 4.8 %collective-permute-start.38 = (bf16[256,512]{1,0:T(8,128)(2,1)S(1)}, bf16[256,512]{1,0:T(8,128)(2,1)S(1)}, u32[]{:S(2)}, u32[]{:S(2)}) collective-permute-start(bf16[256,512]{1,0:T(8,128)(2,1)S(1)} %collective-permute-done.34.refs_2_), channel_id=1, source_target_pairs={{0,4},{1,5},{2,6},{3,7},{4,0},{5,1},{6,2},{7,3},{8,12},{9,13},{10,... | collective-permute-start | bytes 786440 | tf_op jit(solution)/shard_map/ppermute | solution.py:29
  148.1 1.5 collective-permute-start.37
  152.0 1.6 %collective-permute-start.40 = (f32[128,512]{1,0:T(8,128)S(1)}, f32[128,512]{1,0:T(8,128)S(1)}, u32[]{:S(2)}, u32[]{:S(2)}) collective-permute-start(f32[128,512]{1,0:T(8,128)S(1)} %get-tuple-element.18), channel_id=1, source_target_pairs={{0,4},{1,5},{2,6},{3,7},{4,0},{5,1},{6,2},{7,3},{8,12},{9,13},{10,... | collective-permute-start | bytes 786440 | tf_op jit(solution)/shard_map/ppermute | solution.py:29

commit v2 on v1

v2 whole, which is shorter than its diff:
```python
import jax
import jax.numpy as jnp
from jax import lax
from jax.experimental import pallas as pl
from jax.experimental.pallas import tpu as pltpu
from jax.sharding import PartitionSpec as P

B = 128
N = 4096
K = 1024
ROWS = 256
COLS = 512
AXES = ("row", "col")
MIB = 1024 * 1024


def device(x, y, core, z):
    return (((x % 4) * 4 + y % 4) * 2 + core) * 4 + z % 4


def pairs(target):
    return [
        (device(x, y, core, z), device(*target(x, y, core, z)))
        for x in range(4) for y in range(4) for core in range(2) for z in range(4)
    ]


def other_core(a):
    return lax.ppermute(a, AXES, pairs(lambda x, y, core, z: (x, y, 1 - core, z)))


def from_z(a, d):
    return lax.ppermute(a, AXES, pairs(lambda x, y, core, z: (x, y, core, z - d)))


def from_x(a, d):
    return lax.ppermute(a, AXES, pairs(lambda x, y, core, z: (x - d, y, core, z)))


def from_y(a, d):
    return lax.ppermute(a, AXES, pairs(lambda x, y, core, z: (x, y - d, core, z)))


def by_offset(own, one, three, two):
    return [own, one, two, three]


def gather_z(a):
    return by_offset(a, *[from_z(a, d) for d in (1, 3, 2)])


def gather_plane(a, b):
    firsts = [from_x(a, 1), from_x(a, 3), from_y(b, 1), from_y(b, 3), from_x(a, 2), from_y(b, 2)]
    a, b, *firsts = lax.optimization_barrier((a, b, *firsts))
    a = jnp.concatenate(by_offset(a, firsts[0], firsts[1], firsts[4]), axis=0)
    b = jnp.concatenate(by_offset(b, firsts[2], firsts[3], firsts[5]), axis=0)
    a, b = lax.optimization_barrier((a, b))
    return by_offset(a, *[from_y(a, d) for d in (1, 3, 2)]), by_offset(b, *[from_x(b, d) for d in (1, 3, 2)])


def block_at(x, y, kind, i, j):
    return ((x + i) & 3) * 8 + ((y + j) & 3) * 2 + kind


def dot_t(a, b):
    return lax.dot_general(a, b, (((1,), (1,)), ((), ())), preferred_element_type=jnp.float32)


def dot(a, b):
    return jnp.dot(a, b, preferred_element_type=jnp.float32)


def first_square(where, keep_d, keep_s, *refs):
    left, right, (panel, square, low), (rows, row, sems) = (
        (refs[0:4], refs[4:8]), (refs[8:12], refs[12:16]), refs[16:19], refs[19:])
    x, y, core, z = where[0], where[1], where[2], where[3]
    row_block, col_block = (x * 4 + y) * 2, z * 8 + core * 4

    def fetch(source, block, target, half):
        return pltpu.make_async_copy(
            source.at[pl.ds(pl.multiple_of(block * B, B), B)],
            rows.at[pl.ds(pl.multiple_of(target * B, B), B), pl.ds(half * 512, 512)],
            sems.at[half, target])

    i = (z - x) & 3
    js = [(core * 2 + pair - y) & 3 for pair in range(2)]
    for c in range(2):
        for j in range(4):
            @pl.when((core == c) & (i == j))
            def _():
                for t in range(4):
                    fetch(right[(t & 1) ^ c][j], js[t >> 1], t, 1).start()

            for pair in range(2):
                @pl.when((core == c) & (js[pair] == j))
                def _():
                    for t in (2 * pair, 2 * pair + 1):
                        fetch(left[(t & 1) ^ c][j], i, t, 0).start()
    kinds = (core, 1 - core)
    for own in range(2):
        fetch(left[own][0], 0, 4 + kinds[own], 0).start()
        fetch(right[own][0], 0, 4 + kinds[own], 1).start()
    for t in range(6):
        fetch(left[0][0], 0, t, 0).wait()
        fetch(right[0][0], 0, t, 1).wait()

    for own in range(2):
        for j in range(4):
            beside = [right[own][i][j * B:(j + 1) * B, :] for i in range(4)]
            chunk = jnp.concatenate([left[own][j][...], jnp.concatenate(beside, axis=0)], axis=1)
            value = dot_t(chunk, rows[...])
            for i in range(4):
                block = block_at(x, y, kinds[own], i, j)
                at = pl.multiple_of(block * B, B)
                for t in range(4):
                    keep = keep_d[0, block, col_block + t].astype(jnp.float32)
                    piece = value[i * B:(i + 1) * B, t * B:(t + 1) * B] * keep
                    panel[pl.ds(at, B), t * B:(t + 1) * B] = piece.astype(jnp.bfloat16)
                for t in range(2):
                    keep = keep_d[0, row_block + t, block].astype(jnp.float32)
                    piece = value[i * B:(i + 1) * B, COLS + t * B:COLS + (t + 1) * B] * keep
                    row[t * B:(t + 1) * B, pl.ds(at, B)] = piece.astype(jnp.bfloat16).T

    finish_square(dot(row[...], panel[...]), keep_s, 0, row_block, col_block, square, low)


def finish_square(value, keep_s, step, row_block, col_block, square, low):
    for t in range(2):
        for u in range(4):
            keep = keep_s[step, row_block + t, col_block + u].astype(jnp.float32)
            piece = value[t * B:(t + 1) * B, u * B:(u + 1) * B] * keep
            square[t * B:(t + 1) * B, u * B:(u + 1) * B] = piece
            low[t * B:(t + 1) * B, u * B:(u + 1) * B] = piece.astype(jnp.bfloat16)


def row_times_panel(own, other, core, z, panel):
    total = None
    for d in range(4):
        for ref, half in ((own[d], core), (other[d], 1 - core)):
            at = pl.multiple_of((((z + d) & 3) * 2 + half) * COLS, COLS)
            term = dot(ref[...], panel[pl.ds(at, COLS), :])
            total = term if total is None else total + term
    return total


def first_density(where, keep_d, *refs):
    own, other, (square, panel), (out,) = refs[:4], refs[4:8], refs[8:10], refs[10:]
    x, y, core, z = where[0], where[1], where[2], where[3]
    cube = row_times_panel(own, other, core, z, panel)
    value = 3.0 * square[...] - 2.0 * cube
    for t in range(2):
        for u in range(4):
            keep = keep_d[1, (x * 4 + y) * 2 + t, z * 8 + core * 4 + u].astype(jnp.float32)
            piece = value[t * B:(t + 1) * B, u * B:(u + 1) * B] * keep
            out[t * B:(t + 1) * B, u * B:(u + 1) * B] = piece.astype(jnp.bfloat16)


def load_panel(parts, panel, sems, x, y):
    copies = []
    for kind in range(2):
        for j in range(4):
            for i in range(4):
                at = pl.multiple_of((block_at(x, y, 0, i, j) if kind == 0 else block_at(x, y, 1, j, i)) * B, B)
                copies.append(pltpu.make_async_copy(
                    parts[kind * 4 + j].at[pl.ds(i * B, B)], panel.at[pl.ds(at, B)],
                    sems.at[(kind * 4 + j) * 4 + i]))
    for copy in copies:
        copy.start()
    for copy in copies:
        copy.wait()


def second_square(where, keep_s, line, *refs):
    parts, (square, low), (panel, sems) = refs[:8], refs[8:10], refs[10:]
    x, y, core, z = where[0], where[1], where[2], where[3]
    load_panel(parts, panel, sems, x, y)
    value = None
    for q in range(8):
        term = dot(line[q * ROWS:(q + 1) * ROWS, :], panel[q * COLS:(q + 1) * COLS, :])
        value = term if value is None else value + term
    finish_square(value, keep_s, 1, (x * 4 + y) * 2, z * 8 + core * 4, square, low)


def second_density(where, *refs):
    own, other, (square,), parts, (stay, leave), (panel, sems) = (
        refs[:4], refs[4:8], refs[8:9], refs[9:17], refs[17:19], refs[19:])
    x, y, core, z = where[0], where[1], where[2], where[3]
    load_panel(parts, panel, sems, x, y)
    value = 3.0 * square[...] - 2.0 * row_times_panel(own, other, core, z, panel)
    first = core == 0
    stay[...] = jnp.where(first, value[:B], value[B:])
    leave[...] = jnp.where(first, value[B:], value[:B])


SMEM = pl.BlockSpec(memory_space=pltpu.SMEM)
VMEM = pl.BlockSpec(memory_space=pltpu.VMEM)
ANY = pl.BlockSpec(memory_space=pl.ANY)


def call(kernel, ins, outs, scratch, flops, moved):
    return pl.pallas_call(
        kernel,
        in_specs=ins,
        out_specs=[VMEM] * len(outs),
        out_shape=outs,
        scratch_shapes=scratch,
        cost_estimate=pl.CostEstimate(flops=flops, bytes_accessed=moved, transcendentals=0),
        compiler_params=pltpu.CompilerParams(vmem_limit_bytes=48 * MIB),
    )


def body(coeffs, coef_pattern, keep_density, keep_square):
    r, z = lax.axis_index("row"), lax.axis_index("col")
    x, y, core = r // 8, (r // 2) % 4, r % 2
    where = jnp.stack([x, y, core, z]).astype(jnp.int32)
    low_block = jax.ShapeDtypeStruct((ROWS, COLS), jnp.bfloat16)
    full_block = jax.ShapeDtypeStruct((ROWS, COLS), jnp.float32)
    panel_scratch = [pltpu.VMEM((N, COLS), jnp.bfloat16), pltpu.SemaphoreType.DMA((32,))]

    wide = jnp.concatenate(gather_z(coeffs), axis=1)
    pattern = lax.dynamic_slice(coef_pattern, (r, 0), (1, 8)).reshape(4, 2)
    pattern = jnp.concatenate([pattern, pattern], axis=0)
    pattern = lax.dynamic_slice(pattern, (z, 0), (4, 2)).reshape(1, 8)
    wide = wide * jnp.repeat(pattern, B, 1).astype(jnp.bfloat16)
    left, right = lax.optimization_barrier((wide[:, :512], wide[:, 512:]))
    left, right = gather_plane(left, right)
    left_other, right_other = [other_core(part) for part in left], [other_core(part) for part in right]
    panel, square, low = call(
        first_square, [SMEM] * 3 + [VMEM] * 16,
        [jax.ShapeDtypeStruct((N, COLS), jnp.bfloat16), full_block, low_block],
        [
            pltpu.VMEM((COLS + ROWS, K), jnp.bfloat16),
            pltpu.VMEM((ROWS, N), jnp.bfloat16),
            pltpu.SemaphoreType.DMA((2, 6)),
        ],
        2 * N * K * (COLS + ROWS) + 2 * ROWS * N * COLS, 13 * MIB,
    )(where, keep_density, keep_square, *left, *left_other, *right, *right_other)

    own = gather_z(low)
    other = [other_core(part) for part in own]
    (current,) = call(
        first_density, [SMEM] * 2 + [VMEM] * 10, [low_block], [], 2 * ROWS * N * COLS, 7 * MIB,
    )(where, keep_density, *own, *other, square, panel)

    line = lax.all_gather(current, AXES, axis=0, tiled=True, axis_index_groups=[
        [device(x, y, core, z) for z in range(4) for core in range(2)] for x in range(4) for y in range(4)])
    even, odd = lax.optimization_barrier((current[:B], current[B:]))
    even, odd = gather_plane(even, odd)
    parts = even + odd
    square, low = call(
        second_square, [SMEM] * 2 + [VMEM] * 9, [full_block, low_block],
        panel_scratch, 2 * ROWS * N * COLS, 7 * MIB,
    )(where, keep_square, line, *parts)

    own = gather_z(low)
    other = [other_core(part) for part in own]
    half = jax.ShapeDtypeStruct((B, COLS), jnp.float32)
    stay, leave = call(
        second_density, [SMEM] + [VMEM] * 17, [half, half],
        panel_scratch, 2 * ROWS * N * COLS, 8 * MIB,
    )(where, *own, *other, square, *parts)
    come = other_core(leave)
    first = core == 0
    return jnp.concatenate([jnp.where(first, stay, come), jnp.where(first, come, stay)], axis=1)


def solution(mesh):
    placed = (P("row", "col"), P(), P(), P())
    return jax.shard_map(
        body, mesh=mesh, in_specs=placed, out_specs=P("row", "col"), check_vma=False
    )
```

time: 155 us -> 211 us (1.36)
  waiting for transfers between devices: 58.6 us -> 78.7 us
  Pallas kernels: 21.7 us -> 35.7 us
  between operations: 0.13 us -> 13.6 us
  local copies, waits for them, and re-layouts: 0.08 us -> 8.7 us
    ppermute x12 -> x24, waiting for transfers between devices: 28.1 us -> 58.9 us  [the longest x12 49.3 us: from_y(): lax.ppermute(a, AXES, pairs(lambda x, y, core, z: (x, y - d, core, z)))]
    ppermute x12 -> x24, starting transfers between devices: 18.5 us -> 32 us  [the longest x12 20.5 us: from_y(): lax.ppermute(a, AXES, pairs(lambda x, y, core, z: (x, y - d, core, z)))]
    pallas_call x3, Pallas kernels: 19.4 us -> 31.5 us  [the longest x1 12 us: body(): call(first_square, [SMEM] * 3 + [VMEM] * 16, [jax.ShapeDtypeStruct((N, CO...]
    ppermute x17, starting transfers between devices: 35.1 us -> 25.7 us  [other_core(): lax.ppermute(a, AXES, pairs(lambda x, y, core, z: (x, y, 1 - core, z)))]
    ppermute x12 -> x9, waiting for transfers between devices: 20.8 us -> 13.4 us  [from_z(): lax.ppermute(a, AXES, pairs(lambda x, y, core, z: (x, y, core, z - d)))]
    unnamed x4 -> x24, local copies, waits for them, and re-layouts: 0.01 us -> 7.06 us
    ppermute x12 -> x9, starting transfers between devices: 17.5 us -> 12.7 us  [from_z(): lax.ppermute(a, AXES, pairs(lambda x, y, core, z: (x, y, core, z - d)))]
    ppermute x17, waiting for transfers between devices: 9.62 us -> 6.35 us  [other_core(): lax.ppermute(a, AXES, pairs(lambda x, y, core, z: (x, y, 1 - core, z)))]
  transfers between devices with their start and end apart: 41 -> 51, of which waited for: 22 -> 21; matrix products, arithmetic and copies ran while one was open for 0% -> 1% of each run, Pallas kernels for 0% -> 0%
where the time goes in v2:
time: 211 us; the launch traced here: 209 us
  waiting for transfers between devices  78.7 us (37%)
  starting transfers between devices  70.3 us (33%)
  Pallas kernels  35.7 us (17%)
  between operations  13.6 us (6%)
  local copies, waits for them, and re-layouts  8.7 us (4%)
  other arithmetic  2.13 us (1%)
    ppermute x12, waiting for transfers between devices, from_y(): lax.ppermute(a, AXES, pairs(lambda x, y, core, z: (x, y - d, core, z)))  49.3 us
    ppermute x17, starting transfers between devices, other_core(): lax.ppermute(a, AXES, pairs(lambda x, y, core, z: (x, y, 1 - core, z)))  25.7 us
    ppermute x12, starting transfers between devices, from_y(): lax.ppermute(a, AXES, pairs(lambda x, y, core, z: (x, y - d, core, z)))  20.5 us
    ppermute x9, waiting for transfers between devices, from_z(): lax.ppermute(a, AXES, pairs(lambda x, y, core, z: (x, y, core, z - d)))  13.4 us
    ppermute x9, starting transfers between devices, from_z(): lax.ppermute(a, AXES, pairs(lambda x, y, core, z: (x, y, core, z - d)))  12.7 us
    pallas_call x1, Pallas kernels, body(): call(first_square, [SMEM] * 3 + [VMEM] * 16, [jax.ShapeDtypeStruct((N, CO...  12 us
    ppermute x12, starting transfers between devices, from_x(): lax.ppermute(a, AXES, pairs(lambda x, y, core, z: (x - d, y, core, z)))  11.5 us
    pallas_call x1, Pallas kernels, body(): call(second_density, [SMEM] + [VMEM] * 17, [half, half], panel_scratch, 2...  9.83 us
  transfers between devices with their start and end apart: 51, of which 21 were waited for; matrix products, arithmetic and copies ran while one was open for 1% of the time, Pallas kernels for 0%

profile of v2, /device:TPU:1, one launch (start us, length us, event | category | flops | bytes accessed | tf_op | source)
XLA Modules:
  0.0 209.1 jit_solution(13625391151078652264)
XLA Ops:
  6.5 4.4 %collective-permute-start.1 = (bf16[128,256]{1,0:T(8,128)(2,1)}, bf16[128,256]{1,0:T(8,128)(2,1)S(1)}, u32[]{:S(2)}, u32[]{:S(2)}) collective-permute-start(bf16[128,256]{1,0:T(8,128)(2,1)} %param.4), channel_id=1, source_target_pairs={{0,2},{1,3},{2,0},{3,1},{4,6},{5,7},{6,4},{7,5},{8,10},{9,11},{10,... | collective-permute-start | bytes 196616 | tf_op jit(solution)/shard_map/ppermute | solution.py:33
  11.4 1.0 collective-permute-start.2
  13.2 1.4 collective-permute-done
  14.7 1.3 collective-permute-done.2
  16.9 2.8 %collective-permute-start.7 = (bf16[128,512]{1,0:T(8,128)(2,1)S(1)}, bf16[128,512]{1,0:T(8,128)(2,1)S(1)}, u32[]{:S(2)}, u32[]{:S(2)}) collective-permute-start(bf16[128,512]{1,0:T(8,128)(2,1)S(1)} %get-tuple-element.38), channel_id=1, source_target_pairs={{0,64},{1,65},{2,66},{3,67},{4,68},{5,69},{6,70},{7,71},{8,72},{9,... | collective-permute-start | bytes 393224 | tf_op jit(solution)/shard_map/ppermute | solution.py:37
  20.0 2.4 %collective-permute-start.3 = (bf16[128,512]{1,0:T(8,128)(2,1)S(1)}, bf16[128,512]{1,0:T(8,128)(2,1)S(1)}, u32[]{:S(2)}, u32[]{:S(2)}) collective-permute-start(bf16[128,512]{1,0:T(8,128)(2,1)S(1)} %get-tuple-element.38), channel_id=1, source_target_pairs={{0,96},{1,97},{2,98},{3,99},{4,100},{5,101},{6,102},{7,103},{8,104... | collective-permute-start | bytes 393224 | tf_op jit(solution)/shard_map/ppermute | solution.py:37
  22.4 2.9 %collective-permute-start.8 = (bf16[128,512]{1,0:T(8,128)(2,1)S(1)}, bf16[128,512]{1,0:T(8,128)(2,1)S(1)}, u32[]{:S(2)}, u32[]{:S(2)}) collective-permute-start(bf16[128,512]{1,0:T(8,128)(2,1)S(1)} %get-tuple-element.42), channel_id=1, source_target_pairs={{0,16},{1,17},{2,18},{3,19},{4,20},{5,21},{6,22},{7,23},{8,24},{9,... | collective-permute-start | bytes 393224 | tf_op jit(solution)/shard_map/ppermute | solution.py:41
  25.7 2.3 %collective-permute-start.5 = (bf16[128,512]{1,0:T(8,128)(2,1)S(1)}, bf16[128,512]{1,0:T(8,128)(2,1)S(1)}, u32[]{:S(2)}, u32[]{:S(2)}) collective-permute-start(bf16[128,512]{1,0:T(8,128)(2,1)S(1)} %get-tuple-element.42), channel_id=1, source_target_pairs={{0,24},{1,25},{2,26},{3,27},{4,28},{5,29},{6,30},{7,31},{8,0},{9,1... | collective-permute-start | bytes 393224 | tf_op jit(solution)/shard_map/ppermute | solution.py:41
  28.0 3.7 %collective-permute-done.6 = bf16[128,512]{1,0:T(8,128)(2,1)S(1)} collective-permute-done((bf16[128,512]{1,0:T(8,128)(2,1)S(1)}, bf16[128,512]{1,0:T(8,128)(2,1)S(1)}, u32[]{:S(2)}, u32[]{:S(2)}) %collective-permute-start.6) | collective-permute-done | bytes 131104 | tf_op jit(solution)/shard_map/ppermute | solution.py:41
  31.8 3.3 %collective-permute-start.12 = (bf16[512,512]{1,0:T(8,128)(2,1)S(1)}, bf16[512,512]{1,0:T(8,128)(2,1)S(1)}, u32[]{:S(2)}, u32[]{:S(2)}) collective-permute-start(bf16[512,512]{1,0:T(8,128)(2,1)S(1)} %get-tuple-element.46.refs_0_), channel_id=1, source_target_pairs={{0,4},{1,5},{2,6},{3,7},{4,0},{5,1},{6,2},{7,3},{8,12},{9,13},{10,... | collective-permute-start | bytes 1572872 | tf_op jit(solution)/shard_map/ppermute | solution.py:29
  35.1 4.2 %collective-permute-start.10 = (bf16[512,512]{1,0:T(8,128)(2,1)S(1)}, bf16[512,512]{1,0:T(8,128)(2,1)S(1)}, u32[]{:S(2)}, u32[]{:S(2)}) collective-permute-start(bf16[512,512]{1,0:T(8,128)(2,1)S(1)} %get-tuple-element.46.refs_0_), channel_id=1, source_target_pairs={{0,16},{1,17},{2,18},{3,19},{4,20},{5,21},{6,22},{7,23},{8,24},{9,... | collective-permute-start | bytes 1572872 | tf_op jit(solution)/shard_map/ppermute | solution.py:41
  39.9 10.5 %collective-permute-done.11.refs_3_ = bf16[512,512]{1,0:T(8,128)(2,1)S(1)} collective-permute-done((bf16[512,512]{1,0:T(8,128)(2,1)S(1)}, bf16[512,512]{1,0:T(8,128)(2,1)S(1)}, u32[]{:S(2)}, u32[]{:S(2)}) %collective-permute-start.11) | collective-permute-done | bytes 524320 | tf_op jit(solution)/shard_map/ppermute | solution.py:41
  50.4 12.2 %collective-permute-done.10.refs_2_ = bf16[512,512]{1,0:T(8,128)(2,1)S(1)} collective-permute-done((bf16[512,512]{1,0:T(8,128)(2,1)S(1)}, bf16[512,512]{1,0:T(8,128)(2,1)S(1)}, u32[]{:S(2)}, u32[]{:S(2)}) %collective-permute-start.10) | collective-permute-done | bytes 524320 | tf_op jit(solution)/shard_map/ppermute | solution.py:41
  63.5 3.3 %collective-permute-start.13 = (bf16[512,512]{1,0:T(8,128)(2,1)S(1)}, bf16[512,512]{1,0:T(8,128)(2,1)}, u32[]{:S(2)}, u32[]{:S(2)}) collective-permute-start(bf16[512,512]{1,0:T(8,128)(2,1)S(1)} %collective-permute-done.9.refs_1_), channel_id=1, source_target_pairs={{0,4},{1,5},{2,6},{3,7},{4,0},{5,1},{6,2},{7,3},{8,12},{9,13},{10,... | collective-permute-start | bytes 1572872 | tf_op jit(solution)/shard_map/ppermute | solution.py:29
  66.8 8.6 %collective-permute-done.16.refs_9_ = bf16[512,512]{1,0:T(8,128)(2,1)} collective-permute-done((bf16[512,512]{1,0:T(8,128)(2,1)S(1)}, bf16[512,512]{1,0:T(8,128)(2,1)}, u32[]{:S(2)}, u32[]{:S(2)}) %collective-permute-start.16) | collective-permute-done | bytes 524320 | tf_op jit(solution)/shard_map/ppermute | solution.py:37
  75.4 1.6 collective-permute-start.21
  78.0 1.0 collective-permute-done.21.refs_14_
  78.9 1.2 collective-permute-done.20.refs_13_
  81.6 1.0 copy-done.10
  82.7 12.0 %shard_map.46 = (bf16[4096,512]{1,0:T(8,128)(2,1)}, f32[256,512]{1,0:T(8,128)S(1)}, bf16[256,512]{1,0:T(8,128)(2,1)S(1)}) custom-call(s32[4]{0:T(128)S(1)} %pad_add_fusion.1.where, s32[2,32,32]{2,1,0:T(8,128)S(1)} %copy-done.6, s32[2,32,32]{2,1,0:T(8,128)S(1)} %copy-done.7, bf16[512,512]{1,0:T(8,128)(2,1)S(1)} %get-tuple-element.46.refs_0_, ...), custom_call_target="tpu_custom_call" | custom-call | flops 7516192768 | bytes 13631488 | tf_op jit(solution)/shard_map/pallas_call | solution.py:228
  94.7 1.6 collective-permute-start.24
  96.3 1.4 collective-permute-start.23
  97.7 1.0 collective-permute-start.26
  98.7 10.6 %collective-permute-done.25.refs_3_ = bf16[256,512]{1,0:T(8,128)(2,1)S(1)} collective-permute-done((bf16[256,512]{1,0:T(8,128)(2,1)S(1)}, bf16[256,512]{1,0:T(8,128)(2,1)S(1)}, u32[]{:S(2)}, u32[]{:S(2)}) %collective-permute-start.25) | collective-permute-done | bytes 262176 | tf_op jit(solution)/shard_map/ppermute | solution.py:33
  109.3 1.0 collective-permute-start.29
  112.2 4.2 %shard_map.47 = bf16[256,512]{1,0:T(8,128)(2,1)} custom-call(s32[4]{0:T(128)S(1)} %pad_add_fusion.1.where, s32[2,32,32]{2,1,0:T(8,128)S(1)} %copy-done.6, bf16[256,512]{1,0:T(8,128)(2,1)S(1)} %get-tuple-element.48.refs_0_, bf16[256,512]{1,0:T(8,128)(2,1)S(1)} %collective-permute-done.23.refs_1_, bf16[256,512]{1,0:T(8,128)(2,1)S(1)} %collective-permute-done.24.refs_2_, ...), custom_call_target="tpu_custom_call" | custom-call | flops 1073741824 | bytes 7340032 | tf_op jit(solution)/shard_map/pallas_call | solution.py:241
  116.4 1.0 fusion
  117.6 1.7 collective-permute-start.31
  119.2 1.0 collective-permute-start.30
  120.3 4.6 %collective-permute-start.35 = (bf16[128,512]{1,0:T(8,128)(2,1)S(1)}, bf16[128,512]{1,0:T(8,128)(2,1)S(1)}, u32[]{:S(2)}, u32[]{:S(2)}) collective-permute-start(bf16[128,512]{1,0:T(8,128)(2,1)S(1)} %get-tuple-element.57), channel_id=1, source_target_pairs={{0,16},{1,17},{2,18},{3,19},{4,20},{5,21},{6,22},{7,23},{8,24},{9,... | collective-permute-start | bytes 393224 | tf_op jit(solution)/shard_map/ppermute | solution.py:41
  124.8 2.7 %collective-permute-start.32 = (bf16[128,512]{1,0:T(8,128)(2,1)S(1)}, bf16[128,512]{1,0:T(8,128)(2,1)S(1)}, u32[]{:S(2)}, u32[]{:S(2)}) collective-permute-start(bf16[128,512]{1,0:T(8,128)(2,1)S(1)} %get-tuple-element.57), channel_id=1, source_target_pairs={{0,24},{1,25},{2,26},{3,27},{4,28},{5,29},{6,30},{7,31},{8,0},{9,1... | collective-permute-start | bytes 393224 | tf_op jit(solution)/shard_map/ppermute | solution.py:41
  127.8 3.3 %collective-permute-done.33 = bf16[128,512]{1,0:T(8,128)(2,1)S(1)} collective-permute-done((bf16[128,512]{1,0:T(8,128)(2,1)S(1)}, bf16[128,512]{1,0:T(8,128)(2,1)S(1)}, u32[]{:S(2)}, u32[]{:S(2)}) %collective-permute-start.33) | collective-permute-done | bytes 131104 | tf_op jit(solution)/shard_map/ppermute | solution.py:41
  132.1 1.8 collective-permute-start.37
  134.7 2.4 %collective-permute-start.40 = (bf16[512,512]{1,0:T(8,128)(2,1)S(1)}, bf16[512,512]{1,0:T(8,128)(2,1)S(1)}, u32[]{:S(2)}, u32[]{:S(2)}) collective-permute-start(bf16[512,512]{1,0:T(8,128)(2,1)S(1)} %pad_maximum_fusion.3.refs_4_.refs_13_), channel_id=1, source_target_pairs={{0,64},{1,65},{2,66},{3,67},{4,68},{5,69},{6,70},{7,71},{8,72},{9,... | collective-permute-start | bytes 1572872 | tf_op jit(solution)/shard_map/ppermute | solution.py:37
  137.2 8.3 %collective-permute-done.38.refs_3_.refs_12_ = bf16[512,512]{1,0:T(8,128)(2,1)S(1)} collective-permute-done((bf16[512,512]{1,0:T(8,128)(2,1)S(1)}, bf16[512,512]{1,0:T(8,128)(2,1)S(1)}, u32[]{:S(2)}, u32[]{:S(2)}) %collective-permute-start.38) | collective-permute-done | bytes 524320 | tf_op jit(solution)/shard_map/ppermute | solution.py:41
  146.1 8.3 %collective-permute-done.37.refs_2_.refs_11_ = bf16[512,512]{1,0:T(8,128)(2,1)S(1)} collective-permute-done((bf16[512,512]{1,0:T(8,128)(2,1)S(1)}, bf16[512,512]{1,0:T(8,128)(2,1)S(1)}, u32[]{:S(2)}, u32[]{:S(2)}) %collective-permute-start.37) | collective-permute-done | bytes 524320 | tf_op jit(solution)/shard_map/ppermute | solution.py:41
  154.4 2.7 %collective-permute-done.36.refs_1_.refs_10_ = bf16[512,512]{1,0:T(8,128)(2,1)S(1)} collective-permute-done((bf16[512,512]{1,0:T(8,128)(2,1)S(1)}, bf16[512,512]{1,0:T(8,128)(2,1)S(1)}, u32[]{:S(2)}, u32[]{:S(2)}) %collective-permute-start.36) | collective-permute-done | bytes 524320 | tf_op jit(solution)/shard_map/ppermute | solution.py:41
  157.9 0.9 collective-permute-done.39.refs_5_.refs_14_
  159.6 1.0 copy-done.3
  160.7 1.0 copy-done.5
  161.7 9.8 %shard_map.48 = (f32[256,512]{1,0:T(8,128)S(1)}, bf16[256,512]{1,0:T(8,128)(2,1)S(1)}) custom-call(s32[4]{0:T(128)S(1)} %pad_add_fusion.1.where, s32[2,32,32]{2,1,0:T(8,128)S(1)} %copy-done.8, bf16[2048,512]{1,0:T(8,128)(2,1)} %all-gather.2.cloned.1.call-done.line, bf16[512,512]{1,0:T(8,128)(2,1)S(1)} %pad_maximum_fusion.2.refs_0_.refs_9_, ...), custom_call_target="tpu_custom_call" | custom-call | flops 1073741824 | bytes 7340032 | tf_op jit(solution)/shard_map/pallas_call | solution.py:250
  171.6 3.7 %collective-permute-start.43 = (bf16[256,512]{1,0:T(8,128)(2,1)S(1)}, bf16[256,512]{1,0:T(8,128)(2,1)S(1)}, u32[]{:S(2)}, u32[]{:S(2)}) collective-permute-start(bf16[256,512]{1,0:T(8,128)(2,1)S(1)} %get-tuple-element.63.refs_0_), channel_id=1, source_target_pairs={{0,2},{1,3},{2,0},{3,1},{4,6},{5,7},{6,4},{7,5},{8,10},{9,11},{10,... | collective-permute-start | bytes 786440 | tf_op jit(solution)/shard_map/ppermute | solution.py:33
  175.3 3.8 %collective-permute-start.45 = (bf16[256,512]{1,0:T(8,128)(2,1)S(1)}, bf16[256,512]{1,0:T(8,128)(2,1)S(1)}, u32[]{:S(2)}, u32[]{:S(2)}) collective-permute-start(bf16[256,512]{1,0:T(8,128)(2,1)S(1)} %get-tuple-element.63.refs_0_), channel_id=1, source_target_pairs={{0,4},{1,5},{2,6},{3,7},{4,0},{5,1},{6,2},{7,3},{8,12},{9,13},{10,... | collective-permute-start | bytes 786440 | tf_op jit(solution)/shard_map/ppermute | solution.py:29
  179.1 6.3 %collective-permute-start.48 = (bf16[256,512]{1,0:T(8,128)(2,1)S(1)}, bf16[256,512]{1,0:T(8,128)(2,1)S(1)}, u32[]{:S(2)}, u32[]{:S(2)}) collective-permute-start(bf16[256,512]{1,0:T(8,128)(2,1)S(1)} %collective-permute-done.44.refs_3_), channel_id=1, source_target_pairs={{0,4},{1,5},{2,6},{3,7},{4,0},{5,1},{6,2},{7,3},{8,12},{9,13},{10,... | collective-permute-start | bytes 786440 | tf_op jit(solution)/shard_map/ppermute | solution.py:29
  185.4 2.8 %collective-permute-start.47 = (bf16[256,512]{1,0:T(8,128)(2,1)S(1)}, bf16[256,512]{1,0:T(8,128)(2,1)S(1)}, u32[]{:S(2)}, u32[]{:S(2)}) collective-permute-start(bf16[256,512]{1,0:T(8,128)(2,1)S(1)} %collective-permute-done.43.refs_2_), channel_id=1, source_target_pairs={{0,4},{1,5},{2,6},{3,7},{4,0},{5,1},{6,2},{7,3},{8,12},{9,13},{10,... | collective-permute-start | bytes 786440 | tf_op jit(solution)/shard_map/ppermute | solution.py:29
  188.2 1.1 collective-permute-done.47.refs_6_
  189.7 9.8 %shard_map.49 = (f32[128,512]{1,0:T(8,128)S(1)}, f32[128,512]{1,0:T(8,128)}) custom-call(s32[4]{0:T(128)S(1)} %pad_add_fusion.1.where, bf16[256,512]{1,0:T(8,128)(2,1)S(1)} %get-tuple-element.63.refs_0_, bf16[256,512]{1,0:T(8,128)(2,1)S(1)} %collective-permute-done.42.refs_1_, bf16[256,512]{1,0:T(8,128)(2,1)S(1)} %collective-permute-done.43.refs_2_, ...), custom_call_target="tpu_custom_call" | custom-call | flops 1073741824 | bytes 8388608 | tf_op jit(solution)/shard_map/pallas_call | solution.py:258
  200.0 1.4 collective-permute-done.49
  (100 shorter events, 15.1 us)
Async XLA Ops:
  6.5 153.1 %all-gather.2.cloned.1.call-start = ((), (), s32[]{:S(2)}) async-start(), calls=%async_computation | async-start | bytes 2359296 | tf_op jit(solution)/shard_map/all_gather | solution.py:245
  6.5 6.7 %collective-permute-start.1 = (bf16[128,256]{1,0:T(8,128)(2,1)}, bf16[128,256]{1,0:T(8,128)(2,1)S(1)}, u32[]{:S(2)}, u32[]{:S(2)}) collective-permute-start(bf16[128,256]{1,0:T(8,128)(2,1)} %param.4), channel_id=1, source_target_pairs={{0,2},{1,3},{2,0},{3,1},{4,6},{5,7},{6,4},{7,5},{8,10},{9,11},{10,... | collective-permute-start | bytes 196616 | tf_op jit(solution)/shard_map/ppermute | solution.py:33
  11.0 3.7 %collective-permute-start = (bf16[128,256]{1,0:T(8,128)(2,1)}, bf16[128,256]{1,0:T(8,128)(2,1)S(1)}, u32[]{:S(2)}, u32[]{:S(2)}) collective-permute-start(bf16[128,256]{1,0:T(8,128)(2,1)} %param.4), channel_id=1, source_target_pairs={{0,3},{1,0},{2,1},{3,2},{4,7},{5,4},{6,5},{7,6},{8,11},{9,8},{10,9... | collective-permute-start | bytes 196616 | tf_op jit(solution)/shard_map/ppermute | solution.py:33
  11.4 4.5 %collective-permute-start.2 = (bf16[128,256]{1,0:T(8,128)(2,1)}, bf16[128,256]{1,0:T(8,128)(2,1)S(1)}, u32[]{:S(2)}, u32[]{:S(2)}) collective-permute-start(bf16[128,256]{1,0:T(8,128)(2,1)} %param.4), channel_id=1, source_target_pairs={{0,1},{1,2},{2,3},{3,0},{4,5},{5,6},{6,7},{7,4},{8,9},{9,10},{10,1... | collective-permute-start | bytes 196616 | tf_op jit(solution)/shard_map/ppermute | solution.py:33
  16.9 8.8 %collective-permute-start.7 = (bf16[128,512]{1,0:T(8,128)(2,1)S(1)}, bf16[128,512]{1,0:T(8,128)(2,1)S(1)}, u32[]{:S(2)}, u32[]{:S(2)}) collective-permute-start(bf16[128,512]{1,0:T(8,128)(2,1)S(1)} %get-tuple-element.38), channel_id=1, source_target_pairs={{0,64},{1,65},{2,66},{3,67},{4,68},{5,69},{6,70},{7,71},{8,72},{9,... | collective-permute-start | bytes 393224 | tf_op jit(solution)/shard_map/ppermute | solution.py:37
  19.7 8.3 %collective-permute-start.4 = (bf16[128,512]{1,0:T(8,128)(2,1)S(1)}, bf16[128,512]{1,0:T(8,128)(2,1)S(1)}, u32[]{:S(2)}, u32[]{:S(2)}) collective-permute-start(bf16[128,512]{1,0:T(8,128)(2,1)S(1)} %get-tuple-element.38), channel_id=1, source_target_pairs={{0,32},{1,33},{2,34},{3,35},{4,36},{5,37},{6,38},{7,39},{8,40},{9,... | collective-permute-start | bytes 393224 | tf_op jit(solution)/shard_map/ppermute | solution.py:37
  20.0 8.0 %collective-permute-start.3 = (bf16[128,512]{1,0:T(8,128)(2,1)S(1)}, bf16[128,512]{1,0:T(8,128)(2,1)S(1)}, u32[]{:S(2)}, u32[]{:S(2)}) collective-permute-start(bf16[128,512]{1,0:T(8,128)(2,1)S(1)} %get-tuple-element.38), channel_id=1, source_target_pairs={{0,96},{1,97},{2,98},{3,99},{4,100},{5,101},{6,102},{7,103},{8,104... | collective-permute-start | bytes 393224 | tf_op jit(solution)/shard_map/ppermute | solution.py:37
  22.4 5.6 %collective-permute-start.8 = (bf16[128,512]{1,0:T(8,128)(2,1)S(1)}, bf16[128,512]{1,0:T(8,128)(2,1)S(1)}, u32[]{:S(2)}, u32[]{:S(2)}) collective-permute-start(bf16[128,512]{1,0:T(8,128)(2,1)S(1)} %get-tuple-element.42), channel_id=1, source_target_pairs={{0,16},{1,17},{2,18},{3,19},{4,20},{5,21},{6,22},{7,23},{8,24},{9,... | collective-permute-start | bytes 393224 | tf_op jit(solution)/shard_map/ppermute | solution.py:41
  25.3 6.4 %collective-permute-start.6 = (bf16[128,512]{1,0:T(8,128)(2,1)S(1)}, bf16[128,512]{1,0:T(8,128)(2,1)S(1)}, u32[]{:S(2)}, u32[]{:S(2)}) collective-permute-start(bf16[128,512]{1,0:T(8,128)(2,1)S(1)} %get-tuple-element.42), channel_id=1, source_target_pairs={{0,8},{1,9},{2,10},{3,11},{4,12},{5,13},{6,14},{7,15},{8,16},{9,17... | collective-permute-start | bytes 393224 | tf_op jit(solution)/shard_map/ppermute | solution.py:41
  25.7 6.0 %collective-permute-start.5 = (bf16[128,512]{1,0:T(8,128)(2,1)S(1)}, bf16[128,512]{1,0:T(8,128)(2,1)S(1)}, u32[]{:S(2)}, u32[]{:S(2)}) collective-permute-start(bf16[128,512]{1,0:T(8,128)(2,1)S(1)} %get-tuple-element.42), channel_id=1, source_target_pairs={{0,24},{1,25},{2,26},{3,27},{4,28},{5,29},{6,30},{7,31},{8,0},{9,1... | collective-permute-start | bytes 393224 | tf_op jit(solution)/shard_map/ppermute | solution.py:41
  31.8 8.1 %collective-permute-start.12 = (bf16[512,512]{1,0:T(8,128)(2,1)S(1)}, bf16[512,512]{1,0:T(8,128)(2,1)S(1)}, u32[]{:S(2)}, u32[]{:S(2)}) collective-permute-start(bf16[512,512]{1,0:T(8,128)(2,1)S(1)} %get-tuple-element.46.refs_0_), channel_id=1, source_target_pairs={{0,4},{1,5},{2,6},{3,7},{4,0},{5,1},{6,2},{7,3},{8,12},{9,13},{10,... | collective-permute-start | bytes 1572872 | tf_op jit(solution)/shard_map/ppermute | solution.py:29
  35.1 15.3 %collective-permute-start.11 = (bf16[512,512]{1,0:T(8,128)(2,1)S(1)}, bf16[512,512]{1,0:T(8,128)(2,1)S(1)}, u32[]{:S(2)}, u32[]{:S(2)}) collective-permute-start(bf16[512,512]{1,0:T(8,128)(2,1)S(1)} %get-tuple-element.46.refs_0_), channel_id=1, source_target_pairs={{0,8},{1,9},{2,10},{3,11},{4,12},{5,13},{6,14},{7,15},{8,16},{9,17... | collective-permute-start | bytes 1572872 | tf_op jit(solution)/shard_map/ppermute | solution.py:41
  35.1 27.5 %collective-permute-start.10 = (bf16[512,512]{1,0:T(8,128)(2,1)S(1)}, bf16[512,512]{1,0:T(8,128)(2,1)S(1)}, u32[]{:S(2)}, u32[]{:S(2)}) collective-permute-start(bf16[512,512]{1,0:T(8,128)(2,1)S(1)} %get-tuple-element.46.refs_0_), channel_id=1, source_target_pairs={{0,16},{1,17},{2,18},{3,19},{4,20},{5,21},{6,22},{7,23},{8,24},{9,... | collective-permute-start | bytes 1572872 | tf_op jit(solution)/shard_map/ppermute | solution.py:41
  39.3 23.4 %collective-permute-start.9 = (bf16[512,512]{1,0:T(8,128)(2,1)S(1)}, bf16[512,512]{1,0:T(8,128)(2,1)S(1)}, u32[]{:S(2)}, u32[]{:S(2)}) collective-permute-start(bf16[512,512]{1,0:T(8,128)(2,1)S(1)} %get-tuple-element.46.refs_0_), channel_id=1, source_target_pairs={{0,24},{1,25},{2,26},{3,27},{4,28},{5,29},{6,30},{7,31},{8,0},{9,1... | collective-permute-start | bytes 1572872 | tf_op jit(solution)/shard_map/ppermute | solution.py:41
  39.3 24.1 %collective-permute-start.19 = (bf16[512,512]{1,0:T(8,128)(2,1)S(1)}, bf16[512,512]{1,0:T(8,128)(2,1)S(1)}, u32[]{:S(2)}, u32[]{:S(2)}) collective-permute-start(bf16[512,512]{1,0:T(8,128)(2,1)S(1)} %get-tuple-element.47.refs_8_), channel_id=1, source_target_pairs={{0,4},{1,5},{2,6},{3,7},{4,0},{5,1},{6,2},{7,3},{8,12},{9,13},{10,... | collective-permute-start | bytes 1572872 | tf_op jit(solution)/shard_map/ppermute | solution.py:29
  39.9 23.6 %collective-permute-start.18 = (bf16[512,512]{1,0:T(8,128)(2,1)S(1)}, bf16[512,512]{1,0:T(8,128)(2,1)}, u32[]{:S(2)}, u32[]{:S(2)}) collective-permute-start(bf16[512,512]{1,0:T(8,128)(2,1)S(1)} %get-tuple-element.47.refs_8_), channel_id=1, source_target_pairs={{0,32},{1,33},{2,34},{3,35},{4,36},{5,37},{6,38},{7,39},{8,40},{9,... | collective-permute-start | bytes 1572872 | tf_op jit(solution)/shard_map/ppermute | solution.py:37
  50.4 16.4 %collective-permute-start.17 = (bf16[512,512]{1,0:T(8,128)(2,1)S(1)}, bf16[512,512]{1,0:T(8,128)(2,1)}, u32[]{:S(2)}, u32[]{:S(2)}) collective-permute-start(bf16[512,512]{1,0:T(8,128)(2,1)S(1)} %get-tuple-element.47.refs_8_), channel_id=1, source_target_pairs={{0,64},{1,65},{2,66},{3,67},{4,68},{5,69},{6,70},{7,71},{8,72},{9,... | collective-permute-start | bytes 1572872 | tf_op jit(solution)/shard_map/ppermute | solution.py:37
  62.6 12.8 %collective-permute-start.16 = (bf16[512,512]{1,0:T(8,128)(2,1)S(1)}, bf16[512,512]{1,0:T(8,128)(2,1)}, u32[]{:S(2)}, u32[]{:S(2)}) collective-permute-start(bf16[512,512]{1,0:T(8,128)(2,1)S(1)} %get-tuple-element.47.refs_8_), channel_id=1, source_target_pairs={{0,96},{1,97},{2,98},{3,99},{4,100},{5,101},{6,102},{7,103},{8,104... | collective-permute-start | bytes 1572872 | tf_op jit(solution)/shard_map/ppermute | solution.py:37
  62.6 14.4 %collective-permute-start.15 = (bf16[512,512]{1,0:T(8,128)(2,1)S(1)}, bf16[512,512]{1,0:T(8,128)(2,1)S(1)}, u32[]{:S(2)}, u32[]{:S(2)}) collective-permute-start(bf16[512,512]{1,0:T(8,128)(2,1)S(1)} %collective-permute-done.11.refs_3_), channel_id=1, source_target_pairs={{0,4},{1,5},{2,6},{3,7},{4,0},{5,1},{6,2},{7,3},{8,12},{9,13},{10,... | collective-permute-start | bytes 1572872 | tf_op jit(solution)/shard_map/ppermute | solution.py:29
  63.4 14.6 %collective-permute-start.14 = (bf16[512,512]{1,0:T(8,128)(2,1)S(1)}, bf16[512,512]{1,0:T(8,128)(2,1)}, u32[]{:S(2)}, u32[]{:S(2)}) collective-permute-start(bf16[512,512]{1,0:T(8,128)(2,1)S(1)} %collective-permute-done.10.refs_2_), channel_id=1, source_target_pairs={{0,4},{1,5},{2,6},{3,7},{4,0},{5,1},{6,2},{7,3},{8,12},{9,13},{10,... | collective-permute-start | bytes 1572872 | tf_op jit(solution)/shard_map/ppermute | solution.py:29
  63.5 14.5 %collective-permute-start.13 = (bf16[512,512]{1,0:T(8,128)(2,1)S(1)}, bf16[512,512]{1,0:T(8,128)(2,1)}, u32[]{:S(2)}, u32[]{:S(2)}) collective-permute-start(bf16[512,512]{1,0:T(8,128)(2,1)S(1)} %collective-permute-done.9.refs_1_), channel_id=1, source_target_pairs={{0,4},{1,5},{2,6},{3,7},{4,0},{5,1},{6,2},{7,3},{8,12},{9,13},{10,... | collective-permute-start | bytes 1572872 | tf_op jit(solution)/shard_map/ppermute | solution.py:29
  66.8 11.2 %collective-permute-start.22 = (bf16[512,512]{1,0:T(8,128)(2,1)}, bf16[512,512]{1,0:T(8,128)(2,1)}, u32[]{:S(2)}, u32[]{:S(2)}) collective-permute-start(bf16[512,512]{1,0:T(8,128)(2,1)} %collective-permute-done.18.refs_11_), channel_id=1, source_target_pairs={{0,4},{1,5},{2,6},{3,7},{4,0},{5,1},{6,2},{7,3},{8,12},{9,13},{10,... | collective-permute-start | bytes 1572872 | tf_op jit(solution)/shard_map/ppermute | solution.py:29
  75.4 3.5 %collective-permute-start.21 = (bf16[512,512]{1,0:T(8,128)(2,1)}, bf16[512,512]{1,0:T(8,128)(2,1)}, u32[]{:S(2)}, u32[]{:S(2)}) collective-permute-start(bf16[512,512]{1,0:T(8,128)(2,1)} %collective-permute-done.17.refs_10_), channel_id=1, source_target_pairs={{0,4},{1,5},{2,6},{3,7},{4,0},{5,1},{6,2},{7,3},{8,12},{9,13},{10,... | collective-permute-start | bytes 1572872 | tf_op jit(solution)/shard_map/ppermute | solution.py:29
  77.9 2.3 %collective-permute-start.20 = (bf16[512,512]{1,0:T(8,128)(2,1)}, bf16[512,512]{1,0:T(8,128)(2,1)}, u32[]{:S(2)}, u32[]{:S(2)}) collective-permute-start(bf16[512,512]{1,0:T(8,128)(2,1)} %collective-permute-done.16.refs_9_), channel_id=1, source_target_pairs={{0,4},{1,5},{2,6},{3,7},{4,0},{5,1},{6,2},{7,3},{8,12},{9,13},{10,... | collective-permute-start | bytes 1572872 | tf_op jit(solution)/shard_map/ppermute | solution.py:29
  94.6 14.7 %collective-permute-start.25 = (bf16[256,512]{1,0:T(8,128)(2,1)S(1)}, bf16[256,512]{1,0:T(8,128)(2,1)S(1)}, u32[]{:S(2)}, u32[]{:S(2)}) collective-permute-start(bf16[256,512]{1,0:T(8,128)(2,1)S(1)} %get-tuple-element.48.refs_0_), channel_id=1, source_target_pairs={{0,1},{1,2},{2,3},{3,0},{4,5},{5,6},{6,7},{7,4},{8,9},{9,10},{10,1... | collective-permute-start | bytes 786440 | tf_op jit(solution)/shard_map/ppermute | solution.py:33
  94.7 15.5 %collective-permute-start.24 = (bf16[256,512]{1,0:T(8,128)(2,1)S(1)}, bf16[256,512]{1,0:T(8,128)(2,1)S(1)}, u32[]{:S(2)}, u32[]{:S(2)}) collective-permute-start(bf16[256,512]{1,0:T(8,128)(2,1)S(1)} %get-tuple-element.48.refs_0_), channel_id=1, source_target_pairs={{0,2},{1,3},{2,0},{3,1},{4,6},{5,7},{6,4},{7,5},{8,10},{9,11},{10,... | collective-permute-start | bytes 786440 | tf_op jit(solution)/shard_map/ppermute | solution.py:33
  96.3 14.0 %collective-permute-start.23 = (bf16[256,512]{1,0:T(8,128)(2,1)S(1)}, bf16[256,512]{1,0:T(8,128)(2,1)S(1)}, u32[]{:S(2)}, u32[]{:S(2)}) collective-permute-start(bf16[256,512]{1,0:T(8,128)(2,1)S(1)} %get-tuple-element.48.refs_0_), channel_id=1, source_target_pairs={{0,3},{1,0},{2,1},{3,2},{4,7},{5,4},{6,5},{7,6},{8,11},{9,8},{10,9... | collective-permute-start | bytes 786440 | tf_op jit(solution)/shard_map/ppermute | solution.py:33
  97.7 13.2 %collective-permute-start.26 = (bf16[256,512]{1,0:T(8,128)(2,1)S(1)}, bf16[256,512]{1,0:T(8,128)(2,1)S(1)}, u32[]{:S(2)}, u32[]{:S(2)}) collective-permute-start(bf16[256,512]{1,0:T(8,128)(2,1)S(1)} %get-tuple-element.48.refs_0_), channel_id=1, source_target_pairs={{0,4},{1,5},{2,6},{3,7},{4,0},{5,1},{6,2},{7,3},{8,12},{9,13},{10,... | collective-permute-start | bytes 786440 | tf_op jit(solution)/shard_map/ppermute | solution.py:29
  109.3 2.1 %collective-permute-start.29 = (bf16[256,512]{1,0:T(8,128)(2,1)S(1)}, bf16[256,512]{1,0:T(8,128)(2,1)S(1)}, u32[]{:S(2)}, u32[]{:S(2)}) collective-permute-start(bf16[256,512]{1,0:T(8,128)(2,1)S(1)} %collective-permute-done.25.refs_3_), channel_id=1, source_target_pairs={{0,4},{1,5},{2,6},{3,7},{4,0},{5,1},{6,2},{7,3},{8,12},{9,13},{10,... | collective-permute-start | bytes 786440 | tf_op jit(solution)/shard_map/ppermute | solution.py:29
  110.3 1.9 collective-permute-start.27
  117.4 7.5 %collective-permute-start.34 = (bf16[128,512]{1,0:T(8,128)(2,1)S(1)}, bf16[128,512]{1,0:T(8,128)(2,1)S(1)}, u32[]{:S(2)}, u32[]{:S(2)}) collective-permute-start(bf16[128,512]{1,0:T(8,128)(2,1)S(1)} %get-tuple-element.53), channel_id=1, source_target_pairs={{0,64},{1,65},{2,66},{3,67},{4,68},{5,69},{6,70},{7,71},{8,72},{9,... | collective-permute-start | bytes 393224 | tf_op jit(solution)/shard_map/ppermute | solution.py:37
  117.6 9.9 %collective-permute-start.31 = (bf16[128,512]{1,0:T(8,128)(2,1)S(1)}, bf16[128,512]{1,0:T(8,128)(2,1)S(1)}, u32[]{:S(2)}, u32[]{:S(2)}) collective-permute-start(bf16[128,512]{1,0:T(8,128)(2,1)S(1)} %get-tuple-element.53), channel_id=1, source_target_pairs={{0,32},{1,33},{2,34},{3,35},{4,36},{5,37},{6,38},{7,39},{8,40},{9,... | collective-permute-start | bytes 393224 | tf_op jit(solution)/shard_map/ppermute | solution.py:37
  119.2 8.3 %collective-permute-start.30 = (bf16[128,512]{1,0:T(8,128)(2,1)S(1)}, bf16[128,512]{1,0:T(8,128)(2,1)S(1)}, u32[]{:S(2)}, u32[]{:S(2)}) collective-permute-start(bf16[128,512]{1,0:T(8,128)(2,1)S(1)} %get-tuple-element.53), channel_id=1, source_target_pairs={{0,96},{1,97},{2,98},{3,99},{4,100},{5,101},{6,102},{7,103},{8,104... | collective-permute-start | bytes 393224 | tf_op jit(solution)/shard_map/ppermute | solution.py:37
  120.3 7.5 %collective-permute-start.35 = (bf16[128,512]{1,0:T(8,128)(2,1)S(1)}, bf16[128,512]{1,0:T(8,128)(2,1)S(1)}, u32[]{:S(2)}, u32[]{:S(2)}) collective-permute-start(bf16[128,512]{1,0:T(8,128)(2,1)S(1)} %get-tuple-element.57), channel_id=1, source_target_pairs={{0,16},{1,17},{2,18},{3,19},{4,20},{5,21},{6,22},{7,23},{8,24},{9,... | collective-permute-start | bytes 393224 | tf_op jit(solution)/shard_map/ppermute | solution.py:41
  124.8 6.2 %collective-permute-start.33 = (bf16[128,512]{1,0:T(8,128)(2,1)S(1)}, bf16[128,512]{1,0:T(8,128)(2,1)S(1)}, u32[]{:S(2)}, u32[]{:S(2)}) collective-permute-start(bf16[128,512]{1,0:T(8,128)(2,1)S(1)} %get-tuple-element.57), channel_id=1, source_target_pairs={{0,8},{1,9},{2,10},{3,11},{4,12},{5,13},{6,14},{7,15},{8,16},{9,17... | collective-permute-start | bytes 393224 | tf_op jit(solution)/shard_map/ppermute | solution.py:41
  124.8 6.2 %collective-permute-start.32 = (bf16[128,512]{1,0:T(8,128)(2,1)S(1)}, bf16[128,512]{1,0:T(8,128)(2,1)S(1)}, u32[]{:S(2)}, u32[]{:S(2)}) collective-permute-start(bf16[128,512]{1,0:T(8,128)(2,1)S(1)} %get-tuple-element.57), channel_id=1, source_target_pairs={{0,24},{1,25},{2,26},{3,27},{4,28},{5,29},{6,30},{7,31},{8,0},{9,1... | collective-permute-start | bytes 393224 | tf_op jit(solution)/shard_map/ppermute | solution.py:41
  131.2 14.3 %collective-permute-start.38 = (bf16[512,512]{1,0:T(8,128)(2,1)S(1)}, bf16[512,512]{1,0:T(8,128)(2,1)S(1)}, u32[]{:S(2)}, u32[]{:S(2)}) collective-permute-start(bf16[512,512]{1,0:T(8,128)(2,1)S(1)} %pad_maximum_fusion.2.refs_0_.refs_9_), channel_id=1, source_target_pairs={{0,8},{1,9},{2,10},{3,11},{4,12},{5,13},{6,14},{7,15},{8,16},{9,17... | collective-permute-start | bytes 1572872 | tf_op jit(solution)/shard_map/ppermute | solution.py:41
  132.1 22.4 %collective-permute-start.37 = (bf16[512,512]{1,0:T(8,128)(2,1)S(1)}, bf16[512,512]{1,0:T(8,128)(2,1)S(1)}, u32[]{:S(2)}, u32[]{:S(2)}) collective-permute-start(bf16[512,512]{1,0:T(8,128)(2,1)S(1)} %pad_maximum_fusion.2.refs_0_.refs_9_), channel_id=1, source_target_pairs={{0,16},{1,17},{2,18},{3,19},{4,20},{5,21},{6,22},{7,23},{8,24},{9,... | collective-permute-start | bytes 1572872 | tf_op jit(solution)/shard_map/ppermute | solution.py:41
  133.9 23.2 %collective-permute-start.36 = (bf16[512,512]{1,0:T(8,128)(2,1)S(1)}, bf16[512,512]{1,0:T(8,128)(2,1)S(1)}, u32[]{:S(2)}, u32[]{:S(2)}) collective-permute-start(bf16[512,512]{1,0:T(8,128)(2,1)S(1)} %pad_maximum_fusion.2.refs_0_.refs_9_), channel_id=1, source_target_pairs={{0,24},{1,25},{2,26},{3,27},{4,28},{5,29},{6,30},{7,31},{8,0},{9,1... | collective-permute-start | bytes 1572872 | tf_op jit(solution)/shard_map/ppermute | solution.py:41
  134.7 22.4 %collective-permute-start.41 = (bf16[512,512]{1,0:T(8,128)(2,1)S(1)}, bf16[512,512]{1,0:T(8,128)(2,1)S(1)}, u32[]{:S(2)}, u32[]{:S(2)}) collective-permute-start(bf16[512,512]{1,0:T(8,128)(2,1)S(1)} %pad_maximum_fusion.3.refs_4_.refs_13_), channel_id=1, source_target_pairs={{0,32},{1,33},{2,34},{3,35},{4,36},{5,37},{6,38},{7,39},{8,40},{9,... | collective-permute-start | bytes 1572872 | tf_op jit(solution)/shard_map/ppermute | solution.py:37
  134.7 22.4 %collective-permute-start.40 = (bf16[512,512]{1,0:T(8,128)(2,1)S(1)}, bf16[512,512]{1,0:T(8,128)(2,1)S(1)}, u32[]{:S(2)}, u32[]{:S(2)}) collective-permute-start(bf16[512,512]{1,0:T(8,128)(2,1)S(1)} %pad_maximum_fusion.3.refs_4_.refs_13_), channel_id=1, source_target_pairs={{0,64},{1,65},{2,66},{3,67},{4,68},{5,69},{6,70},{7,71},{8,72},{9,... | collective-permute-start | bytes 1572872 | tf_op jit(solution)/shard_map/ppermute | solution.py:37
  145.5 13.3 %collective-permute-start.39 = (bf16[512,512]{1,0:T(8,128)(2,1)S(1)}, bf16[512,512]{1,0:T(8,128)(2,1)S(1)}, u32[]{:S(2)}, u32[]{:S(2)}) collective-permute-start(bf16[512,512]{1,0:T(8,128)(2,1)S(1)} %pad_maximum_fusion.3.refs_4_.refs_13_), channel_id=1, source_target_pairs={{0,96},{1,97},{2,98},{3,99},{4,100},{5,101},{6,102},{7,103},{8,104... | collective-permute-start | bytes 1572872 | tf_op jit(solution)/shard_map/ppermute | solution.py:37
  171.5 7.6 %collective-permute-start.44 = (bf16[256,512]{1,0:T(8,128)(2,1)S(1)}, bf16[256,512]{1,0:T(8,128)(2,1)S(1)}, u32[]{:S(2)}, u32[]{:S(2)}) collective-permute-start(bf16[256,512]{1,0:T(8,128)(2,1)S(1)} %get-tuple-element.63.refs_0_), channel_id=1, source_target_pairs={{0,1},{1,2},{2,3},{3,0},{4,5},{5,6},{6,7},{7,4},{8,9},{9,10},{10,1... | collective-permute-start | bytes 786440 | tf_op jit(solution)/shard_map/ppermute | solution.py:33
  171.6 13.8 %collective-permute-start.43 = (bf16[256,512]{1,0:T(8,128)(2,1)S(1)}, bf16[256,512]{1,0:T(8,128)(2,1)S(1)}, u32[]{:S(2)}, u32[]{:S(2)}) collective-permute-start(bf16[256,512]{1,0:T(8,128)(2,1)S(1)} %get-tuple-element.63.refs_0_), channel_id=1, source_target_pairs={{0,2},{1,3},{2,0},{3,1},{4,6},{5,7},{6,4},{7,5},{8,10},{9,11},{10,... | collective-permute-start | bytes 786440 | tf_op jit(solution)/shard_map/ppermute | solution.py:33
  175.3 12.9 %collective-permute-start.42 = (bf16[256,512]{1,0:T(8,128)(2,1)S(1)}, bf16[256,512]{1,0:T(8,128)(2,1)S(1)}, u32[]{:S(2)}, u32[]{:S(2)}) collective-permute-start(bf16[256,512]{1,0:T(8,128)(2,1)S(1)} %get-tuple-element.63.refs_0_), channel_id=1, source_target_pairs={{0,3},{1,0},{2,1},{3,2},{4,7},{5,4},{6,5},{7,6},{8,11},{9,8},{10,9... | collective-permute-start | bytes 786440 | tf_op jit(solution)/shard_map/ppermute | solution.py:33
  175.3 12.9 %collective-permute-start.45 = (bf16[256,512]{1,0:T(8,128)(2,1)S(1)}, bf16[256,512]{1,0:T(8,128)(2,1)S(1)}, u32[]{:S(2)}, u32[]{:S(2)}) collective-permute-start(bf16[256,512]{1,0:T(8,128)(2,1)S(1)} %get-tuple-element.63.refs_0_), channel_id=1, source_target_pairs={{0,4},{1,5},{2,6},{3,7},{4,0},{5,1},{6,2},{7,3},{8,12},{9,13},{10,... | collective-permute-start | bytes 786440 | tf_op jit(solution)/shard_map/ppermute | solution.py:29
  179.1 9.1 %collective-permute-start.48 = (bf16[256,512]{1,0:T(8,128)(2,1)S(1)}, bf16[256,512]{1,0:T(8,128)(2,1)S(1)}, u32[]{:S(2)}, u32[]{:S(2)}) collective-permute-start(bf16[256,512]{1,0:T(8,128)(2,1)S(1)} %collective-permute-done.44.refs_3_), channel_id=1, source_target_pairs={{0,4},{1,5},{2,6},{3,7},{4,0},{5,1},{6,2},{7,3},{8,12},{9,13},{10,... | collective-permute-start | bytes 786440 | tf_op jit(solution)/shard_map/ppermute | solution.py:29
  185.4 4.0 %collective-permute-start.47 = (bf16[256,512]{1,0:T(8,128)(2,1)S(1)}, bf16[256,512]{1,0:T(8,128)(2,1)S(1)}, u32[]{:S(2)}, u32[]{:S(2)}) collective-permute-start(bf16[256,512]{1,0:T(8,128)(2,1)S(1)} %collective-permute-done.43.refs_2_), channel_id=1, source_target_pairs={{0,4},{1,5},{2,6},{3,7},{4,0},{5,1},{6,2},{7,3},{8,12},{9,13},{10,... | collective-permute-start | bytes 786440 | tf_op jit(solution)/shard_map/ppermute | solution.py:29
  (15 other events, 111.6 us)
Sparse Core Ops, SparseCore 0:
  116.5 26.6 all-gather.1

commit v3 on v2

v3 whole, which is shorter than its diff:
```python
import jax
import jax.numpy as jnp
from jax import lax
from jax.experimental import pallas as pl
from jax.experimental.pallas import tpu as pltpu
from jax.sharding import PartitionSpec as P

B = 128
N = 4096
K = 1024
ROWS = 256
COLS = 512
AXES = ("row", "col")
MIB = 1024 * 1024


def device(x, y, core, z):
    return (((x % 4) * 4 + y % 4) * 2 + core) * 4 + z % 4


def pairs(target):
    return [
        (device(x, y, core, z), device(*target(x, y, core, z)))
        for x in range(4) for y in range(4) for core in range(2) for z in range(4)
    ]


def other_core(a):
    return lax.ppermute(a, AXES, pairs(lambda x, y, core, z: (x, y, 1 - core, z)))


def from_z(a, d):
    return lax.ppermute(a, AXES, pairs(lambda x, y, core, z: (x, y, core, z - d)))


def from_first(a, d):
    return lax.ppermute(a, AXES, pairs(
        lambda x, y, core, z: (x - d, y, core, z) if core == 0 else (x, y - d, core, z)))


def from_second(a, d):
    return lax.ppermute(a, AXES, pairs(
        lambda x, y, core, z: (x, y - d, core, z) if core == 0 else (x - d, y, core, z)))


def by_offset(own, one, three, two):
    return [own, one, two, three]


def gather_z(a):
    return by_offset(a, *[from_z(a, d) for d in (1, 3, 2)])


def gather_plane(a):
    one, three, two, far = from_first(a, 1), from_first(a, 3), from_first(a, 2), from_second(a, 2)
    a, one, three, two, far = lax.optimization_barrier((a, one, three, two, far))
    line = jnp.concatenate(by_offset(a, one, three, two), axis=0)
    far_line = jnp.concatenate(by_offset(far, *[from_first(far, d) for d in (1, 3, 2)]), axis=0)
    return by_offset(line, from_second(line, 1), from_second(line, 3), far_line)


def place(x, y, kind, first, second):
    px = jnp.where(kind == 0, x + first, x + second) & 3
    py = jnp.where(kind == 0, y + second, y + first) & 3
    return px, py


def dot_t(a, b):
    return lax.dot_general(a, b, (((1,), (1,)), ((), ())), preferred_element_type=jnp.float32)


def dot(a, b):
    return jnp.dot(a, b, preferred_element_type=jnp.float32)


def first_square(where, keep_d, keep_s, *refs):
    parts, (panel, square, low), (rows, row, sems) = (refs[0:4], refs[4:8]), refs[8:11], refs[11:]
    x, y, core, z = where[0], where[1], where[2], where[3]
    row_block, col_block = (x * 4 + y) * 2, z * 8 + core * 4
    kinds = (core, 1 - core)

    def fetch(source, block, target):
        return pltpu.make_async_copy(
            source.at[pl.ds(pl.multiple_of(block * B, B), B)],
            rows.at[pl.ds(pl.multiple_of(target * B, B), B)], sems.at[target])

    for t in range(4):
        dx, dy = (z - x) & 3, (core * 2 + (t >> 1) - y) & 3
        first, second = (dx, dy) if t & 1 == 0 else (dy, dx)
        for c in range(2):
            for j in range(4):
                @pl.when((core == c) & (second == j))
                def _():
                    fetch(parts[(t & 1) ^ c][j], first, t).start()
    for own in range(2):
        fetch(parts[own][0], 0, 4 + kinds[own]).start()
    for t in range(6):
        fetch(parts[0][0], 0, t).wait()

    for own in range(2):
        for j in range(4):
            value = dot_t(parts[own][j][...], rows[...])
            for i in range(4):
                px, py = place(x, y, kinds[own], i, j)
                block = px * 8 + py * 2 + kinds[own]
                at = pl.multiple_of(block * B, B)
                for t in range(4):
                    keep = keep_d[0, block, col_block + t].astype(jnp.float32)
                    piece = value[i * B:(i + 1) * B, t * B:(t + 1) * B] * keep
                    panel[pl.ds(at, B), t * B:(t + 1) * B] = piece.astype(jnp.bfloat16)
                for t in range(2):
                    keep = keep_d[0, row_block + t, block].astype(jnp.float32)
                    piece = value[i * B:(i + 1) * B, COLS + t * B:COLS + (t + 1) * B] * keep
                    row[t * B:(t + 1) * B, pl.ds(at, B)] = piece.astype(jnp.bfloat16).T

    finish_square(dot(row[...], panel[...]), keep_s, 0, row_block, col_block, square, low)


def finish_square(value, keep_s, step, row_block, col_block, square, low):
    for t in range(2):
        for u in range(4):
            keep = keep_s[step, row_block + t, col_block + u].astype(jnp.float32)
            piece = value[t * B:(t + 1) * B, u * B:(u + 1) * B] * keep
            square[t * B:(t + 1) * B, u * B:(u + 1) * B] = piece
            low[t * B:(t + 1) * B, u * B:(u + 1) * B] = piece.astype(jnp.bfloat16)


def row_times_panel(own, other, core, z, panel):
    total = None
    for d in range(4):
        for ref, half in ((own[d], core), (other[d], 1 - core)):
            at = pl.multiple_of((((z + d) & 3) * 2 + half) * COLS, COLS)
            term = dot(ref[...], panel[pl.ds(at, COLS), :])
            total = term if total is None else total + term
    return total


def first_density(where, keep_d, *refs):
    own, other, (square, panel), (out,) = refs[:4], refs[4:8], refs[8:10], refs[10:]
    x, y, core, z = where[0], where[1], where[2], where[3]
    cube = row_times_panel(own, other, core, z, panel)
    value = 3.0 * square[...] - 2.0 * cube
    for t in range(2):
        for u in range(4):
            keep = keep_d[1, (x * 4 + y) * 2 + t, z * 8 + core * 4 + u].astype(jnp.float32)
            piece = value[t * B:(t + 1) * B, u * B:(u + 1) * B] * keep
            out[t * B:(t + 1) * B, u * B:(u + 1) * B] = piece.astype(jnp.bfloat16)


def load_panel(parts, panel, sems, x, y, core):
    copies = []
    for second, part in enumerate(parts):
        for first in range(4):
            px, py = place(x, y, core, first, second)
            at = pl.multiple_of((px * 4 + py) * ROWS, ROWS)
            copies.append(pltpu.make_async_copy(
                part.at[pl.ds(first * ROWS, ROWS)], panel.at[pl.ds(at, ROWS)], sems.at[second * 4 + first]))
    for copy in copies:
        copy.start()
    for copy in copies:
        copy.wait()


def second_square(where, keep_s, line, *refs):
    parts, (square, low), (panel, sems) = refs[:4], refs[4:6], refs[6:]
    x, y, core, z = where[0], where[1], where[2], where[3]
    load_panel(parts, panel, sems, x, y, core)
    value = None
    for q in range(8):
        term = dot(line[q * ROWS:(q + 1) * ROWS, :], panel[q * COLS:(q + 1) * COLS, :])
        value = term if value is None else value + term
    finish_square(value, keep_s, 1, (x * 4 + y) * 2, z * 8 + core * 4, square, low)


def second_density(where, *refs):
    own, other, (square,), parts, (stay, leave), (panel, sems) = (
        refs[:4], refs[4:8], refs[8:9], refs[9:13], refs[13:15], refs[15:])
    x, y, core, z = where[0], where[1], where[2], where[3]
    load_panel(parts, panel, sems, x, y, core)
    value = 3.0 * square[...] - 2.0 * row_times_panel(own, other, core, z, panel)
    first = core == 0
    stay[...] = jnp.where(first, value[:B], value[B:])
    leave[...] = jnp.where(first, value[B:], value[:B])


SMEM = pl.BlockSpec(memory_space=pltpu.SMEM)
VMEM = pl.BlockSpec(memory_space=pltpu.VMEM)
ANY = pl.BlockSpec(memory_space=pl.ANY)


def call(kernel, ins, outs, scratch, flops, moved, limit):
    return pl.pallas_call(
        kernel,
        in_specs=ins,
        out_specs=[VMEM] * len(outs),
        out_shape=outs,
        scratch_shapes=scratch,
        cost_estimate=pl.CostEstimate(flops=flops, bytes_accessed=moved, transcendentals=0),
        compiler_params=pltpu.CompilerParams(vmem_limit_bytes=limit * MIB),
    )


def body(coeffs, coef_pattern, keep_density, keep_square):
    r, z = lax.axis_index("row"), lax.axis_index("col")
    x, y, core = r // 8, (r // 2) % 4, r % 2
    where = jnp.stack([x, y, core, z]).astype(jnp.int32)
    low_block = jax.ShapeDtypeStruct((ROWS, COLS), jnp.bfloat16)
    full_block = jax.ShapeDtypeStruct((ROWS, COLS), jnp.float32)
    panel_scratch = [pltpu.VMEM((N, COLS), jnp.bfloat16), pltpu.SemaphoreType.DMA((16,))]

    wide = jnp.concatenate(gather_z(coeffs), axis=1)
    pattern = lax.dynamic_slice(coef_pattern, (r, 0), (1, 8)).reshape(4, 2)
    pattern = jnp.concatenate([pattern, pattern], axis=0)
    pattern = lax.dynamic_slice(pattern, (z, 0), (4, 2)).reshape(1, 8)
    wide = wide * jnp.repeat(pattern, B, 1).astype(jnp.bfloat16)
    parts = gather_plane(wide)
    others = [other_core(part) for part in parts]
    panel, square, low = call(
        first_square, [SMEM] * 3 + [VMEM] * 8,
        [jax.ShapeDtypeStruct((N, COLS), jnp.bfloat16), full_block, low_block],
        [
            pltpu.VMEM((COLS + ROWS, K), jnp.bfloat16),
            pltpu.VMEM((ROWS, N), jnp.bfloat16),
            pltpu.SemaphoreType.DMA((6,)),
        ],
        2 * N * K * (COLS + ROWS) + 2 * ROWS * N * COLS, 13 * MIB, 16,
    )(where, keep_density, keep_square, *parts, *others)

    own = gather_z(low)
    other = [other_core(part) for part in own]
    (current,) = call(
        first_density, [SMEM] * 2 + [VMEM] * 10, [low_block], [], 2 * ROWS * N * COLS, 7 * MIB, 8,
    )(where, keep_density, *own, *other, square, panel)

    line = lax.all_gather(current, AXES, axis=0, tiled=True, axis_index_groups=[
        [device(x, y, core, z) for z in range(4) for core in range(2)] for x in range(4) for y in range(4)])
    parts = gather_plane(current)
    square, low = call(
        second_square, [SMEM] * 2 + [VMEM] + [ANY] * 4, [full_block, low_block],
        panel_scratch, 2 * ROWS * N * COLS, 7 * MIB, 12,
    )(where, keep_square, line, *parts)

    own = gather_z(low)
    other = [other_core(part) for part in own]
    half = jax.ShapeDtypeStruct((B, COLS), jnp.float32)
    stay, leave = call(
        second_density, [SMEM] + [VMEM] * 9 + [ANY] * 4, [half, half],
        panel_scratch, 2 * ROWS * N * COLS, 8 * MIB, 12,
    )(where, *own, *other, square, *parts)
    come = other_core(leave)
    first = core == 0
    return jnp.concatenate([jnp.where(first, stay, come), jnp.where(first, come, stay)], axis=1)


def solution(mesh):
    placed = (P("row", "col"), P(), P(), P())
    return jax.shard_map(
        body, mesh=mesh, in_specs=placed, out_specs=P("row", "col"), check_vma=False
    )
```

time: 211 us -> 164 us (0.78)
  starting transfers between devices: 70.3 us -> 53 us
  Pallas kernels: 35.7 us -> 20.6 us
  waiting for transfers between devices: 78.7 us -> 69.3 us
  local copies, waits for them, and re-layouts: 8.7 us -> 5.68 us
    ppermute x24 -> x18, waiting for transfers between devices: 58.9 us -> 42.2 us  [the longest x12 33 us: from_first(): lax.ppermute(a, AXES, pairs(lambda x, y, core, z: (x - d, y, core, z) if...]
    pallas_call x3, Pallas kernels: 31.5 us -> 17.5 us  [the longest x1 11.6 us: body(): call(first_square, [SMEM] * 3 + [VMEM] * 8, [jax.ShapeDtypeStruct((N, COL...]
    ppermute x24 -> x18, starting transfers between devices: 32 us -> 22.6 us  [the longest x12 12.4 us: from_first(): lax.ppermute(a, AXES, pairs(lambda x, y, core, z: (x - d, y, core, z) if...]
    ppermute x17 -> x13, starting transfers between devices: 25.7 us -> 18.5 us  [other_core(): lax.ppermute(a, AXES, pairs(lambda x, y, core, z: (x, y, 1 - core, z)))]
    ppermute x9, waiting for transfers between devices: 13.4 us -> 19.1 us  [from_z(): lax.ppermute(a, AXES, pairs(lambda x, y, core, z: (x, y, core, z - d)))]
    ppermute x17 -> x13, waiting for transfers between devices: 6.35 us -> 7.93 us  [other_core(): lax.ppermute(a, AXES, pairs(lambda x, y, core, z: (x, y, 1 - core, z)))]
  transfers between devices with their start and end apart: 51 -> 41, of which waited for: 21 -> 27; matrix products, arithmetic and copies ran while one was open for 1% -> 1% of each run, Pallas kernels for 0% -> 0%
where the time goes in v3:
time: 164 us
  waiting for transfers between devices  69.3 us (42%)
  starting transfers between devices  53 us (32%)
  Pallas kernels  20.6 us (13%)
  between operations  13.6 us (8%)
  local copies, waits for them, and re-layouts  5.68 us (3%)
  other arithmetic  1.99 us (1%)
    ppermute x12, waiting for transfers between devices, from_first(): lax.ppermute(a, AXES, pairs(lambda x, y, core, z: (x - d, y, core, z) if...  33 us
    ppermute x9, waiting for transfers between devices, from_z(): lax.ppermute(a, AXES, pairs(lambda x, y, core, z: (x, y, core, z - d)))  19.1 us
    ppermute x13, starting transfers between devices, other_core(): lax.ppermute(a, AXES, pairs(lambda x, y, core, z: (x, y, 1 - core, z)))  18.5 us
    ppermute x12, starting transfers between devices, from_first(): lax.ppermute(a, AXES, pairs(lambda x, y, core, z: (x - d, y, core, z) if...  12.4 us
    ppermute x9, starting transfers between devices, from_z(): lax.ppermute(a, AXES, pairs(lambda x, y, core, z: (x, y, core, z - d)))  12 us
    pallas_call x1, Pallas kernels, body(): call(first_square, [SMEM] * 3 + [VMEM] * 8, [jax.ShapeDtypeStruct((N, COL...  11.6 us
    ppermute x6, starting transfers between devices, from_second(): lax.ppermute(a, AXES, pairs(lambda x, y, core, z: (x, y - d, core, z) if...  10.2 us
    ppermute x6, waiting for transfers between devices, from_second(): lax.ppermute(a, AXES, pairs(lambda x, y, core, z: (x, y - d, core, z) if...  9.2 us
  transfers between devices with their start and end apart: 41, of which 27 were waited for; matrix products, arithmetic and copies ran while one was open for 1% of the time, Pallas kernels for 0%

profile of v3, /device:TPU:1, one launch (start us, length us, event | category | flops | bytes accessed | tf_op | source)
XLA Modules:
  0.0 164.1 jit_solution(4299626439720395568)
XLA Ops:
  6.5 4.5 %collective-permute-start.1 = (bf16[128,256]{1,0:T(8,128)(2,1)}, bf16[128,256]{1,0:T(8,128)(2,1)S(1)}, u32[]{:S(2)}, u32[]{:S(2)}) collective-permute-start(bf16[128,256]{1,0:T(8,128)(2,1)} %param.4), channel_id=1, source_target_pairs={{0,2},{1,3},{2,0},{3,1},{4,6},{5,7},{6,4},{7,5},{8,10},{9,11},{10,... | collective-permute-start | bytes 196616 | tf_op jit(solution)/shard_map/ppermute | solution.py:33
  11.5 1.0 collective-permute-start.2
  13.3 1.4 collective-permute-done
  14.8 1.3 collective-permute-done.2
  16.9 2.8 %collective-permute-start.6 = (bf16[128,1024]{1,0:T(8,128)(2,1)S(1)}, bf16[128,1024]{1,0:T(8,128)(2,1)S(1)}, u32[]{:S(2)}, u32[]{:S(2)}) collective-permute-start(bf16[128,1024]{1,0:T(8,128)(2,1)S(1)} %maximum_multiply_fusion), channel_id=1, source_target_pairs={{0,16},{1,17},{2,18},{3,19},{4,68},{5,69},{6,70},{7,71},{8,24},{9,... | collective-permute-start | bytes 786440 | tf_op jit(solution)/shard_map/ppermute | solution.py:42
  19.7 2.9 %collective-permute-start.5 = (bf16[128,1024]{1,0:T(8,128)(2,1)S(1)}, bf16[128,1024]{1,0:T(8,128)(2,1)S(1)}, u32[]{:S(2)}, u32[]{:S(2)}) collective-permute-start(bf16[128,1024]{1,0:T(8,128)(2,1)S(1)} %maximum_multiply_fusion), channel_id=1, source_target_pairs={{0,64},{1,65},{2,66},{3,67},{4,20},{5,21},{6,22},{7,23},{8,72},{9,... | collective-permute-start | bytes 786440 | tf_op jit(solution)/shard_map/ppermute | solution.py:37
  23.1 2.3 %collective-permute-start.3 = (bf16[128,1024]{1,0:T(8,128)(2,1)S(1)}, bf16[128,1024]{1,0:T(8,128)(2,1)S(1)}, u32[]{:S(2)}, u32[]{:S(2)}) collective-permute-start(bf16[128,1024]{1,0:T(8,128)(2,1)S(1)} %maximum_multiply_fusion), channel_id=1, source_target_pairs={{0,96},{1,97},{2,98},{3,99},{4,28},{5,29},{6,30},{7,31},{8,104},{9... | collective-permute-start | bytes 786440 | tf_op jit(solution)/shard_map/ppermute | solution.py:37
  25.3 4.2 %collective-permute-done.5 = bf16[128,1024]{1,0:T(8,128)(2,1)S(1)} collective-permute-done((bf16[128,1024]{1,0:T(8,128)(2,1)S(1)}, bf16[128,1024]{1,0:T(8,128)(2,1)S(1)}, u32[]{:S(2)}, u32[]{:S(2)}) %collective-permute-start.5) | collective-permute-done | bytes 262176 | tf_op jit(solution)/shard_map/ppermute | solution.py:37
  29.5 2.9 %collective-permute-done.4 = bf16[128,1024]{1,0:T(8,128)(2,1)S(1)} collective-permute-done((bf16[128,1024]{1,0:T(8,128)(2,1)S(1)}, bf16[128,1024]{1,0:T(8,128)(2,1)S(1)}, u32[]{:S(2)}, u32[]{:S(2)}) %collective-permute-start.4) | collective-permute-done | bytes 262176 | tf_op jit(solution)/shard_map/ppermute | solution.py:37
  33.3 2.4 %collective-permute-start.7 = (bf16[512,1024]{1,0:T(8,128)(2,1)S(1)}, bf16[512,1024]{1,0:T(8,128)(2,1)}, u32[]{:S(2)}, u32[]{:S(2)}) collective-permute-start(bf16[512,1024]{1,0:T(8,128)(2,1)S(1)} %constant_dynamic-update-slice_fusion.refs_0_), channel_id=1, source_target_pairs={{0,24},{1,25},{2,26},{3,27},{4,100},{5,101},{6,102},{7,103},{8,0},... | collective-permute-start | bytes 3145736 | tf_op jit(solution)/shard_map/ppermute | solution.py:42
  35.6 2.1 %collective-permute-start.8 = (bf16[128,1024]{1,0:T(8,128)(2,1)S(1)}, bf16[128,1024]{1,0:T(8,128)(2,1)S(1)}, u32[]{:S(2)}, u32[]{:S(2)}) collective-permute-start(bf16[128,1024]{1,0:T(8,128)(2,1)S(1)} %collective-permute-done.6), channel_id=1, source_target_pairs={{0,96},{1,97},{2,98},{3,99},{4,28},{5,29},{6,30},{7,31},{8,104},{9... | collective-permute-start | bytes 786440 | tf_op jit(solution)/shard_map/ppermute | solution.py:37
  38.3 5.8 %collective-permute-done.8 = bf16[128,1024]{1,0:T(8,128)(2,1)S(1)} collective-permute-done((bf16[128,1024]{1,0:T(8,128)(2,1)S(1)}, bf16[128,1024]{1,0:T(8,128)(2,1)S(1)}, u32[]{:S(2)}, u32[]{:S(2)}) %collective-permute-start.8) | collective-permute-done | bytes 262176 | tf_op jit(solution)/shard_map/ppermute | solution.py:37
  44.1 3.6 %collective-permute-start.12 = (bf16[512,1024]{1,0:T(8,128)(2,1)S(1)}, bf16[512,1024]{1,0:T(8,128)(2,1)}, u32[]{:S(2)}, u32[]{:S(2)}) collective-permute-start(bf16[512,1024]{1,0:T(8,128)(2,1)S(1)} %constant_dynamic-update-slice_fusion.refs_0_), channel_id=1, source_target_pairs={{0,4},{1,5},{2,6},{3,7},{4,0},{5,1},{6,2},{7,3},{8,12},{9,13},{10,... | collective-permute-start | bytes 3145736 | tf_op jit(solution)/shard_map/ppermute | solution.py:29
  47.8 2.9 %collective-permute-done.10 = bf16[128,1024]{1,0:T(8,128)(2,1)S(1)} collective-permute-done((bf16[128,1024]{1,0:T(8,128)(2,1)S(1)}, bf16[128,1024]{1,0:T(8,128)(2,1)S(1)}, u32[]{:S(2)}, u32[]{:S(2)}) %collective-permute-start.10) | collective-permute-done | bytes 262176 | tf_op jit(solution)/shard_map/ppermute | solution.py:37
  50.6 3.0 %collective-permute-start.14 = (bf16[512,1024]{1,0:T(8,128)(2,1)S(1)}, bf16[512,1024]{1,0:T(8,128)(2,1)}, u32[]{:S(2)}, u32[]{:S(2)}) collective-permute-start(bf16[512,1024]{1,0:T(8,128)(2,1)S(1)} %constant_dynamic-update-slice_fusion.4.refs_2_), channel_id=1, source_target_pairs={{0,4},{1,5},{2,6},{3,7},{4,0},{5,1},{6,2},{7,3},{8,12},{9,13},{10,... | collective-permute-start | bytes 3145736 | tf_op jit(solution)/shard_map/ppermute | solution.py:29
  53.8 1.4 collective-permute-start.15
  56.0 1.8 %collective-permute-done.15.refs_7_ = bf16[512,1024]{1,0:T(8,128)(2,1)} collective-permute-done((bf16[512,1024]{1,0:T(8,128)(2,1)}, bf16[512,1024]{1,0:T(8,128)(2,1)}, u32[]{:S(2)}, u32[]{:S(2)}) %collective-permute-start.15) | collective-permute-done | bytes 1048608 | tf_op jit(solution)/shard_map/ppermute | solution.py:29
  57.9 1.5 collective-permute-done.13.refs_5_
  59.4 11.6 %shard_map.46 = (bf16[4096,512]{1,0:T(8,128)(2,1)S(1)}, f32[256,512]{1,0:T(8,128)S(1)}, bf16[256,512]{1,0:T(8,128)(2,1)S(1)}) custom-call(s32[4]{0:T(128)S(1)} %pad_add_fusion.1.where, s32[2,32,32]{2,1,0:T(8,128)S(1)} %copy-done.4, s32[2,32,32]{2,1,0:T(8,128)S(1)} %copy-done.5, bf16[512,1024]{1,0:T(8,128)(2,1)S(1)} %constant_dynamic-update-slice_fusion.refs_0_, ...), custom_call_target="tpu_custom_call" | custom-call | flops 7516192768 | bytes 13631488 | tf_op jit(solution)/shard_map/pallas_call | solution.py:218
  71.1 1.6 collective-permute-start.17
  72.7 1.4 collective-permute-start.16
  74.0 1.2 collective-permute-start.19
  75.2 10.2 %collective-permute-done.18.refs_3_ = bf16[256,512]{1,0:T(8,128)(2,1)S(1)} collective-permute-done((bf16[256,512]{1,0:T(8,128)(2,1)S(1)}, bf16[256,512]{1,0:T(8,128)(2,1)S(1)}, u32[]{:S(2)}, u32[]{:S(2)}) %collective-permute-start.18) | collective-permute-done | bytes 262176 | tf_op jit(solution)/shard_map/ppermute | solution.py:33
  85.4 1.2 collective-permute-start.22
  88.5 3.1 %shard_map.47 = bf16[256,512]{1,0:T(8,128)(2,1)} custom-call(s32[4]{0:T(128)S(1)} %pad_add_fusion.1.where, s32[2,32,32]{2,1,0:T(8,128)S(1)} %copy-done.4, bf16[256,512]{1,0:T(8,128)(2,1)S(1)} %get-tuple-element.27.refs_0_, bf16[256,512]{1,0:T(8,128)(2,1)S(1)} %collective-permute-done.16.refs_1_, bf16[256,512]{1,0:T(8,128)(2,1)S(1)} %collective-permute-done.17.refs_2_, ...), custom_call_target="tpu_custom_call" | custom-call | flops 1073741824 | bytes 7340032 | tf_op jit(solution)/shard_map/pallas_call | solution.py:231
  91.6 1.9 %collective-permute-start.26 = (bf16[256,512]{1,0:T(8,128)(2,1)}, bf16[256,512]{1,0:T(8,128)(2,1)S(1)}, u32[]{:S(2)}, u32[]{:S(2)}) collective-permute-start(bf16[256,512]{1,0:T(8,128)(2,1)} %shard_map.47), channel_id=1, source_target_pairs={{0,16},{1,17},{2,18},{3,19},{4,68},{5,69},{6,70},{7,71},{8,24},{9,... | collective-permute-start | bytes 786440 | tf_op jit(solution)/shard_map/ppermute | solution.py:42
  94.0 2.2 %collective-permute-start.23 = (bf16[256,512]{1,0:T(8,128)(2,1)}, bf16[256,512]{1,0:T(8,128)(2,1)S(1)}, u32[]{:S(2)}, u32[]{:S(2)}) collective-permute-start(bf16[256,512]{1,0:T(8,128)(2,1)} %shard_map.47), channel_id=1, source_target_pairs={{0,96},{1,97},{2,98},{3,99},{4,28},{5,29},{6,30},{7,31},{8,104},{9... | collective-permute-start | bytes 786440 | tf_op jit(solution)/shard_map/ppermute | solution.py:37
  96.1 4.4 %collective-permute-done.26 = bf16[256,512]{1,0:T(8,128)(2,1)S(1)} collective-permute-done((bf16[256,512]{1,0:T(8,128)(2,1)}, bf16[256,512]{1,0:T(8,128)(2,1)S(1)}, u32[]{:S(2)}, u32[]{:S(2)}) %collective-permute-start.26) | collective-permute-done | bytes 262176 | tf_op jit(solution)/shard_map/ppermute | solution.py:42
  100.5 1.9 %collective-permute-done.25 = bf16[256,512]{1,0:T(8,128)(2,1)S(1)} collective-permute-done((bf16[256,512]{1,0:T(8,128)(2,1)}, bf16[256,512]{1,0:T(8,128)(2,1)S(1)}, u32[]{:S(2)}, u32[]{:S(2)}) %collective-permute-start.25) | collective-permute-done | bytes 262176 | tf_op jit(solution)/shard_map/ppermute | solution.py:37
  102.4 3.1 %collective-permute-done.24 = bf16[256,512]{1,0:T(8,128)(2,1)S(1)} collective-permute-done((bf16[256,512]{1,0:T(8,128)(2,1)}, bf16[256,512]{1,0:T(8,128)(2,1)S(1)}, u32[]{:S(2)}, u32[]{:S(2)}) %collective-permute-start.24) | collective-permute-done | bytes 262176 | tf_op jit(solution)/shard_map/ppermute | solution.py:37
  105.5 1.0 constant_dynamic-update-slice_fusion.11
  106.5 1.3 collective-permute-start.31
  107.8 1.5 collective-permute-start.27
  110.8 6.9 %collective-permute-done.28 = bf16[256,512]{1,0:T(8,128)(2,1)S(1)} collective-permute-done((bf16[256,512]{1,0:T(8,128)(2,1)S(1)}, bf16[256,512]{1,0:T(8,128)(2,1)S(1)}, u32[]{:S(2)}, u32[]{:S(2)}) %collective-permute-start.28) | collective-permute-done | bytes 262176 | tf_op jit(solution)/shard_map/ppermute | solution.py:37
  117.7 2.0 %collective-permute-done.29 = bf16[256,512]{1,0:T(8,128)(2,1)S(1)} collective-permute-done((bf16[256,512]{1,0:T(8,128)(2,1)S(1)}, bf16[256,512]{1,0:T(8,128)(2,1)S(1)}, u32[]{:S(2)}, u32[]{:S(2)}) %collective-permute-start.29) | collective-permute-done | bytes 262176 | tf_op jit(solution)/shard_map/ppermute | solution.py:37
  119.7 3.0 %collective-permute-done.30 = bf16[256,512]{1,0:T(8,128)(2,1)S(1)} collective-permute-done((bf16[256,512]{1,0:T(8,128)(2,1)S(1)}, bf16[256,512]{1,0:T(8,128)(2,1)S(1)}, u32[]{:S(2)}, u32[]{:S(2)}) %collective-permute-start.30) | collective-permute-done | bytes 262176 | tf_op jit(solution)/shard_map/ppermute | solution.py:37
  122.7 4.6 %collective-permute-done.31.refs_3_.refs_12_ = bf16[1024,512]{1,0:T(8,128)(2,1)S(1)} collective-permute-done((bf16[1024,512]{1,0:T(8,128)(2,1)S(1)}, bf16[1024,512]{1,0:T(8,128)(2,1)S(1)}, u32[]{:S(2)}, u32[]{:S(2)}) %collective-permute-start.31) | collective-permute-done | bytes 1048608 | tf_op jit(solution)/shard_map/ppermute | solution.py:42
  128.3 1.2 copy-done.2
  129.6 1.6 copy-done.3
  131.2 2.9 %shard_map.48 = (f32[256,512]{1,0:T(8,128)S(1)}, bf16[256,512]{1,0:T(8,128)(2,1)S(1)}) custom-call(s32[4]{0:T(128)S(1)} %pad_add_fusion.1.where, s32[2,32,32]{2,1,0:T(8,128)S(1)} %copy-done.5, bf16[2048,512]{1,0:T(8,128)(2,1)S(1)} %copy-done.3, bf16[1024,512]{1,0:T(8,128)(2,1)S(1)} %constant_dynamic-update-slice_fusion.8.refs_0_.refs_9_, ...), custom_call_target="tpu_custom_call" | custom-call | flops 1073741824 | bytes 7340032 | tf_op jit(solution)/shard_map/pallas_call | solution.py:238
  134.1 3.0 %collective-permute-start.33 = (bf16[256,512]{1,0:T(8,128)(2,1)S(1)}, bf16[256,512]{1,0:T(8,128)(2,1)S(1)}, u32[]{:S(2)}, u32[]{:S(2)}) collective-permute-start(bf16[256,512]{1,0:T(8,128)(2,1)S(1)} %get-tuple-element.35.refs_0_), channel_id=1, source_target_pairs={{0,2},{1,3},{2,0},{3,1},{4,6},{5,7},{6,4},{7,5},{8,10},{9,11},{10,... | collective-permute-start | bytes 786440 | tf_op jit(solution)/shard_map/ppermute | solution.py:33
  137.1 1.7 %collective-permute-start.35 = (bf16[256,512]{1,0:T(8,128)(2,1)S(1)}, bf16[256,512]{1,0:T(8,128)(2,1)S(1)}, u32[]{:S(2)}, u32[]{:S(2)}) collective-permute-start(bf16[256,512]{1,0:T(8,128)(2,1)S(1)} %get-tuple-element.35.refs_0_), channel_id=1, source_target_pairs={{0,4},{1,5},{2,6},{3,7},{4,0},{5,1},{6,2},{7,3},{8,12},{9,13},{10,... | collective-permute-start | bytes 786440 | tf_op jit(solution)/shard_map/ppermute | solution.py:29
  138.8 3.7 %collective-permute-done.34.refs_3_ = bf16[256,512]{1,0:T(8,128)(2,1)S(1)} collective-permute-done((bf16[256,512]{1,0:T(8,128)(2,1)S(1)}, bf16[256,512]{1,0:T(8,128)(2,1)S(1)}, u32[]{:S(2)}, u32[]{:S(2)}) %collective-permute-start.34) | collective-permute-done | bytes 262176 | tf_op jit(solution)/shard_map/ppermute | solution.py:33
  142.5 2.9 %collective-permute-start.38 = (bf16[256,512]{1,0:T(8,128)(2,1)S(1)}, bf16[256,512]{1,0:T(8,128)(2,1)S(1)}, u32[]{:S(2)}, u32[]{:S(2)}) collective-permute-start(bf16[256,512]{1,0:T(8,128)(2,1)S(1)} %collective-permute-done.34.refs_3_), channel_id=1, source_target_pairs={{0,4},{1,5},{2,6},{3,7},{4,0},{5,1},{6,2},{7,3},{8,12},{9,13},{10,... | collective-permute-start | bytes 786440 | tf_op jit(solution)/shard_map/ppermute | solution.py:29
  145.4 2.5 %collective-permute-done.33.refs_2_ = bf16[256,512]{1,0:T(8,128)(2,1)S(1)} collective-permute-done((bf16[256,512]{1,0:T(8,128)(2,1)S(1)}, bf16[256,512]{1,0:T(8,128)(2,1)S(1)}, u32[]{:S(2)}, u32[]{:S(2)}) %collective-permute-start.33) | collective-permute-done | bytes 262176 | tf_op jit(solution)/shard_map/ppermute | solution.py:33
  147.9 2.1 %collective-permute-start.37 = (bf16[256,512]{1,0:T(8,128)(2,1)S(1)}, bf16[256,512]{1,0:T(8,128)(2,1)S(1)}, u32[]{:S(2)}, u32[]{:S(2)}) collective-permute-start(bf16[256,512]{1,0:T(8,128)(2,1)S(1)} %collective-permute-done.33.refs_2_), channel_id=1, source_target_pairs={{0,4},{1,5},{2,6},{3,7},{4,0},{5,1},{6,2},{7,3},{8,12},{9,13},{10,... | collective-permute-start | bytes 786440 | tf_op jit(solution)/shard_map/ppermute | solution.py:29
  151.5 3.1 %shard_map.49 = (f32[128,512]{1,0:T(8,128)S(1)}, f32[128,512]{1,0:T(8,128)}) custom-call(s32[4]{0:T(128)S(1)} %pad_add_fusion.1.where, bf16[256,512]{1,0:T(8,128)(2,1)S(1)} %get-tuple-element.35.refs_0_, bf16[256,512]{1,0:T(8,128)(2,1)S(1)} %collective-permute-done.32.refs_1_, bf16[256,512]{1,0:T(8,128)(2,1)S(1)} %collective-permute-done.33.refs_2_, ...), custom_call_target="tpu_custom_call" | custom-call | flops 1073741824 | bytes 8388608 | tf_op jit(solution)/shard_map/pallas_call | solution.py:246
  155.0 1.4 collective-permute-done.39
  (79 shorter events, 13.0 us)
Async XLA Ops:
  6.5 6.0 %copy-start = (s32[32,8]{0,1:T(8,128)S(1)}, s32[32,8]{0,1:T(8,128)}, u32[]{:S(2)}) copy-start(s32[32,8]{0,1:T(8,128)} %param.5) | copy-start | bytes 3076
  6.5 52.8 %copy-start.5 = (s32[2,32,32]{2,1,0:T(8,128)S(1)}, s32[2,32,32]{2,1,0:T(8,128)}, u32[]{:S(2)}) copy-start(s32[2,32,32]{2,1,0:T(8,128)} %keep_s.3) | copy-start | bytes 24580
  6.5 52.9 %copy-start.4 = (s32[2,32,32]{2,1,0:T(8,128)S(1)}, s32[2,32,32]{2,1,0:T(8,128)}, u32[]{:S(2)}) copy-start(s32[2,32,32]{2,1,0:T(8,128)} %keep_d.3) | copy-start | bytes 24580
  6.5 121.8 %all-gather.2.cloned.1.call-start = ((), (), s32[]{:S(2)}) async-start(), calls=%async_computation | async-start | bytes 2359296 | tf_op jit(solution)/shard_map/all_gather | solution.py:235
  6.5 6.8 %collective-permute-start.1 = (bf16[128,256]{1,0:T(8,128)(2,1)}, bf16[128,256]{1,0:T(8,128)(2,1)S(1)}, u32[]{:S(2)}, u32[]{:S(2)}) collective-permute-start(bf16[128,256]{1,0:T(8,128)(2,1)} %param.4), channel_id=1, source_target_pairs={{0,2},{1,3},{2,0},{3,1},{4,6},{5,7},{6,4},{7,5},{8,10},{9,11},{10,... | collective-permute-start | bytes 196616 | tf_op jit(solution)/shard_map/ppermute | solution.py:33
  11.1 3.7 %collective-permute-start = (bf16[128,256]{1,0:T(8,128)(2,1)}, bf16[128,256]{1,0:T(8,128)(2,1)S(1)}, u32[]{:S(2)}, u32[]{:S(2)}) collective-permute-start(bf16[128,256]{1,0:T(8,128)(2,1)} %param.4), channel_id=1, source_target_pairs={{0,3},{1,0},{2,1},{3,2},{4,7},{5,4},{6,5},{7,6},{8,11},{9,8},{10,9... | collective-permute-start | bytes 196616 | tf_op jit(solution)/shard_map/ppermute | solution.py:33
  11.5 4.5 %collective-permute-start.2 = (bf16[128,256]{1,0:T(8,128)(2,1)}, bf16[128,256]{1,0:T(8,128)(2,1)S(1)}, u32[]{:S(2)}, u32[]{:S(2)}) collective-permute-start(bf16[128,256]{1,0:T(8,128)(2,1)} %param.4), channel_id=1, source_target_pairs={{0,1},{1,2},{2,3},{3,0},{4,5},{5,6},{6,7},{7,4},{8,9},{9,10},{10,1... | collective-permute-start | bytes 196616 | tf_op jit(solution)/shard_map/ppermute | solution.py:33
  16.9 8.4 %collective-permute-start.6 = (bf16[128,1024]{1,0:T(8,128)(2,1)S(1)}, bf16[128,1024]{1,0:T(8,128)(2,1)S(1)}, u32[]{:S(2)}, u32[]{:S(2)}) collective-permute-start(bf16[128,1024]{1,0:T(8,128)(2,1)S(1)} %maximum_multiply_fusion), channel_id=1, source_target_pairs={{0,16},{1,17},{2,18},{3,19},{4,68},{5,69},{6,70},{7,71},{8,24},{9,... | collective-permute-start | bytes 786440 | tf_op jit(solution)/shard_map/ppermute | solution.py:42
  19.7 9.8 %collective-permute-start.5 = (bf16[128,1024]{1,0:T(8,128)(2,1)S(1)}, bf16[128,1024]{1,0:T(8,128)(2,1)S(1)}, u32[]{:S(2)}, u32[]{:S(2)}) collective-permute-start(bf16[128,1024]{1,0:T(8,128)(2,1)S(1)} %maximum_multiply_fusion), channel_id=1, source_target_pairs={{0,64},{1,65},{2,66},{3,67},{4,20},{5,21},{6,22},{7,23},{8,72},{9,... | collective-permute-start | bytes 786440 | tf_op jit(solution)/shard_map/ppermute | solution.py:37
  22.7 9.7 %collective-permute-start.4 = (bf16[128,1024]{1,0:T(8,128)(2,1)S(1)}, bf16[128,1024]{1,0:T(8,128)(2,1)S(1)}, u32[]{:S(2)}, u32[]{:S(2)}) collective-permute-start(bf16[128,1024]{1,0:T(8,128)(2,1)S(1)} %maximum_multiply_fusion), channel_id=1, source_target_pairs={{0,32},{1,33},{2,34},{3,35},{4,12},{5,13},{6,14},{7,15},{8,40},{9,... | collective-permute-start | bytes 786440 | tf_op jit(solution)/shard_map/ppermute | solution.py:37
  23.1 9.7 %collective-permute-start.3 = (bf16[128,1024]{1,0:T(8,128)(2,1)S(1)}, bf16[128,1024]{1,0:T(8,128)(2,1)S(1)}, u32[]{:S(2)}, u32[]{:S(2)}) collective-permute-start(bf16[128,1024]{1,0:T(8,128)(2,1)S(1)} %maximum_multiply_fusion), channel_id=1, source_target_pairs={{0,96},{1,97},{2,98},{3,99},{4,28},{5,29},{6,30},{7,31},{8,104},{9... | collective-permute-start | bytes 786440 | tf_op jit(solution)/shard_map/ppermute | solution.py:37
  32.9 20.9 %collective-permute-start.11 = (bf16[512,1024]{1,0:T(8,128)(2,1)S(1)}, bf16[512,1024]{1,0:T(8,128)(2,1)}, u32[]{:S(2)}, u32[]{:S(2)}) collective-permute-start(bf16[512,1024]{1,0:T(8,128)(2,1)S(1)} %constant_dynamic-update-slice_fusion.refs_0_), channel_id=1, source_target_pairs={{0,8},{1,9},{2,10},{3,11},{4,36},{5,37},{6,38},{7,39},{8,16},{9,17... | collective-permute-start | bytes 3145736 | tf_op jit(solution)/shard_map/ppermute | solution.py:42
  33.3 22.0 %collective-permute-start.7 = (bf16[512,1024]{1,0:T(8,128)(2,1)S(1)}, bf16[512,1024]{1,0:T(8,128)(2,1)}, u32[]{:S(2)}, u32[]{:S(2)}) collective-permute-start(bf16[512,1024]{1,0:T(8,128)(2,1)S(1)} %constant_dynamic-update-slice_fusion.refs_0_), channel_id=1, source_target_pairs={{0,24},{1,25},{2,26},{3,27},{4,100},{5,101},{6,102},{7,103},{8,0},... | collective-permute-start | bytes 3145736 | tf_op jit(solution)/shard_map/ppermute | solution.py:42
  35.6 8.5 %collective-permute-start.8 = (bf16[128,1024]{1,0:T(8,128)(2,1)S(1)}, bf16[128,1024]{1,0:T(8,128)(2,1)S(1)}, u32[]{:S(2)}, u32[]{:S(2)}) collective-permute-start(bf16[128,1024]{1,0:T(8,128)(2,1)S(1)} %collective-permute-done.6), channel_id=1, source_target_pairs={{0,96},{1,97},{2,98},{3,99},{4,28},{5,29},{6,30},{7,31},{8,104},{9... | collective-permute-start | bytes 786440 | tf_op jit(solution)/shard_map/ppermute | solution.py:37
  37.7 10.1 %collective-permute-start.9 = (bf16[128,1024]{1,0:T(8,128)(2,1)S(1)}, bf16[128,1024]{1,0:T(8,128)(2,1)S(1)}, u32[]{:S(2)}, u32[]{:S(2)}) collective-permute-start(bf16[128,1024]{1,0:T(8,128)(2,1)S(1)} %collective-permute-done.6), channel_id=1, source_target_pairs={{0,64},{1,65},{2,66},{3,67},{4,20},{5,21},{6,22},{7,23},{8,72},{9,... | collective-permute-start | bytes 786440 | tf_op jit(solution)/shard_map/ppermute | solution.py:37
  38.2 12.4 %collective-permute-start.10 = (bf16[128,1024]{1,0:T(8,128)(2,1)S(1)}, bf16[128,1024]{1,0:T(8,128)(2,1)S(1)}, u32[]{:S(2)}, u32[]{:S(2)}) collective-permute-start(bf16[128,1024]{1,0:T(8,128)(2,1)S(1)} %collective-permute-done.6), channel_id=1, source_target_pairs={{0,32},{1,33},{2,34},{3,35},{4,12},{5,13},{6,14},{7,15},{8,40},{9,... | collective-permute-start | bytes 786440 | tf_op jit(solution)/shard_map/ppermute | solution.py:37
  44.1 11.2 %collective-permute-start.12 = (bf16[512,1024]{1,0:T(8,128)(2,1)S(1)}, bf16[512,1024]{1,0:T(8,128)(2,1)}, u32[]{:S(2)}, u32[]{:S(2)}) collective-permute-start(bf16[512,1024]{1,0:T(8,128)(2,1)S(1)} %constant_dynamic-update-slice_fusion.refs_0_), channel_id=1, source_target_pairs={{0,4},{1,5},{2,6},{3,7},{4,0},{5,1},{6,2},{7,3},{8,12},{9,13},{10,... | collective-permute-start | bytes 3145736 | tf_op jit(solution)/shard_map/ppermute | solution.py:29
  50.6 5.4 %collective-permute-start.14 = (bf16[512,1024]{1,0:T(8,128)(2,1)S(1)}, bf16[512,1024]{1,0:T(8,128)(2,1)}, u32[]{:S(2)}, u32[]{:S(2)}) collective-permute-start(bf16[512,1024]{1,0:T(8,128)(2,1)S(1)} %constant_dynamic-update-slice_fusion.4.refs_2_), channel_id=1, source_target_pairs={{0,4},{1,5},{2,6},{3,7},{4,0},{5,1},{6,2},{7,3},{8,12},{9,13},{10,... | collective-permute-start | bytes 3145736 | tf_op jit(solution)/shard_map/ppermute | solution.py:29
  53.8 4.1 %collective-permute-start.15 = (bf16[512,1024]{1,0:T(8,128)(2,1)}, bf16[512,1024]{1,0:T(8,128)(2,1)}, u32[]{:S(2)}, u32[]{:S(2)}) collective-permute-start(bf16[512,1024]{1,0:T(8,128)(2,1)} %collective-permute-done.11.refs_3_), channel_id=1, source_target_pairs={{0,4},{1,5},{2,6},{3,7},{4,0},{5,1},{6,2},{7,3},{8,12},{9,13},{10,... | collective-permute-start | bytes 3145736 | tf_op jit(solution)/shard_map/ppermute | solution.py:29
  55.3 4.1 %collective-permute-start.13 = (bf16[512,1024]{1,0:T(8,128)(2,1)}, bf16[512,1024]{1,0:T(8,128)(2,1)}, u32[]{:S(2)}, u32[]{:S(2)}) collective-permute-start(bf16[512,1024]{1,0:T(8,128)(2,1)} %collective-permute-done.7.refs_1_), channel_id=1, source_target_pairs={{0,4},{1,5},{2,6},{3,7},{4,0},{5,1},{6,2},{7,3},{8,12},{9,13},{10,... | collective-permute-start | bytes 3145736 | tf_op jit(solution)/shard_map/ppermute | solution.py:29
  71.0 14.4 %collective-permute-start.18 = (bf16[256,512]{1,0:T(8,128)(2,1)S(1)}, bf16[256,512]{1,0:T(8,128)(2,1)S(1)}, u32[]{:S(2)}, u32[]{:S(2)}) collective-permute-start(bf16[256,512]{1,0:T(8,128)(2,1)S(1)} %get-tuple-element.27.refs_0_), channel_id=1, source_target_pairs={{0,1},{1,2},{2,3},{3,0},{4,5},{5,6},{6,7},{7,4},{8,9},{9,10},{10,1... | collective-permute-start | bytes 786440 | tf_op jit(solution)/shard_map/ppermute | solution.py:33
  71.1 15.5 %collective-permute-start.17 = (bf16[256,512]{1,0:T(8,128)(2,1)S(1)}, bf16[256,512]{1,0:T(8,128)(2,1)S(1)}, u32[]{:S(2)}, u32[]{:S(2)}) collective-permute-start(bf16[256,512]{1,0:T(8,128)(2,1)S(1)} %get-tuple-element.27.refs_0_), channel_id=1, source_target_pairs={{0,2},{1,3},{2,0},{3,1},{4,6},{5,7},{6,4},{7,5},{8,10},{9,11},{10,... | collective-permute-start | bytes 786440 | tf_op jit(solution)/shard_map/ppermute | solution.py:33
  72.7 14.0 %collective-permute-start.16 = (bf16[256,512]{1,0:T(8,128)(2,1)S(1)}, bf16[256,512]{1,0:T(8,128)(2,1)S(1)}, u32[]{:S(2)}, u32[]{:S(2)}) collective-permute-start(bf16[256,512]{1,0:T(8,128)(2,1)S(1)} %get-tuple-element.27.refs_0_), channel_id=1, source_target_pairs={{0,3},{1,0},{2,1},{3,2},{4,7},{5,4},{6,5},{7,6},{8,11},{9,8},{10,9... | collective-permute-start | bytes 786440 | tf_op jit(solution)/shard_map/ppermute | solution.py:33
  74.0 13.2 %collective-permute-start.19 = (bf16[256,512]{1,0:T(8,128)(2,1)S(1)}, bf16[256,512]{1,0:T(8,128)(2,1)S(1)}, u32[]{:S(2)}, u32[]{:S(2)}) collective-permute-start(bf16[256,512]{1,0:T(8,128)(2,1)S(1)} %get-tuple-element.27.refs_0_), channel_id=1, source_target_pairs={{0,4},{1,5},{2,6},{3,7},{4,0},{5,1},{6,2},{7,3},{8,12},{9,13},{10,... | collective-permute-start | bytes 786440 | tf_op jit(solution)/shard_map/ppermute | solution.py:29
  85.4 2.4 %collective-permute-start.22 = (bf16[256,512]{1,0:T(8,128)(2,1)S(1)}, bf16[256,512]{1,0:T(8,128)(2,1)S(1)}, u32[]{:S(2)}, u32[]{:S(2)}) collective-permute-start(bf16[256,512]{1,0:T(8,128)(2,1)S(1)} %collective-permute-done.18.refs_3_), channel_id=1, source_target_pairs={{0,4},{1,5},{2,6},{3,7},{4,0},{5,1},{6,2},{7,3},{8,12},{9,13},{10,... | collective-permute-start | bytes 786440 | tf_op jit(solution)/shard_map/ppermute | solution.py:29
  86.6 1.5 collective-permute-start.21
  86.6 1.9 %collective-permute-start.20 = (bf16[256,512]{1,0:T(8,128)(2,1)S(1)}, bf16[256,512]{1,0:T(8,128)(2,1)S(1)}, u32[]{:S(2)}, u32[]{:S(2)}) collective-permute-start(bf16[256,512]{1,0:T(8,128)(2,1)S(1)} %collective-permute-done.16.refs_1_), channel_id=1, source_target_pairs={{0,4},{1,5},{2,6},{3,7},{4,0},{5,1},{6,2},{7,3},{8,12},{9,13},{10,... | collective-permute-start | bytes 786440 | tf_op jit(solution)/shard_map/ppermute | solution.py:29
  91.6 8.9 %collective-permute-start.26 = (bf16[256,512]{1,0:T(8,128)(2,1)}, bf16[256,512]{1,0:T(8,128)(2,1)S(1)}, u32[]{:S(2)}, u32[]{:S(2)}) collective-permute-start(bf16[256,512]{1,0:T(8,128)(2,1)} %shard_map.47), channel_id=1, source_target_pairs={{0,16},{1,17},{2,18},{3,19},{4,68},{5,69},{6,70},{7,71},{8,24},{9,... | collective-permute-start | bytes 786440 | tf_op jit(solution)/shard_map/ppermute | solution.py:42
  93.5 8.9 %collective-permute-start.25 = (bf16[256,512]{1,0:T(8,128)(2,1)}, bf16[256,512]{1,0:T(8,128)(2,1)S(1)}, u32[]{:S(2)}, u32[]{:S(2)}) collective-permute-start(bf16[256,512]{1,0:T(8,128)(2,1)} %shard_map.47), channel_id=1, source_target_pairs={{0,64},{1,65},{2,66},{3,67},{4,20},{5,21},{6,22},{7,23},{8,72},{9,... | collective-permute-start | bytes 786440 | tf_op jit(solution)/shard_map/ppermute | solution.py:37
  93.5 12.0 %collective-permute-start.24 = (bf16[256,512]{1,0:T(8,128)(2,1)}, bf16[256,512]{1,0:T(8,128)(2,1)S(1)}, u32[]{:S(2)}, u32[]{:S(2)}) collective-permute-start(bf16[256,512]{1,0:T(8,128)(2,1)} %shard_map.47), channel_id=1, source_target_pairs={{0,32},{1,33},{2,34},{3,35},{4,12},{5,13},{6,14},{7,15},{8,40},{9,... | collective-permute-start | bytes 786440 | tf_op jit(solution)/shard_map/ppermute | solution.py:37
  94.0 11.5 %collective-permute-start.23 = (bf16[256,512]{1,0:T(8,128)(2,1)}, bf16[256,512]{1,0:T(8,128)(2,1)S(1)}, u32[]{:S(2)}, u32[]{:S(2)}) collective-permute-start(bf16[256,512]{1,0:T(8,128)(2,1)} %shard_map.47), channel_id=1, source_target_pairs={{0,96},{1,97},{2,98},{3,99},{4,28},{5,29},{6,30},{7,31},{8,104},{9... | collective-permute-start | bytes 786440 | tf_op jit(solution)/shard_map/ppermute | solution.py:37
  106.5 20.8 %collective-permute-start.31 = (bf16[1024,512]{1,0:T(8,128)(2,1)S(1)}, bf16[1024,512]{1,0:T(8,128)(2,1)S(1)}, u32[]{:S(2)}, u32[]{:S(2)}) collective-permute-start(bf16[1024,512]{1,0:T(8,128)(2,1)S(1)} %constant_dynamic-update-slice_fusion.8.refs_0_.refs_9_), channel_id=1, source_target_pairs={{0,8},{1,9},{2,10},{3,11},{4,36},{5,37},{6,38},{7,39},{8,16},{9,17... | collective-permute-start | bytes 3145736 | tf_op jit(solution)/shard_map/ppermute | solution.py:42
  107.8 19.6 %collective-permute-start.27 = (bf16[1024,512]{1,0:T(8,128)(2,1)S(1)}, bf16[1024,512]{1,0:T(8,128)(2,1)S(1)}, u32[]{:S(2)}, u32[]{:S(2)}) collective-permute-start(bf16[1024,512]{1,0:T(8,128)(2,1)S(1)} %constant_dynamic-update-slice_fusion.8.refs_0_.refs_9_), channel_id=1, source_target_pairs={{0,24},{1,25},{2,26},{3,27},{4,100},{5,101},{6,102},{7,103},{8,0},... | collective-permute-start | bytes 3145736 | tf_op jit(solution)/shard_map/ppermute | solution.py:42
  109.3 8.4 %collective-permute-start.28 = (bf16[256,512]{1,0:T(8,128)(2,1)S(1)}, bf16[256,512]{1,0:T(8,128)(2,1)S(1)}, u32[]{:S(2)}, u32[]{:S(2)}) collective-permute-start(bf16[256,512]{1,0:T(8,128)(2,1)S(1)} %collective-permute-done.26), channel_id=1, source_target_pairs={{0,96},{1,97},{2,98},{3,99},{4,28},{5,29},{6,30},{7,31},{8,104},{9... | collective-permute-start | bytes 786440 | tf_op jit(solution)/shard_map/ppermute | solution.py:37
  109.8 9.9 %collective-permute-start.29 = (bf16[256,512]{1,0:T(8,128)(2,1)S(1)}, bf16[256,512]{1,0:T(8,128)(2,1)S(1)}, u32[]{:S(2)}, u32[]{:S(2)}) collective-permute-start(bf16[256,512]{1,0:T(8,128)(2,1)S(1)} %collective-permute-done.26), channel_id=1, source_target_pairs={{0,64},{1,65},{2,66},{3,67},{4,20},{5,21},{6,22},{7,23},{8,72},{9,... | collective-permute-start | bytes 786440 | tf_op jit(solution)/shard_map/ppermute | solution.py:37
  110.5 12.2 %collective-permute-start.30 = (bf16[256,512]{1,0:T(8,128)(2,1)S(1)}, bf16[256,512]{1,0:T(8,128)(2,1)S(1)}, u32[]{:S(2)}, u32[]{:S(2)}) collective-permute-start(bf16[256,512]{1,0:T(8,128)(2,1)S(1)} %collective-permute-done.26), channel_id=1, source_target_pairs={{0,32},{1,33},{2,34},{3,35},{4,12},{5,13},{6,14},{7,15},{8,40},{9,... | collective-permute-start | bytes 786440 | tf_op jit(solution)/shard_map/ppermute | solution.py:37
  127.4 1.0 copy-start.1
  128.3 1.2 copy-start.2
  129.6 1.6 copy-start.3
  134.0 8.5 %collective-permute-start.34 = (bf16[256,512]{1,0:T(8,128)(2,1)S(1)}, bf16[256,512]{1,0:T(8,128)(2,1)S(1)}, u32[]{:S(2)}, u32[]{:S(2)}) collective-permute-start(bf16[256,512]{1,0:T(8,128)(2,1)S(1)} %get-tuple-element.35.refs_0_), channel_id=1, source_target_pairs={{0,1},{1,2},{2,3},{3,0},{4,5},{5,6},{6,7},{7,4},{8,9},{9,10},{10,1... | collective-permute-start | bytes 786440 | tf_op jit(solution)/shard_map/ppermute | solution.py:33
  134.1 13.8 %collective-permute-start.33 = (bf16[256,512]{1,0:T(8,128)(2,1)S(1)}, bf16[256,512]{1,0:T(8,128)(2,1)S(1)}, u32[]{:S(2)}, u32[]{:S(2)}) collective-permute-start(bf16[256,512]{1,0:T(8,128)(2,1)S(1)} %get-tuple-element.35.refs_0_), channel_id=1, source_target_pairs={{0,2},{1,3},{2,0},{3,1},{4,6},{5,7},{6,4},{7,5},{8,10},{9,11},{10,... | collective-permute-start | bytes 786440 | tf_op jit(solution)/shard_map/ppermute | solution.py:33
  137.1 12.9 %collective-permute-start.32 = (bf16[256,512]{1,0:T(8,128)(2,1)S(1)}, bf16[256,512]{1,0:T(8,128)(2,1)S(1)}, u32[]{:S(2)}, u32[]{:S(2)}) collective-permute-start(bf16[256,512]{1,0:T(8,128)(2,1)S(1)} %get-tuple-element.35.refs_0_), channel_id=1, source_target_pairs={{0,3},{1,0},{2,1},{3,2},{4,7},{5,4},{6,5},{7,6},{8,11},{9,8},{10,9... | collective-permute-start | bytes 786440 | tf_op jit(solution)/shard_map/ppermute | solution.py:33
  137.1 13.2 %collective-permute-start.35 = (bf16[256,512]{1,0:T(8,128)(2,1)S(1)}, bf16[256,512]{1,0:T(8,128)(2,1)S(1)}, u32[]{:S(2)}, u32[]{:S(2)}) collective-permute-start(bf16[256,512]{1,0:T(8,128)(2,1)S(1)} %get-tuple-element.35.refs_0_), channel_id=1, source_target_pairs={{0,4},{1,5},{2,6},{3,7},{4,0},{5,1},{6,2},{7,3},{8,12},{9,13},{10,... | collective-permute-start | bytes 786440 | tf_op jit(solution)/shard_map/ppermute | solution.py:29
  142.5 7.7 %collective-permute-start.38 = (bf16[256,512]{1,0:T(8,128)(2,1)S(1)}, bf16[256,512]{1,0:T(8,128)(2,1)S(1)}, u32[]{:S(2)}, u32[]{:S(2)}) collective-permute-start(bf16[256,512]{1,0:T(8,128)(2,1)S(1)} %collective-permute-done.34.refs_3_), channel_id=1, source_target_pairs={{0,4},{1,5},{2,6},{3,7},{4,0},{5,1},{6,2},{7,3},{8,12},{9,13},{10,... | collective-permute-start | bytes 786440 | tf_op jit(solution)/shard_map/ppermute | solution.py:29
  147.9 3.2 %collective-permute-start.37 = (bf16[256,512]{1,0:T(8,128)(2,1)S(1)}, bf16[256,512]{1,0:T(8,128)(2,1)S(1)}, u32[]{:S(2)}, u32[]{:S(2)}) collective-permute-start(bf16[256,512]{1,0:T(8,128)(2,1)S(1)} %collective-permute-done.33.refs_2_), channel_id=1, source_target_pairs={{0,4},{1,5},{2,6},{3,7},{4,0},{5,1},{6,2},{7,3},{8,12},{9,13},{10,... | collective-permute-start | bytes 786440 | tf_op jit(solution)/shard_map/ppermute | solution.py:29
  150.0 1.5 collective-permute-start.36
  154.6 1.8 %collective-permute-start.39 = (f32[128,512]{1,0:T(8,128)}, f32[128,512]{1,0:T(8,128)S(1)}, u32[]{:S(2)}, u32[]{:S(2)}) collective-permute-start(f32[128,512]{1,0:T(8,128)} %get-tuple-element.38), channel_id=1, source_target_pairs={{0,4},{1,5},{2,6},{3,7},{4,0},{5,1},{6,2},{7,3},{8,12},{9,13},{10,... | collective-permute-start | bytes 786440 | tf_op jit(solution)/shard_map/ppermute | solution.py:29
Sparse Core Ops, SparseCore 0:
  91.7 23.7 all-gather.1

commit v4 on v3

v4 whole, which is shorter than its diff:
```python
import jax
import jax.numpy as jnp
from jax import lax
from jax.experimental import pallas as pl
from jax.experimental.pallas import tpu as pltpu
from jax.sharding import PartitionSpec as P

B = 128
N = 4096
K = 1024
ROWS = 256
COLS = 512
DEPTH = 256
AXES = ("row", "col")
MIB = 1024 * 1024


def device(x, y, core, z):
    return (((x % 4) * 4 + y % 4) * 2 + core) * 4 + z % 4


def pairs(target):
    return [
        (device(x, y, core, z), device(*target(x, y, core, z)))
        for x in range(4) for y in range(4) for core in range(2) for z in range(4)
    ]


def other_core(a):
    return lax.ppermute(a, AXES, pairs(lambda x, y, core, z: (x, y, 1 - core, z)))


def from_z(a, d):
    return lax.ppermute(a, AXES, pairs(lambda x, y, core, z: (x, y, core, z - d)))


def from_first(a, d):
    return lax.ppermute(a, AXES, pairs(
        lambda x, y, core, z: (x - d, y, core, z) if core == 0 else (x, y - d, core, z)))


def from_second(a, d):
    return lax.ppermute(a, AXES, pairs(
        lambda x, y, core, z: (x, y - d, core, z) if core == 0 else (x - d, y, core, z)))


def gather(a, fetch):
    one, three, two = fetch(a, 1), fetch(a, 3), fetch(a, 2)
    return [a, one, two, three]


def place(x, y, kind, first, second):
    px = jnp.where(kind == 0, x + first, x + second) & 3
    py = jnp.where(kind == 0, y + second, y + first) & 3
    return px, py


def dot_t(a, b):
    return lax.dot_general(a, b, (((1,), (1,)), ((), ())), preferred_element_type=jnp.float32)


def dot(a, b):
    return jnp.dot(a, b, preferred_element_type=jnp.float32)


def aligned(block, size):
    return pl.ds(pl.multiple_of(block * size, size), size)


def pick_rows(where, own, other, rows):
    x, y, core, z = where[0], where[1], where[2], where[3]
    for t in range(6):
        kind = t & 1
        if t < 4:
            dx, dy = (z - x) & 3, (core * 2 + (t >> 1) - y) & 3
            first, second = (dx, dy) if kind == 0 else (dy, dx)
            at = aligned(second * 4 + first, B)
        else:
            at = pl.ds(0, B)
        rows[t * B:(t + 1) * B, :] = jnp.where(kind == core, own[at, :], other[at, :])


def early_density(where, *refs):
    sets, total, rows = refs[:-2], refs[-2], refs[-1]
    add = len(sets) % 2 == 1
    if add:
        before, sets = sets[0], sets[1:]
    for n in range(len(sets) // 2):
        own, other = sets[2 * n], sets[2 * n + 1]
        pick_rows(where, own, other, rows.at[:, pl.ds(n * DEPTH, DEPTH)])
    for half in range(2):
        for j in range(4):
            part = jnp.concatenate([sets[2 * n + half][j * 512:(j + 1) * 512, :] for n in range(len(sets) // 2)], axis=1)
            at = slice((half * 4 + j) * 512, (half * 4 + j + 1) * 512)
            value = dot_t(part, rows[...])
            total[at, :] = before[at, :] + value if add else value


def first_square(where, keep_d, keep_s, before, own, other, panel, square, low, rows, row):
    x, y, core, z = where[0], where[1], where[2], where[3]
    row_block, col_block = (x * 4 + y) * 2, z * 8 + core * 4
    pick_rows(where, own, other, rows)
    for half, (part, kind) in enumerate(((own, core), (other, 1 - core))):
        for j in range(4):
            at = slice((half * 4 + j) * 512, (half * 4 + j + 1) * 512)
            value = before[at, :] + dot_t(part[j * 512:(j + 1) * 512, :], rows[...])
            for i in range(4):
                px, py = place(x, y, kind, i, j)
                block = px * 8 + py * 2 + kind
                for t in range(4):
                    keep = keep_d[0, block, col_block + t].astype(jnp.float32)
                    piece = value[i * B:(i + 1) * B, t * B:(t + 1) * B] * keep
                    panel[aligned(block, B), t * B:(t + 1) * B] = piece.astype(jnp.bfloat16)
                for t in range(2):
                    keep = keep_d[0, row_block + t, block].astype(jnp.float32)
                    piece = value[i * B:(i + 1) * B, COLS + t * B:COLS + (t + 1) * B] * keep
                    row[t * B:(t + 1) * B, aligned(block, B)] = piece.astype(jnp.bfloat16).T
    finish_square(dot(row[...], panel[...]), keep_s, 0, row_block, col_block, square, low)


def finish_square(value, keep_s, step, row_block, col_block, square, low):
    for t in range(2):
        for u in range(4):
            keep = keep_s[step, row_block + t, col_block + u].astype(jnp.float32)
            piece = value[t * B:(t + 1) * B, u * B:(u + 1) * B] * keep
            square[t * B:(t + 1) * B, u * B:(u + 1) * B] = piece
            low[t * B:(t + 1) * B, u * B:(u + 1) * B] = piece.astype(jnp.bfloat16)


def parts_times_panel(parts, core, z, panel):
    total = None
    for ref, d, half in parts:
        term = dot(ref[...], panel[aligned(((z + d) & 3) * 2 + half, COLS), :])
        total = term if total is None else total + term
    return total


def early_cube(where, *refs):
    own, other, panel, out = refs[:4], refs[4], refs[5], refs[6]
    core, z = where[2], where[3]
    parts = [(own[d], d, core) for d in range(4)] + [(other, 0, 1 - core)]
    out[...] = parts_times_panel(parts, core, z, panel)


def late_cube(where, others, early, panel):
    core, z = where[2], where[3]
    parts = [(others[d - 1], d, 1 - core) for d in (1, 2, 3)]
    return early[...] + parts_times_panel(parts, core, z, panel)


def first_density(where, keep_d, *refs):
    others, (early, square, panel, out) = refs[:3], refs[3:]
    x, y, core, z = where[0], where[1], where[2], where[3]
    value = 3.0 * square[...] - 2.0 * late_cube(where, others, early, panel)
    for t in range(2):
        for u in range(4):
            keep = keep_d[1, (x * 4 + y) * 2 + t, z * 8 + core * 4 + u].astype(jnp.float32)
            piece = value[t * B:(t + 1) * B, u * B:(u + 1) * B] * keep
            out[t * B:(t + 1) * B, u * B:(u + 1) * B] = piece.astype(jnp.bfloat16)


def chips_times(where, line, chips, panel, sems):
    x, y, core = where[0], where[1], where[2]
    copies, left, right = [], [], []
    for n, (ref, offset, first, second) in enumerate(chips):
        px, py = place(x, y, core, first, second)
        copies.append(pltpu.make_async_copy(
            ref.at[pl.ds(offset, ROWS)], panel.at[aligned(px * 4 + py, ROWS)], sems.at[n]))
        copies[-1].start()
        at = aligned(px * 2 + (py >> 1), ROWS)
        left.append(jnp.where(py & 1 == 0, line[at, :ROWS], line[at, ROWS:]))
        right.append(ref[offset:offset + ROWS, :])
    total = None
    for n in range(0, len(chips), 4):
        term = dot(jnp.concatenate(left[n:n + 4], axis=1), jnp.concatenate(right[n:n + 4], axis=0))
        total = term if total is None else total + term
    return total, copies


def early_square(where, *refs):
    own, other, near, far, (early, line, panel), (sems,) = (
        refs[:4], refs[4:8], refs[8], refs[9:13], refs[13:16], refs[16:])
    core, z = where[2], where[3]
    for d in range(4):
        line[aligned(((z + d) & 3) * 2 + core, ROWS), :] = own[d][...]
        line[aligned(((z + d) & 3) * 2 + 1 - core, ROWS), :] = other[d][...]
    chips = [(near, i * ROWS, i, 0) for i in range(4)] + [(far[i], 0, i, 2) for i in range(4)]
    value, copies = chips_times(where, line, chips, panel, sems)
    early[...] = value
    for copy in copies:
        copy.wait()


def second_square(where, keep_s, one, three, early, line, _, square, low, panel, sems):
    x, y, core, z = where[0], where[1], where[2], where[3]
    chips = [(ref, i * ROWS, i, j) for ref, j in ((one, 1), (three, 3)) for i in range(4)]
    value, copies = chips_times(where, line, chips, panel, sems)
    finish_square(early[...] + value, keep_s, 1, (x * 4 + y) * 2, z * 8 + core * 4, square, low)
    for copy in copies:
        copy.wait()


def second_density(where, *refs):
    others, (early, square, panel, stay, leave) = refs[:3], refs[3:]
    value = 3.0 * square[...] - 2.0 * late_cube(where, others, early, panel)
    first = where[2] == 0
    stay[...] = jnp.where(first, value[:B], value[B:])
    leave[...] = jnp.where(first, value[B:], value[:B])


SMEM = pl.BlockSpec(memory_space=pltpu.SMEM)
VMEM = pl.BlockSpec(memory_space=pltpu.VMEM)


def call(kernel, n_smem, ins, outs, scratch, flops, moved, aliases={}):
    return pl.pallas_call(
        kernel,
        in_specs=[SMEM] * n_smem + [VMEM] * (len(ins) - n_smem),
        out_specs=[VMEM] * len(outs),
        out_shape=outs,
        scratch_shapes=scratch,
        input_output_aliases=aliases,
        cost_estimate=pl.CostEstimate(flops=flops, bytes_accessed=moved, transcendentals=0),
        compiler_params=pltpu.CompilerParams(vmem_limit_bytes=12 * MIB),
    )(*ins)


def body(coeffs, coef_pattern, keep_density, keep_square):
    r, z = lax.axis_index("row"), lax.axis_index("col")
    x, y, core = r // 8, (r // 2) % 4, r % 2
    where = jnp.stack([x, y, core, z]).astype(jnp.int32)
    low_block = jax.ShapeDtypeStruct((ROWS, COLS), jnp.bfloat16)
    full_block = jax.ShapeDtypeStruct((ROWS, COLS), jnp.float32)
    panel_shape = jax.ShapeDtypeStruct((N, COLS), jnp.bfloat16)
    total_shape = jax.ShapeDtypeStruct((N, COLS + ROWS), jnp.float32)
    block_flops = 2 * ROWS * N * COLS
    density_flops = 2 * N * K * (COLS + ROWS)

    patterns = []
    for i in range(4):
        px, py = place(x, y, core, i, 0)
        patterns.append(lax.dynamic_slice(coef_pattern, (px * 8 + py * 2 + core, z * 2), (1, 2)))
    patterns = jnp.repeat(jnp.repeat(jnp.concatenate(patterns, axis=0), B, 0), B, 1).astype(jnp.bfloat16)
    line = jnp.concatenate(gather(coeffs, from_first), axis=0) * patterns
    kept = jnp.concatenate(gather(line, from_second), axis=0)
    own = gather(kept, from_z)
    other = [other_core(part) for part in own]

    (total,) = call(
        early_density, 1, [where, own[0], other[0]], [total_shape],
        [pltpu.VMEM((COLS + ROWS, DEPTH), jnp.bfloat16)], density_flops // 4, 14 * MIB)
    (total,) = call(
        early_density, 1, [where, total, own[1], other[1], own[3], other[3]], [total_shape],
        [pltpu.VMEM((COLS + ROWS, 2 * DEPTH), jnp.bfloat16)], density_flops // 2, 28 * MIB, {1: 0})
    panel, square, low = call(
        first_square, 3, [where, keep_density, keep_square, total, own[2], other[2]],
        [panel_shape, full_block, low_block],
        [pltpu.VMEM((COLS + ROWS, DEPTH), jnp.bfloat16), pltpu.VMEM((ROWS, N), jnp.bfloat16)],
        density_flops // 4 + block_flops, 19 * MIB)

    own = gather(low, from_z)
    other = [other_core(part) for part in own]
    (early,) = call(
        early_cube, 1, [where, *own, other[0], panel], [full_block], [], block_flops * 5 // 8, 4 * MIB)
    (current,) = call(
        first_density, 2, [where, keep_density, *other[1:], early, square, panel], [low_block], [],
        block_flops * 3 // 8, 3 * MIB)

    one, three, two, far = (
        from_first(current, 1), from_first(current, 3), from_first(current, 2), from_second(current, 2))
    start, one, three, two, far = lax.optimization_barrier((current, one, three, two, far))
    near = jnp.concatenate([start, one, two, three], axis=0)
    above, below = from_second(near, 1), from_second(near, 3)
    far = gather(far, from_first)
    own = gather(start, from_z)
    other = [other_core(part) for part in own]
    early, line, panel = call(
        early_square, 1, [where, *own, *other, near, *far],
        [full_block, jax.ShapeDtypeStruct((8 * ROWS, COLS), jnp.bfloat16), panel_shape],
        [pltpu.SemaphoreType.DMA((8,))], block_flops // 2, 10 * MIB)
    square, low, panel = call(
        second_square, 2, [where, keep_square, above, below, early, line, panel],
        [full_block, low_block, panel_shape],
        [pltpu.SemaphoreType.DMA((8,))], block_flops // 2, 8 * MIB, {6: 2})

    own = gather(low, from_z)
    other = [other_core(part) for part in own]
    (early,) = call(
        early_cube, 1, [where, *own, other[0], panel], [full_block], [], block_flops * 5 // 8, 4 * MIB)
    half = jax.ShapeDtypeStruct((B, COLS), jnp.float32)
    stay, leave = call(
        second_density, 1, [where, *other[1:], early, square, panel], [half, half], [],
        block_flops * 3 // 8, 3 * MIB)
    come = other_core(leave)
    first = core == 0
    return jnp.concatenate([jnp.where(first, stay, come), jnp.where(first, come, stay)], axis=1)


def solution(mesh):
    placed = (P("row", "col"), P(), P(), P())
    return jax.shard_map(
        body, mesh=mesh, in_specs=placed, out_specs=P("row", "col"), check_vma=False
    )
```

time: 164 us -> 178 us (1.085)
  starting transfers between devices: 53 us -> 79.1 us
  between operations: 13.6 us -> 0.28 us
  local copies, waits for them, and re-layouts: 5.68 us -> 0.82 us
  Pallas kernels: 20.6 us -> 24.1 us
    ppermute x13 -> x17, starting transfers between devices: 18.5 us -> 53.5 us  [other_core(): lax.ppermute(a, AXES, pairs(lambda x, y, core, z: (x, y, 1 - core, z)))]
    ppermute x9 -> x12, waiting for transfers between devices: 19.1 us -> 40.6 us  [from_z(): lax.ppermute(a, AXES, pairs(lambda x, y, core, z: (x, y, core, z - d)))]
    ppermute x12 -> x9, waiting for transfers between devices: 33 us -> 18.9 us  [from_first(): lax.ppermute(a, AXES, pairs(lambda x, y, core, z: (x - d, y, core, z) if...]
    ppermute x13 -> x17, waiting for transfers between devices: 7.93 us -> 2.62 us  [other_core(): lax.ppermute(a, AXES, pairs(lambda x, y, core, z: (x, y, 1 - core, z)))]
    unnamed x24 -> x7, local copies, waits for them, and re-layouts: 4.97 us -> 0.07 us
    ppermute x6, starting transfers between devices: 10.2 us -> 5.73 us  [from_second(): lax.ppermute(a, AXES, pairs(lambda x, y, core, z: (x, y - d, core, z) if...]
    ppermute x12 -> x9, starting transfers between devices: 12.4 us -> 8.01 us  [from_first(): lax.ppermute(a, AXES, pairs(lambda x, y, core, z: (x - d, y, core, z) if...]
    pallas_call x4 -> x9, Pallas kernels: 20.6 us -> 24.1 us  [call(): pl.pallas_call(kernel, in_specs=[SMEM] * n_smem + [VMEM] * (len(ins) - n_...]
  transfers between devices with their start and end apart: 41 -> 44, of which waited for: 27 -> 19; matrix products, arithmetic and copies ran while one was open for 1% -> 1% of each run, Pallas kernels for 0% -> 8%
where the time goes in v4:
time: 178 us
  starting transfers between devices  79.1 us (44%)
  waiting for transfers between devices  70.9 us (40%)
  Pallas kernels  24.1 us (14%)
  other arithmetic  2.91 us (2%)
    ppermute x17, starting transfers between devices, other_core(): lax.ppermute(a, AXES, pairs(lambda x, y, core, z: (x, y, 1 - core, z)))  53.5 us
    ppermute x12, waiting for transfers between devices, from_z(): lax.ppermute(a, AXES, pairs(lambda x, y, core, z: (x, y, core, z - d)))  40.6 us
    pallas_call x9, Pallas kernels, call(): pl.pallas_call(kernel, in_specs=[SMEM] * n_smem + [VMEM] * (len(ins) - n_...  24.1 us
    ppermute x9, waiting for transfers between devices, from_first(): lax.ppermute(a, AXES, pairs(lambda x, y, core, z: (x - d, y, core, z) if...  18.9 us
    ppermute x12, starting transfers between devices, from_z(): lax.ppermute(a, AXES, pairs(lambda x, y, core, z: (x, y, core, z - d)))  11.8 us
    ppermute x6, waiting for transfers between devices, from_second(): lax.ppermute(a, AXES, pairs(lambda x, y, core, z: (x, y - d, core, z) if...  8.71 us
    ppermute x9, starting transfers between devices, from_first(): lax.ppermute(a, AXES, pairs(lambda x, y, core, z: (x - d, y, core, z) if...  8.01 us
    ppermute x6, starting transfers between devices, from_second(): lax.ppermute(a, AXES, pairs(lambda x, y, core, z: (x, y - d, core, z) if...  5.73 us
  transfers between devices with their start and end apart: 44, of which 19 were waited for; matrix products, arithmetic and copies ran while one was open for 1% of the time, Pallas kernels for 8%

profile of v4, /device:TPU:1, one launch (start us, length us, event | category | flops | bytes accessed | tf_op | source)
XLA Modules:
  0.0 178.0 jit_solution(4502869694273899641)
XLA Ops:
  0.0 3.6 %collective-permute-start = (bf16[128,256]{1,0:T(8,128)(2,1)}, bf16[128,256]{1,0:T(8,128)(2,1)S(1)}, u32[]{:S(2)}, u32[]{:S(2)}) collective-permute-start(bf16[128,256]{1,0:T(8,128)(2,1)} %param.4), channel_id=1, source_target_pairs={{0,96},{1,97},{2,98},{3,99},{4,28},{5,29},{6,30},{7,31},{8,104},{9... | collective-permute-start | bytes 196616 | tf_op jit(solution)/shard_map/ppermute | solution.py:38
  5.7 2.8 %collective-permute-done.1 = bf16[128,256]{1,0:T(8,128)(2,1)S(1)} collective-permute-done((bf16[128,256]{1,0:T(8,128)(2,1)}, bf16[128,256]{1,0:T(8,128)(2,1)S(1)}, u32[]{:S(2)}, u32[]{:S(2)}) %collective-permute-start.1) | collective-permute-done | bytes 65568 | tf_op jit(solution)/shard_map/ppermute | solution.py:38
  10.9 2.3 %collective-permute-start.3 = (bf16[512,256]{1,0:T(8,128)(2,1)S(1)}, bf16[512,256]{1,0:T(8,128)(2,1)S(1)}, u32[]{:S(2)}, u32[]{:S(2)}) collective-permute-start(bf16[512,256]{1,0:T(8,128)(2,1)S(1)} %bitcast_multiply_fusion), channel_id=1, source_target_pairs={{0,24},{1,25},{2,26},{3,27},{4,100},{5,101},{6,102},{7,103},{8,0},... | collective-permute-start | bytes 786440 | tf_op jit(solution)/shard_map/ppermute | solution.py:43
  14.3 5.0 %collective-permute-done.3 = bf16[512,256]{1,0:T(8,128)(2,1)S(1)} collective-permute-done((bf16[512,256]{1,0:T(8,128)(2,1)S(1)}, bf16[512,256]{1,0:T(8,128)(2,1)S(1)}, u32[]{:S(2)}, u32[]{:S(2)}) %collective-permute-start.3) | collective-permute-done | bytes 262176 | tf_op jit(solution)/shard_map/ppermute | solution.py:43
  19.3 0.9 collective-permute-done.4
  20.3 2.8 %collective-permute-done.5 = bf16[512,256]{1,0:T(8,128)(2,1)S(1)} collective-permute-done((bf16[512,256]{1,0:T(8,128)(2,1)S(1)}, bf16[512,256]{1,0:T(8,128)(2,1)S(1)}, u32[]{:S(2)}, u32[]{:S(2)}) %collective-permute-start.5) | collective-permute-done | bytes 262176 | tf_op jit(solution)/shard_map/ppermute | solution.py:43
  23.1 1.7 collective-permute-start.9
  24.8 2.2 %collective-permute-start.7 = (bf16[2048,256]{1,0:T(8,128)(2,1)S(1)}, bf16[2048,256]{1,0:T(8,128)(2,1)S(1)}, u32[]{:S(2)}, u32[]{:S(2)}) collective-permute-start(bf16[2048,256]{1,0:T(8,128)(2,1)S(1)} %pad_maximum_fusion.refs_0_), channel_id=1, source_target_pairs={{0,3},{1,0},{2,1},{3,2},{4,7},{5,4},{6,5},{7,6},{8,11},{9,8},{10,9... | collective-permute-start | bytes 3145736 | tf_op jit(solution)/shard_map/ppermute | solution.py:34
  27.0 1.2 collective-permute-start.11
  28.2 4.1 %collective-permute-start.6 = (bf16[2048,256]{1,0:T(8,128)(2,1)S(1)}, bf16[2048,256]{1,0:T(8,128)(2,1)S(1)}, u32[]{:S(2)}, u32[]{:S(2)}) collective-permute-start(bf16[2048,256]{1,0:T(8,128)(2,1)S(1)} %pad_maximum_fusion.refs_0_), channel_id=1, source_target_pairs={{0,4},{1,5},{2,6},{3,7},{4,0},{5,1},{6,2},{7,3},{8,12},{9,13},{10,... | collective-permute-start | bytes 3145736 | tf_op jit(solution)/shard_map/ppermute | solution.py:30
  32.3 14.8 %collective-permute-done.9.refs_3_ = bf16[2048,256]{1,0:T(8,128)(2,1)S(1)} collective-permute-done((bf16[2048,256]{1,0:T(8,128)(2,1)S(1)}, bf16[2048,256]{1,0:T(8,128)(2,1)S(1)}, u32[]{:S(2)}, u32[]{:S(2)}) %collective-permute-start.9) | collective-permute-done | bytes 1048608 | tf_op jit(solution)/shard_map/ppermute | solution.py:34
  47.1 6.5 %collective-permute-start.10 = (bf16[2048,256]{1,0:T(8,128)(2,1)S(1)}, bf16[2048,256]{1,0:T(8,128)(2,1)S(1)}, u32[]{:S(2)}, u32[]{:S(2)}) collective-permute-start(bf16[2048,256]{1,0:T(8,128)(2,1)S(1)} %collective-permute-done.9.refs_3_), channel_id=1, source_target_pairs={{0,4},{1,5},{2,6},{3,7},{4,0},{5,1},{6,2},{7,3},{8,12},{9,13},{10,... | collective-permute-start | bytes 3145736 | tf_op jit(solution)/shard_map/ppermute | solution.py:30
  53.6 19.3 %collective-permute-start.8 = (bf16[2048,256]{1,0:T(8,128)(2,1)S(1)}, bf16[2048,256]{1,0:T(8,128)(2,1)S(1)}, u32[]{:S(2)}, u32[]{:S(2)}) collective-permute-start(bf16[2048,256]{1,0:T(8,128)(2,1)S(1)} %collective-permute-done.7.refs_1_), channel_id=1, source_target_pairs={{0,4},{1,5},{2,6},{3,7},{4,0},{5,1},{6,2},{7,3},{8,12},{9,13},{10,... | collective-permute-start | bytes 3145736 | tf_op jit(solution)/shard_map/ppermute | solution.py:30
  72.9 1.8 %collective-permute-start.12 = (bf16[2048,256]{1,0:T(8,128)(2,1)S(1)}, bf16[2048,256]{1,0:T(8,128)(2,1)S(1)}, u32[]{:S(2)}, u32[]{:S(2)}) collective-permute-start(bf16[2048,256]{1,0:T(8,128)(2,1)S(1)} %collective-permute-done.11.own), channel_id=1, source_target_pairs={{0,4},{1,5},{2,6},{3,7},{4,0},{5,1},{6,2},{7,3},{8,12},{9,13},{10,... | collective-permute-start | bytes 3145736 | tf_op jit(solution)/shard_map/ppermute | solution.py:30
  74.8 2.4 %shard_map.46.refs_0_ = f32[4096,768]{1,0:T(8,128)S(1)} custom-call(s32[4]{0:T(128)S(1)} %pad_add_fusion.where, bf16[2048,256]{1,0:T(8,128)(2,1)S(1)} %pad_maximum_fusion.refs_0_, bf16[2048,256]{1,0:T(8,128)(2,1)S(1)} %collective-permute-done.6.refs_1_), custom_call_target="tpu_custom_call" | custom-call | flops 1610612736 | bytes 14680064 | tf_op jit(solution)/shard_map/pallas_call | solution.py:216
  77.2 6.5 %shard_map.47.before = f32[4096,768]{1,0:T(8,128)S(1)} custom-call(s32[4]{0:T(128)S(1)} %pad_add_fusion.where, f32[4096,768]{1,0:T(8,128)S(1)} %shard_map.46.refs_0_, bf16[2048,256]{1,0:T(8,128)(2,1)S(1)} %collective-permute-done.7.refs_1_, bf16[2048,256]{1,0:T(8,128)(2,1)S(1)} %collective-permute-done.8.refs_2_, ...), custom_call_target="tpu_custom_call", output_to_operand_aliasing={{}: (1, {})} | custom-call | flops 3221225472 | bytes 29360128 | tf_op jit(solution)/shard_map/pallas_call | solution.py:216
  83.7 5.5 %shard_map.48 = (bf16[4096,512]{1,0:T(8,128)(2,1)S(1)}, f32[256,512]{1,0:T(8,128)S(1)}, bf16[256,512]{1,0:T(8,128)(2,1)S(1)}) custom-call(s32[4]{0:T(128)S(1)} %pad_add_fusion.where, s32[2,32,32]{2,1,0:T(8,128)S(1)} %copy-done, s32[2,32,32]{2,1,0:T(8,128)S(1)} %copy-done.1, f32[4096,768]{1,0:T(8,128)S(1)} %shard_map.47.before, ...), custom_call_target="tpu_custom_call" | custom-call | flops 2684354560 | bytes 19922944 | tf_op jit(solution)/shard_map/pallas_call | solution.py:216
  89.2 1.7 collective-permute-start.13
  90.9 1.1 collective-permute-start.15
  92.7 4.6 %collective-permute-done.13.refs_1_ = bf16[256,512]{1,0:T(8,128)(2,1)S(1)} collective-permute-done((bf16[256,512]{1,0:T(8,128)(2,1)S(1)}, bf16[256,512]{1,0:T(8,128)(2,1)S(1)}, u32[]{:S(2)}, u32[]{:S(2)}) %collective-permute-start.13) | collective-permute-done | bytes 262176 | tf_op jit(solution)/shard_map/ppermute | solution.py:34
  97.3 5.8 %collective-permute-start.14 = (bf16[256,512]{1,0:T(8,128)(2,1)S(1)}, bf16[256,512]{1,0:T(8,128)(2,1)S(1)}, u32[]{:S(2)}, u32[]{:S(2)}) collective-permute-start(bf16[256,512]{1,0:T(8,128)(2,1)S(1)} %collective-permute-done.13.refs_1_), channel_id=1, source_target_pairs={{0,4},{1,5},{2,6},{3,7},{4,0},{5,1},{6,2},{7,3},{8,12},{9,13},{10,... | collective-permute-start | bytes 786440 | tf_op jit(solution)/shard_map/ppermute | solution.py:30
  103.1 3.2 %collective-permute-done.17.refs_3_ = bf16[256,512]{1,0:T(8,128)(2,1)S(1)} collective-permute-done((bf16[256,512]{1,0:T(8,128)(2,1)S(1)}, bf16[256,512]{1,0:T(8,128)(2,1)S(1)}, u32[]{:S(2)}, u32[]{:S(2)}) %collective-permute-start.17) | collective-permute-done | bytes 262176 | tf_op jit(solution)/shard_map/ppermute | solution.py:34
  106.7 1.4 shard_map.49.refs_3_
  108.1 1.7 shard_map.50.refs_0_
  113.0 2.5 %collective-permute-done.20 = bf16[256,512]{1,0:T(8,128)(2,1)S(1)} collective-permute-done((bf16[256,512]{1,0:T(8,128)(2,1)S(1)}, bf16[256,512]{1,0:T(8,128)(2,1)S(1)}, u32[]{:S(2)}, u32[]{:S(2)}) %collective-permute-start.20) | collective-permute-done | bytes 262176 | tf_op jit(solution)/shard_map/ppermute | solution.py:38
  115.4 7.4 %collective-permute-done.21 = bf16[256,512]{1,0:T(8,128)(2,1)S(1)} collective-permute-done((bf16[256,512]{1,0:T(8,128)(2,1)S(1)}, bf16[256,512]{1,0:T(8,128)(2,1)S(1)}, u32[]{:S(2)}, u32[]{:S(2)}) %collective-permute-start.21) | collective-permute-done | bytes 262176 | tf_op jit(solution)/shard_map/ppermute | solution.py:38
  123.7 1.1 collective-permute-start.25
  124.8 1.1 collective-permute-start.27
  126.4 3.2 %collective-permute-done.26.refs_1_ = bf16[256,512]{1,0:T(8,128)(2,1)S(1)} collective-permute-done((bf16[256,512]{1,0:T(8,128)(2,1)S(1)}, bf16[256,512]{1,0:T(8,128)(2,1)S(1)}, u32[]{:S(2)}, u32[]{:S(2)}) %collective-permute-start.26) | collective-permute-done | bytes 262176 | tf_op jit(solution)/shard_map/ppermute | solution.py:34
  129.7 3.5 %collective-permute-start.29 = (bf16[256,512]{1,0:T(8,128)(2,1)S(1)}, bf16[256,512]{1,0:T(8,128)(2,1)S(1)}, u32[]{:S(2)}, u32[]{:S(2)}) collective-permute-start(bf16[256,512]{1,0:T(8,128)(2,1)S(1)} %shard_map.50.refs_0_), channel_id=1, source_target_pairs={{0,4},{1,5},{2,6},{3,7},{4,0},{5,1},{6,2},{7,3},{8,12},{9,13},{10,... | collective-permute-start | bytes 786440 | tf_op jit(solution)/shard_map/ppermute | solution.py:30
  133.7 6.4 %collective-permute-done.28.refs_3_ = bf16[256,512]{1,0:T(8,128)(2,1)S(1)} collective-permute-done((bf16[256,512]{1,0:T(8,128)(2,1)S(1)}, bf16[256,512]{1,0:T(8,128)(2,1)S(1)}, u32[]{:S(2)}, u32[]{:S(2)}) %collective-permute-start.28) | collective-permute-done | bytes 262176 | tf_op jit(solution)/shard_map/ppermute | solution.py:34
  141.6 2.4 %collective-permute-start.30 = (bf16[256,512]{1,0:T(8,128)(2,1)S(1)}, bf16[256,512]{1,0:T(8,128)(2,1)S(1)}, u32[]{:S(2)}, u32[]{:S(2)}) collective-permute-start(bf16[256,512]{1,0:T(8,128)(2,1)S(1)} %collective-permute-done.26.refs_1_), channel_id=1, source_target_pairs={{0,4},{1,5},{2,6},{3,7},{4,0},{5,1},{6,2},{7,3},{8,12},{9,13},{10,... | collective-permute-start | bytes 786440 | tf_op jit(solution)/shard_map/ppermute | solution.py:30
  144.0 3.2 %collective-permute-done.34.refs_11_ = bf16[256,512]{1,0:T(8,128)(2,1)S(1)} collective-permute-done((bf16[256,512]{1,0:T(8,128)(2,1)S(1)}, bf16[256,512]{1,0:T(8,128)(2,1)S(1)}, u32[]{:S(2)}, u32[]{:S(2)}) %collective-permute-start.34) | collective-permute-done | bytes 262176 | tf_op jit(solution)/shard_map/ppermute | solution.py:38
  147.2 1.5 collective-permute-start.31
  148.7 1.3 collective-permute-done.35.refs_12_
  150.0 1.4 collective-permute-start.32
  151.4 1.2 collective-permute-done.32.refs_7_
  152.5 1.8 %shard_map.51 = (f32[256,512]{1,0:T(8,128)S(1)}, bf16[2048,512]{1,0:T(8,128)(2,1)S(1)}, bf16[4096,512]{1,0:T(8,128)(2,1)S(1)}) custom-call(s32[4]{0:T(128)S(1)} %pad_add_fusion.where, bf16[256,512]{1,0:T(8,128)(2,1)S(1)} %shard_map.50.refs_0_, bf16[256,512]{1,0:T(8,128)(2,1)S(1)} %collective-permute-done.26.refs_1_, ...), custom_call_target="tpu_custom_call" | custom-call | flops 536870912 | bytes 10485760 | tf_op jit(solution)/shard_map/pallas_call | solution.py:216
  154.4 2.2 %shard_map.52 = (f32[256,512]{1,0:T(8,128)S(1)}, bf16[256,512]{1,0:T(8,128)(2,1)S(1)}, bf16[4096,512]{1,0:T(8,128)(2,1)S(1)}) custom-call(s32[4]{0:T(128)S(1)} %pad_add_fusion.where, s32[2,32,32]{2,1,0:T(8,128)S(1)} %copy-done.1, bf16[1024,512]{1,0:T(8,128)(2,1)S(1)} %collective-permute-done.24.one, ...), custom_call_target="tpu_custom_call", output_to_operand_aliasing={{2}: (6, {})} | custom-call | flops 536870912 | bytes 8388608 | tf_op jit(solution)/shard_map/pallas_call | solution.py:216
  157.1 1.1 collective-permute-start.38
  158.7 1.2 collective-permute-start.42
  159.9 4.4 %collective-permute-done.36.refs_1_ = bf16[256,512]{1,0:T(8,128)(2,1)S(1)} collective-permute-done((bf16[256,512]{1,0:T(8,128)(2,1)S(1)}, bf16[256,512]{1,0:T(8,128)(2,1)S(1)}, u32[]{:S(2)}, u32[]{:S(2)}) %collective-permute-start.36) | collective-permute-done | bytes 262176 | tf_op jit(solution)/shard_map/ppermute | solution.py:34
  164.2 2.0 %collective-permute-start.37 = (bf16[256,512]{1,0:T(8,128)(2,1)S(1)}, bf16[256,512]{1,0:T(8,128)(2,1)S(1)}, u32[]{:S(2)}, u32[]{:S(2)}) collective-permute-start(bf16[256,512]{1,0:T(8,128)(2,1)S(1)} %collective-permute-done.36.refs_1_), channel_id=1, source_target_pairs={{0,4},{1,5},{2,6},{3,7},{4,0},{5,1},{6,2},{7,3},{8,12},{9,13},{10,... | collective-permute-start | bytes 786440 | tf_op jit(solution)/shard_map/ppermute | solution.py:30
  166.3 2.2 %collective-permute-start.39 = (bf16[256,512]{1,0:T(8,128)(2,1)S(1)}, bf16[256,512]{1,0:T(8,128)(2,1)S(1)}, u32[]{:S(2)}, u32[]{:S(2)}) collective-permute-start(bf16[256,512]{1,0:T(8,128)(2,1)S(1)} %collective-permute-done.38.refs_2_), channel_id=1, source_target_pairs={{0,4},{1,5},{2,6},{3,7},{4,0},{5,1},{6,2},{7,3},{8,12},{9,13},{10,... | collective-permute-start | bytes 786440 | tf_op jit(solution)/shard_map/ppermute | solution.py:30
  168.4 4.0 %collective-permute-done.40.refs_3_ = bf16[256,512]{1,0:T(8,128)(2,1)S(1)} collective-permute-done((bf16[256,512]{1,0:T(8,128)(2,1)S(1)}, bf16[256,512]{1,0:T(8,128)(2,1)S(1)}, u32[]{:S(2)}, u32[]{:S(2)}) %collective-permute-start.40) | collective-permute-done | bytes 262176 | tf_op jit(solution)/shard_map/ppermute | solution.py:34
  172.9 1.4 shard_map.53.refs_3_
  174.3 1.2 shard_map.54
  175.7 1.4 collective-permute-done.43
  (67 shorter events, 16.2 us)
Async XLA Ops:
  0.0 5.7 %collective-permute-start = (bf16[128,256]{1,0:T(8,128)(2,1)}, bf16[128,256]{1,0:T(8,128)(2,1)S(1)}, u32[]{:S(2)}, u32[]{:S(2)}) collective-permute-start(bf16[128,256]{1,0:T(8,128)(2,1)} %param.4), channel_id=1, source_target_pairs={{0,96},{1,97},{2,98},{3,99},{4,28},{5,29},{6,30},{7,31},{8,104},{9... | collective-permute-start | bytes 196616 | tf_op jit(solution)/shard_map/ppermute | solution.py:38
  3.6 4.9 %collective-permute-start.1 = (bf16[128,256]{1,0:T(8,128)(2,1)}, bf16[128,256]{1,0:T(8,128)(2,1)S(1)}, u32[]{:S(2)}, u32[]{:S(2)}) collective-permute-start(bf16[128,256]{1,0:T(8,128)(2,1)} %param.4), channel_id=1, source_target_pairs={{0,64},{1,65},{2,66},{3,67},{4,20},{5,21},{6,22},{7,23},{8,72},{9,... | collective-permute-start | bytes 196616 | tf_op jit(solution)/shard_map/ppermute | solution.py:38
  3.9 5.5 %collective-permute-start.2 = (bf16[128,256]{1,0:T(8,128)(2,1)}, bf16[128,256]{1,0:T(8,128)(2,1)S(1)}, u32[]{:S(2)}, u32[]{:S(2)}) collective-permute-start(bf16[128,256]{1,0:T(8,128)(2,1)} %param.4), channel_id=1, source_target_pairs={{0,32},{1,33},{2,34},{3,35},{4,12},{5,13},{6,14},{7,15},{8,40},{9,... | collective-permute-start | bytes 196616 | tf_op jit(solution)/shard_map/ppermute | solution.py:38
  10.9 8.4 %collective-permute-start.3 = (bf16[512,256]{1,0:T(8,128)(2,1)S(1)}, bf16[512,256]{1,0:T(8,128)(2,1)S(1)}, u32[]{:S(2)}, u32[]{:S(2)}) collective-permute-start(bf16[512,256]{1,0:T(8,128)(2,1)S(1)} %bitcast_multiply_fusion), channel_id=1, source_target_pairs={{0,24},{1,25},{2,26},{3,27},{4,100},{5,101},{6,102},{7,103},{8,0},... | collective-permute-start | bytes 786440 | tf_op jit(solution)/shard_map/ppermute | solution.py:43
  13.2 7.1 %collective-permute-start.4 = (bf16[512,256]{1,0:T(8,128)(2,1)S(1)}, bf16[512,256]{1,0:T(8,128)(2,1)S(1)}, u32[]{:S(2)}, u32[]{:S(2)}) collective-permute-start(bf16[512,256]{1,0:T(8,128)(2,1)S(1)} %bitcast_multiply_fusion), channel_id=1, source_target_pairs={{0,16},{1,17},{2,18},{3,19},{4,68},{5,69},{6,70},{7,71},{8,24},{9,... | collective-permute-start | bytes 786440 | tf_op jit(solution)/shard_map/ppermute | solution.py:43
  13.7 9.3 %collective-permute-start.5 = (bf16[512,256]{1,0:T(8,128)(2,1)S(1)}, bf16[512,256]{1,0:T(8,128)(2,1)S(1)}, u32[]{:S(2)}, u32[]{:S(2)}) collective-permute-start(bf16[512,256]{1,0:T(8,128)(2,1)S(1)} %bitcast_multiply_fusion), channel_id=1, source_target_pairs={{0,8},{1,9},{2,10},{3,11},{4,36},{5,37},{6,38},{7,39},{8,16},{9,17... | collective-permute-start | bytes 786440 | tf_op jit(solution)/shard_map/ppermute | solution.py:43
  23.1 24.1 %collective-permute-start.9 = (bf16[2048,256]{1,0:T(8,128)(2,1)S(1)}, bf16[2048,256]{1,0:T(8,128)(2,1)S(1)}, u32[]{:S(2)}, u32[]{:S(2)}) collective-permute-start(bf16[2048,256]{1,0:T(8,128)(2,1)S(1)} %pad_maximum_fusion.refs_0_), channel_id=1, source_target_pairs={{0,1},{1,2},{2,3},{3,0},{4,5},{5,6},{6,7},{7,4},{8,9},{9,10},{10,1... | collective-permute-start | bytes 3145736 | tf_op jit(solution)/shard_map/ppermute | solution.py:34
  24.8 28.8 %collective-permute-start.7 = (bf16[2048,256]{1,0:T(8,128)(2,1)S(1)}, bf16[2048,256]{1,0:T(8,128)(2,1)S(1)}, u32[]{:S(2)}, u32[]{:S(2)}) collective-permute-start(bf16[2048,256]{1,0:T(8,128)(2,1)S(1)} %pad_maximum_fusion.refs_0_), channel_id=1, source_target_pairs={{0,3},{1,0},{2,1},{3,2},{4,7},{5,4},{6,5},{7,6},{8,11},{9,8},{10,9... | collective-permute-start | bytes 3145736 | tf_op jit(solution)/shard_map/ppermute | solution.py:34
  27.0 45.9 %collective-permute-start.11 = (bf16[2048,256]{1,0:T(8,128)(2,1)S(1)}, bf16[2048,256]{1,0:T(8,128)(2,1)S(1)}, u32[]{:S(2)}, u32[]{:S(2)}) collective-permute-start(bf16[2048,256]{1,0:T(8,128)(2,1)S(1)} %pad_maximum_fusion.refs_0_), channel_id=1, source_target_pairs={{0,2},{1,3},{2,0},{3,1},{4,6},{5,7},{6,4},{7,5},{8,10},{9,11},{10,... | collective-permute-start | bytes 3145736 | tf_op jit(solution)/shard_map/ppermute | solution.py:34
  28.2 46.5 %collective-permute-start.6 = (bf16[2048,256]{1,0:T(8,128)(2,1)S(1)}, bf16[2048,256]{1,0:T(8,128)(2,1)S(1)}, u32[]{:S(2)}, u32[]{:S(2)}) collective-permute-start(bf16[2048,256]{1,0:T(8,128)(2,1)S(1)} %pad_maximum_fusion.refs_0_), channel_id=1, source_target_pairs={{0,4},{1,5},{2,6},{3,7},{4,0},{5,1},{6,2},{7,3},{8,12},{9,13},{10,... | collective-permute-start | bytes 3145736 | tf_op jit(solution)/shard_map/ppermute | solution.py:30
  47.1 30.0 %collective-permute-start.10 = (bf16[2048,256]{1,0:T(8,128)(2,1)S(1)}, bf16[2048,256]{1,0:T(8,128)(2,1)S(1)}, u32[]{:S(2)}, u32[]{:S(2)}) collective-permute-start(bf16[2048,256]{1,0:T(8,128)(2,1)S(1)} %collective-permute-done.9.refs_3_), channel_id=1, source_target_pairs={{0,4},{1,5},{2,6},{3,7},{4,0},{5,1},{6,2},{7,3},{8,12},{9,13},{10,... | collective-permute-start | bytes 3145736 | tf_op jit(solution)/shard_map/ppermute | solution.py:30
  53.6 23.6 %collective-permute-start.8 = (bf16[2048,256]{1,0:T(8,128)(2,1)S(1)}, bf16[2048,256]{1,0:T(8,128)(2,1)S(1)}, u32[]{:S(2)}, u32[]{:S(2)}) collective-permute-start(bf16[2048,256]{1,0:T(8,128)(2,1)S(1)} %collective-permute-done.7.refs_1_), channel_id=1, source_target_pairs={{0,4},{1,5},{2,6},{3,7},{4,0},{5,1},{6,2},{7,3},{8,12},{9,13},{10,... | collective-permute-start | bytes 3145736 | tf_op jit(solution)/shard_map/ppermute | solution.py:30
  72.9 10.8 %collective-permute-start.12 = (bf16[2048,256]{1,0:T(8,128)(2,1)S(1)}, bf16[2048,256]{1,0:T(8,128)(2,1)S(1)}, u32[]{:S(2)}, u32[]{:S(2)}) collective-permute-start(bf16[2048,256]{1,0:T(8,128)(2,1)S(1)} %collective-permute-done.11.own), channel_id=1, source_target_pairs={{0,4},{1,5},{2,6},{3,7},{4,0},{5,1},{6,2},{7,3},{8,12},{9,13},{10,... | collective-permute-start | bytes 3145736 | tf_op jit(solution)/shard_map/ppermute | solution.py:30
  77.2 6.5 %copy-start = (s32[2,32,32]{2,1,0:T(8,128)S(1)}, s32[2,32,32]{2,1,0:T(8,128)}, u32[]{:S(2)}) copy-start(s32[2,32,32]{2,1,0:T(8,128)} %keep_d.3) | copy-start | bytes 24580
  77.2 6.5 %copy-start.1 = (s32[2,32,32]{2,1,0:T(8,128)S(1)}, s32[2,32,32]{2,1,0:T(8,128)}, u32[]{:S(2)}) copy-start(s32[2,32,32]{2,1,0:T(8,128)} %keep_s.3) | copy-start | bytes 24580
  89.2 8.0 %collective-permute-start.13 = (bf16[256,512]{1,0:T(8,128)(2,1)S(1)}, bf16[256,512]{1,0:T(8,128)(2,1)S(1)}, u32[]{:S(2)}, u32[]{:S(2)}) collective-permute-start(bf16[256,512]{1,0:T(8,128)(2,1)S(1)} %get-tuple-element.21.refs_0_), channel_id=1, source_target_pairs={{0,3},{1,0},{2,1},{3,2},{4,7},{5,4},{6,5},{7,6},{8,11},{9,8},{10,9... | collective-permute-start | bytes 786440 | tf_op jit(solution)/shard_map/ppermute | solution.py:34
  90.9 12.2 %collective-permute-start.15 = (bf16[256,512]{1,0:T(8,128)(2,1)S(1)}, bf16[256,512]{1,0:T(8,128)(2,1)S(1)}, u32[]{:S(2)}, u32[]{:S(2)}) collective-permute-start(bf16[256,512]{1,0:T(8,128)(2,1)S(1)} %get-tuple-element.21.refs_0_), channel_id=1, source_target_pairs={{0,2},{1,3},{2,0},{3,1},{4,6},{5,7},{6,4},{7,5},{8,10},{9,11},{10,... | collective-permute-start | bytes 786440 | tf_op jit(solution)/shard_map/ppermute | solution.py:34
  91.9 14.3 %collective-permute-start.17 = (bf16[256,512]{1,0:T(8,128)(2,1)S(1)}, bf16[256,512]{1,0:T(8,128)(2,1)S(1)}, u32[]{:S(2)}, u32[]{:S(2)}) collective-permute-start(bf16[256,512]{1,0:T(8,128)(2,1)S(1)} %get-tuple-element.21.refs_0_), channel_id=1, source_target_pairs={{0,1},{1,2},{2,3},{3,0},{4,5},{5,6},{6,7},{7,4},{8,9},{9,10},{10,1... | collective-permute-start | bytes 786440 | tf_op jit(solution)/shard_map/ppermute | solution.py:34
  91.9 14.8 %collective-permute-start.19 = (bf16[256,512]{1,0:T(8,128)(2,1)S(1)}, bf16[256,512]{1,0:T(8,128)(2,1)S(1)}, u32[]{:S(2)}, u32[]{:S(2)}) collective-permute-start(bf16[256,512]{1,0:T(8,128)(2,1)S(1)} %get-tuple-element.21.refs_0_), channel_id=1, source_target_pairs={{0,4},{1,5},{2,6},{3,7},{4,0},{5,1},{6,2},{7,3},{8,12},{9,13},{10,... | collective-permute-start | bytes 786440 | tf_op jit(solution)/shard_map/ppermute | solution.py:30
  97.3 10.8 %collective-permute-start.14 = (bf16[256,512]{1,0:T(8,128)(2,1)S(1)}, bf16[256,512]{1,0:T(8,128)(2,1)S(1)}, u32[]{:S(2)}, u32[]{:S(2)}) collective-permute-start(bf16[256,512]{1,0:T(8,128)(2,1)S(1)} %collective-permute-done.13.refs_1_), channel_id=1, source_target_pairs={{0,4},{1,5},{2,6},{3,7},{4,0},{5,1},{6,2},{7,3},{8,12},{9,13},{10,... | collective-permute-start | bytes 786440 | tf_op jit(solution)/shard_map/ppermute | solution.py:30
  103.1 5.1 %collective-permute-start.16 = (bf16[256,512]{1,0:T(8,128)(2,1)S(1)}, bf16[256,512]{1,0:T(8,128)(2,1)S(1)}, u32[]{:S(2)}, u32[]{:S(2)}) collective-permute-start(bf16[256,512]{1,0:T(8,128)(2,1)S(1)} %collective-permute-done.15.refs_2_), channel_id=1, source_target_pairs={{0,4},{1,5},{2,6},{3,7},{4,0},{5,1},{6,2},{7,3},{8,12},{9,13},{10,... | collective-permute-start | bytes 786440 | tf_op jit(solution)/shard_map/ppermute | solution.py:30
  106.2 1.9 %collective-permute-start.18 = (bf16[256,512]{1,0:T(8,128)(2,1)S(1)}, bf16[256,512]{1,0:T(8,128)(2,1)S(1)}, u32[]{:S(2)}, u32[]{:S(2)}) collective-permute-start(bf16[256,512]{1,0:T(8,128)(2,1)S(1)} %collective-permute-done.17.refs_3_), channel_id=1, source_target_pairs={{0,4},{1,5},{2,6},{3,7},{4,0},{5,1},{6,2},{7,3},{8,12},{9,13},{10,... | collective-permute-start | bytes 786440 | tf_op jit(solution)/shard_map/ppermute | solution.py:30
  109.8 5.6 %collective-permute-start.20 = (bf16[256,512]{1,0:T(8,128)(2,1)S(1)}, bf16[256,512]{1,0:T(8,128)(2,1)S(1)}, u32[]{:S(2)}, u32[]{:S(2)}) collective-permute-start(bf16[256,512]{1,0:T(8,128)(2,1)S(1)} %shard_map.50.refs_0_), channel_id=1, source_target_pairs={{0,96},{1,97},{2,98},{3,99},{4,28},{5,29},{6,30},{7,31},{8,104},{9... | collective-permute-start | bytes 786440 | tf_op jit(solution)/shard_map/ppermute | solution.py:38
  110.5 12.3 %collective-permute-start.21 = (bf16[256,512]{1,0:T(8,128)(2,1)S(1)}, bf16[256,512]{1,0:T(8,128)(2,1)S(1)}, u32[]{:S(2)}, u32[]{:S(2)}) collective-permute-start(bf16[256,512]{1,0:T(8,128)(2,1)S(1)} %shard_map.50.refs_0_), channel_id=1, source_target_pairs={{0,32},{1,33},{2,34},{3,35},{4,12},{5,13},{6,14},{7,15},{8,40},{9,... | collective-permute-start | bytes 786440 | tf_op jit(solution)/shard_map/ppermute | solution.py:38
  111.4 11.4 %collective-permute-start.22 = (bf16[256,512]{1,0:T(8,128)(2,1)S(1)}, bf16[256,512]{1,0:T(8,128)(2,1)S(1)}, u32[]{:S(2)}, u32[]{:S(2)}) collective-permute-start(bf16[256,512]{1,0:T(8,128)(2,1)S(1)} %shard_map.50.refs_0_), channel_id=1, source_target_pairs={{0,64},{1,65},{2,66},{3,67},{4,20},{5,21},{6,22},{7,23},{8,72},{9,... | collective-permute-start | bytes 786440 | tf_op jit(solution)/shard_map/ppermute | solution.py:38
  112.1 10.7 %collective-permute-start.23 = (bf16[256,512]{1,0:T(8,128)(2,1)S(1)}, bf16[256,512]{1,0:T(8,128)(2,1)S(1)}, u32[]{:S(2)}, u32[]{:S(2)}) collective-permute-start(bf16[256,512]{1,0:T(8,128)(2,1)S(1)} %shard_map.50.refs_0_), channel_id=1, source_target_pairs={{0,16},{1,17},{2,18},{3,19},{4,68},{5,69},{6,70},{7,71},{8,24},{9,... | collective-permute-start | bytes 786440 | tf_op jit(solution)/shard_map/ppermute | solution.py:43
  122.8 6.9 %collective-permute-start.26 = (bf16[256,512]{1,0:T(8,128)(2,1)S(1)}, bf16[256,512]{1,0:T(8,128)(2,1)S(1)}, u32[]{:S(2)}, u32[]{:S(2)}) collective-permute-start(bf16[256,512]{1,0:T(8,128)(2,1)S(1)} %shard_map.50.refs_0_), channel_id=1, source_target_pairs={{0,3},{1,0},{2,1},{3,2},{4,7},{5,4},{6,5},{7,6},{8,11},{9,8},{10,9... | collective-permute-start | bytes 786440 | tf_op jit(solution)/shard_map/ppermute | solution.py:34
  123.3 31.1 %collective-permute-start.24 = (bf16[1024,512]{1,0:T(8,128)(2,1)S(1)}, bf16[1024,512]{1,0:T(8,128)(2,1)S(1)}, u32[]{:S(2)}, u32[]{:S(2)}) collective-permute-start(bf16[1024,512]{1,0:T(8,128)(2,1)S(1)} %constant_dynamic-update-slice_fusion.refs_8_), channel_id=1, source_target_pairs={{0,24},{1,25},{2,26},{3,27},{4,100},{5,101},{6,102},{7,103},{8,0},... | collective-permute-start | bytes 3145736 | tf_op jit(solution)/shard_map/ppermute | solution.py:43
  123.7 30.7 %collective-permute-start.25 = (bf16[1024,512]{1,0:T(8,128)(2,1)S(1)}, bf16[1024,512]{1,0:T(8,128)(2,1)S(1)}, u32[]{:S(2)}, u32[]{:S(2)}) collective-permute-start(bf16[1024,512]{1,0:T(8,128)(2,1)S(1)} %constant_dynamic-update-slice_fusion.refs_8_), channel_id=1, source_target_pairs={{0,8},{1,9},{2,10},{3,11},{4,36},{5,37},{6,38},{7,39},{8,16},{9,17... | collective-permute-start | bytes 3145736 | tf_op jit(solution)/shard_map/ppermute | solution.py:43
  124.8 8.3 %collective-permute-start.27 = (bf16[256,512]{1,0:T(8,128)(2,1)S(1)}, bf16[256,512]{1,0:T(8,128)(2,1)S(1)}, u32[]{:S(2)}, u32[]{:S(2)}) collective-permute-start(bf16[256,512]{1,0:T(8,128)(2,1)S(1)} %shard_map.50.refs_0_), channel_id=1, source_target_pairs={{0,2},{1,3},{2,0},{3,1},{4,6},{5,7},{6,4},{7,5},{8,10},{9,11},{10,... | collective-permute-start | bytes 786440 | tf_op jit(solution)/shard_map/ppermute | solution.py:34
  125.9 14.2 %collective-permute-start.28 = (bf16[256,512]{1,0:T(8,128)(2,1)S(1)}, bf16[256,512]{1,0:T(8,128)(2,1)S(1)}, u32[]{:S(2)}, u32[]{:S(2)}) collective-permute-start(bf16[256,512]{1,0:T(8,128)(2,1)S(1)} %shard_map.50.refs_0_), channel_id=1, source_target_pairs={{0,1},{1,2},{2,3},{3,0},{4,5},{5,6},{6,7},{7,4},{8,9},{9,10},{10,1... | collective-permute-start | bytes 786440 | tf_op jit(solution)/shard_map/ppermute | solution.py:34
  129.7 11.0 %collective-permute-start.29 = (bf16[256,512]{1,0:T(8,128)(2,1)S(1)}, bf16[256,512]{1,0:T(8,128)(2,1)S(1)}, u32[]{:S(2)}, u32[]{:S(2)}) collective-permute-start(bf16[256,512]{1,0:T(8,128)(2,1)S(1)} %shard_map.50.refs_0_), channel_id=1, source_target_pairs={{0,4},{1,5},{2,6},{3,7},{4,0},{5,1},{6,2},{7,3},{8,12},{9,13},{10,... | collective-permute-start | bytes 786440 | tf_op jit(solution)/shard_map/ppermute | solution.py:30
  133.2 8.4 %collective-permute-start.33 = (bf16[256,512]{1,0:T(8,128)(2,1)S(1)}, bf16[256,512]{1,0:T(8,128)(2,1)S(1)}, u32[]{:S(2)}, u32[]{:S(2)}) collective-permute-start(bf16[256,512]{1,0:T(8,128)(2,1)S(1)} %collective-permute-done.23.refs_9_), channel_id=1, source_target_pairs={{0,96},{1,97},{2,98},{3,99},{4,28},{5,29},{6,30},{7,31},{8,104},{9... | collective-permute-start | bytes 786440 | tf_op jit(solution)/shard_map/ppermute | solution.py:38
  140.2 7.1 %collective-permute-start.34 = (bf16[256,512]{1,0:T(8,128)(2,1)S(1)}, bf16[256,512]{1,0:T(8,128)(2,1)S(1)}, u32[]{:S(2)}, u32[]{:S(2)}) collective-permute-start(bf16[256,512]{1,0:T(8,128)(2,1)S(1)} %collective-permute-done.23.refs_9_), channel_id=1, source_target_pairs={{0,64},{1,65},{2,66},{3,67},{4,20},{5,21},{6,22},{7,23},{8,72},{9,... | collective-permute-start | bytes 786440 | tf_op jit(solution)/shard_map/ppermute | solution.py:38
  140.7 9.3 %collective-permute-start.35 = (bf16[256,512]{1,0:T(8,128)(2,1)S(1)}, bf16[256,512]{1,0:T(8,128)(2,1)S(1)}, u32[]{:S(2)}, u32[]{:S(2)}) collective-permute-start(bf16[256,512]{1,0:T(8,128)(2,1)S(1)} %collective-permute-done.23.refs_9_), channel_id=1, source_target_pairs={{0,32},{1,33},{2,34},{3,35},{4,12},{5,13},{6,14},{7,15},{8,40},{9,... | collective-permute-start | bytes 786440 | tf_op jit(solution)/shard_map/ppermute | solution.py:38
  141.6 9.8 %collective-permute-start.30 = (bf16[256,512]{1,0:T(8,128)(2,1)S(1)}, bf16[256,512]{1,0:T(8,128)(2,1)S(1)}, u32[]{:S(2)}, u32[]{:S(2)}) collective-permute-start(bf16[256,512]{1,0:T(8,128)(2,1)S(1)} %collective-permute-done.26.refs_1_), channel_id=1, source_target_pairs={{0,4},{1,5},{2,6},{3,7},{4,0},{5,1},{6,2},{7,3},{8,12},{9,13},{10,... | collective-permute-start | bytes 786440 | tf_op jit(solution)/shard_map/ppermute | solution.py:30
  147.2 4.2 %collective-permute-start.31 = (bf16[256,512]{1,0:T(8,128)(2,1)S(1)}, bf16[256,512]{1,0:T(8,128)(2,1)S(1)}, u32[]{:S(2)}, u32[]{:S(2)}) collective-permute-start(bf16[256,512]{1,0:T(8,128)(2,1)S(1)} %collective-permute-done.27.refs_2_), channel_id=1, source_target_pairs={{0,4},{1,5},{2,6},{3,7},{4,0},{5,1},{6,2},{7,3},{8,12},{9,13},{10,... | collective-permute-start | bytes 786440 | tf_op jit(solution)/shard_map/ppermute | solution.py:30
  150.0 2.6 %collective-permute-start.32 = (bf16[256,512]{1,0:T(8,128)(2,1)S(1)}, bf16[256,512]{1,0:T(8,128)(2,1)S(1)}, u32[]{:S(2)}, u32[]{:S(2)}) collective-permute-start(bf16[256,512]{1,0:T(8,128)(2,1)S(1)} %collective-permute-done.28.refs_3_), channel_id=1, source_target_pairs={{0,4},{1,5},{2,6},{3,7},{4,0},{5,1},{6,2},{7,3},{8,12},{9,13},{10,... | collective-permute-start | bytes 786440 | tf_op jit(solution)/shard_map/ppermute | solution.py:30
  156.7 7.6 %collective-permute-start.36 = (bf16[256,512]{1,0:T(8,128)(2,1)S(1)}, bf16[256,512]{1,0:T(8,128)(2,1)S(1)}, u32[]{:S(2)}, u32[]{:S(2)}) collective-permute-start(bf16[256,512]{1,0:T(8,128)(2,1)S(1)} %get-tuple-element.32.refs_0_), channel_id=1, source_target_pairs={{0,3},{1,0},{2,1},{3,2},{4,7},{5,4},{6,5},{7,6},{8,11},{9,8},{10,9... | collective-permute-start | bytes 786440 | tf_op jit(solution)/shard_map/ppermute | solution.py:34
  157.1 9.2 %collective-permute-start.38 = (bf16[256,512]{1,0:T(8,128)(2,1)S(1)}, bf16[256,512]{1,0:T(8,128)(2,1)S(1)}, u32[]{:S(2)}, u32[]{:S(2)}) collective-permute-start(bf16[256,512]{1,0:T(8,128)(2,1)S(1)} %get-tuple-element.32.refs_0_), channel_id=1, source_target_pairs={{0,2},{1,3},{2,0},{3,1},{4,6},{5,7},{6,4},{7,5},{8,10},{9,11},{10,... | collective-permute-start | bytes 786440 | tf_op jit(solution)/shard_map/ppermute | solution.py:34
  158.1 14.3 %collective-permute-start.40 = (bf16[256,512]{1,0:T(8,128)(2,1)S(1)}, bf16[256,512]{1,0:T(8,128)(2,1)S(1)}, u32[]{:S(2)}, u32[]{:S(2)}) collective-permute-start(bf16[256,512]{1,0:T(8,128)(2,1)S(1)} %get-tuple-element.32.refs_0_), channel_id=1, source_target_pairs={{0,1},{1,2},{2,3},{3,0},{4,5},{5,6},{6,7},{7,4},{8,9},{9,10},{10,1... | collective-permute-start | bytes 786440 | tf_op jit(solution)/shard_map/ppermute | solution.py:34
  158.7 14.2 %collective-permute-start.42 = (bf16[256,512]{1,0:T(8,128)(2,1)S(1)}, bf16[256,512]{1,0:T(8,128)(2,1)S(1)}, u32[]{:S(2)}, u32[]{:S(2)}) collective-permute-start(bf16[256,512]{1,0:T(8,128)(2,1)S(1)} %get-tuple-element.32.refs_0_), channel_id=1, source_target_pairs={{0,4},{1,5},{2,6},{3,7},{4,0},{5,1},{6,2},{7,3},{8,12},{9,13},{10,... | collective-permute-start | bytes 786440 | tf_op jit(solution)/shard_map/ppermute | solution.py:30
  164.2 10.0 %collective-permute-start.37 = (bf16[256,512]{1,0:T(8,128)(2,1)S(1)}, bf16[256,512]{1,0:T(8,128)(2,1)S(1)}, u32[]{:S(2)}, u32[]{:S(2)}) collective-permute-start(bf16[256,512]{1,0:T(8,128)(2,1)S(1)} %collective-permute-done.36.refs_1_), channel_id=1, source_target_pairs={{0,4},{1,5},{2,6},{3,7},{4,0},{5,1},{6,2},{7,3},{8,12},{9,13},{10,... | collective-permute-start | bytes 786440 | tf_op jit(solution)/shard_map/ppermute | solution.py:30
  166.3 8.0 %collective-permute-start.39 = (bf16[256,512]{1,0:T(8,128)(2,1)S(1)}, bf16[256,512]{1,0:T(8,128)(2,1)S(1)}, u32[]{:S(2)}, u32[]{:S(2)}) collective-permute-start(bf16[256,512]{1,0:T(8,128)(2,1)S(1)} %collective-permute-done.38.refs_2_), channel_id=1, source_target_pairs={{0,4},{1,5},{2,6},{3,7},{4,0},{5,1},{6,2},{7,3},{8,12},{9,13},{10,... | collective-permute-start | bytes 786440 | tf_op jit(solution)/shard_map/ppermute | solution.py:30
  172.4 1.9 %collective-permute-start.41 = (bf16[256,512]{1,0:T(8,128)(2,1)S(1)}, bf16[256,512]{1,0:T(8,128)(2,1)S(1)}, u32[]{:S(2)}, u32[]{:S(2)}) collective-permute-start(bf16[256,512]{1,0:T(8,128)(2,1)S(1)} %collective-permute-done.40.refs_3_), channel_id=1, source_target_pairs={{0,4},{1,5},{2,6},{3,7},{4,0},{5,1},{6,2},{7,3},{8,12},{9,13},{10,... | collective-permute-start | bytes 786440 | tf_op jit(solution)/shard_map/ppermute | solution.py:30
  175.5 1.6 collective-permute-start.43

commit v5 on v4

v5 whole, which is shorter than its diff:
```python
import jax
import jax.numpy as jnp
from jax import lax
from jax.experimental import pallas as pl
from jax.experimental.pallas import tpu as pltpu
from jax.sharding import PartitionSpec as P

B = 128
N = 4096
K = 1024
ROWS = 256
COLS = 512
AXES = ("row", "col")
MIB = 1024 * 1024


def device(x, y, core, z):
    return (((x % 4) * 4 + y % 4) * 2 + core) * 4 + z % 4


def pairs(target):
    return [
        (device(x, y, core, z), device(*target(x, y, core, z)))
        for x in range(4) for y in range(4) for core in range(2) for z in range(4)
    ]


def other_core(a):
    return lax.ppermute(a, AXES, pairs(lambda x, y, core, z: (x, y, 1 - core, z)))


def from_z(a, d):
    return lax.ppermute(a, AXES, pairs(lambda x, y, core, z: (x, y, core, z - d)))


def from_first(a, d):
    return lax.ppermute(a, AXES, pairs(
        lambda x, y, core, z: (x - d, y, core, z) if core == 0 else (x, y - d, core, z)))


def from_second(a, d):
    return lax.ppermute(a, AXES, pairs(
        lambda x, y, core, z: (x, y - d, core, z) if core == 0 else (x - d, y, core, z)))


def gather(a, fetch):
    one, three, two = fetch(a, 1), fetch(a, 3), fetch(a, 2)
    return [a, one, two, three]


def place(x, y, kind, first, second):
    px = jnp.where(kind == 0, x + first, x + second) & 3
    py = jnp.where(kind == 0, y + second, y + first) & 3
    return px, py


def dot_t(a, b):
    return lax.dot_general(a, b, (((1,), (1,)), ((), ())), preferred_element_type=jnp.float32)


def dot(a, b):
    return jnp.dot(a, b, preferred_element_type=jnp.float32)


def aligned(block, size):
    return pl.ds(pl.multiple_of(block * size, size), size)


def block_at(x, y, kind, place_in_order):
    px, py = place(x, y, kind, place_in_order % 4, place_in_order // 4)
    return px * 8 + py * 2 + kind


def some_rows(where, keep_d, own, other, ns, line):
    x, y, core = where[0], where[1], where[2]
    mine, its = own[0][:B, :], other[0][:B, :]
    rows = jnp.concatenate([jnp.where(core == 0, mine, its), jnp.where(core == 0, its, mine)], axis=0)
    for half, (parts, kind) in enumerate(((own, core), (other, 1 - core))):
        for n in ns:
            value = dot_t(rows, parts[n][...])
            for u in range(4):
                block = block_at(x, y, kind, n * 4 + u)
                at = (half * 16 + n * 4 + u) * B
                for t in range(2):
                    keep = keep_d[0, (x * 4 + y) * 2 + t, block].astype(jnp.float32)
                    piece = value[t * B:(t + 1) * B, u * B:(u + 1) * B] * keep
                    line[t * B:(t + 1) * B, at:at + B] = piece.astype(jnp.bfloat16)


def some_columns(where, keep_d, parts, half, n, m, column, panel):
    x, y, core = where[0], where[1], where[2]
    kind = core if half == 0 else 1 - core
    value = dot_t(parts[n][...], column[...])
    for i in range(4):
        row_block = block_at(x, y, kind, n * 4 + i)
        at = (half * 16 + n * 4 + i) * B
        for u in range(4):
            keep = keep_d[0, row_block, block_at(x, y, core, m * 4 + u)].astype(jnp.float32)
            piece = value[i * B:(i + 1) * B, u * B:(u + 1) * B] * keep
            to = (m * 4 + u) * B
            panel[at:at + B, to:to + B] = piece.astype(jnp.bfloat16)


EARLY = (0, 1, 3)


def early_density(where, keep_d, own0, own1, own3, other0, other1, other3, panel, line):
    own, other = {0: own0, 1: own1, 3: own3}, {0: other0, 1: other1, 3: other3}
    some_rows(where, keep_d, own, other, EARLY, line)
    for half, parts in enumerate((own, other)):
        for n in EARLY:
            for m in EARLY:
                some_columns(where, keep_d, parts, half, n, m, own[m], panel)


def first_square(where, keep_d, keep_s, *refs):
    own, other, (panel, line, low, square, total) = refs[:4], refs[4:8], refs[10:]
    x, y, core, z = where[0], where[1], where[2], where[3]
    some_rows(where, keep_d, own, other, (2,), line)
    for half, parts in enumerate((own, other)):
        for n in range(4):
            for m in range(4):
                if n == 2 or m == 2:
                    some_columns(where, keep_d, parts, half, n, m, own[m], panel)

    @pl.loop(0, 8)
    def _(part):
        at = aligned(part, 256)
        value = dot(line[...], panel[:, at])
        for t in range(2):
            for u in range(2):
                block = block_at(x, y, core, part * 2 + u)
                keep = keep_s[0, (x * 4 + y) * 2 + t, block].astype(jnp.float32)
                piece = value[t * B:(t + 1) * B, u * B:(u + 1) * B] * keep
                total[t * B:(t + 1) * B, aligned(part * 2 + u, B)] = piece
                low[t * B:(t + 1) * B, aligned(part * 2 + u, B)] = piece.astype(jnp.bfloat16)
    for t in range(4):
        square[:, t * B:(t + 1) * B] = total[:, aligned(column_at(where, t), B)]


def column_at(where, t):
    x, y, core, z = where[0], where[1], where[2], where[3]
    dx, dy = (z - x) & 3, (t - y) & 3
    return jnp.where(core == 0, dy * 4 + dx, dx * 4 + dy)


def early_first_cube(where, low, panel, early, columns):
    for t in range(4):
        at = aligned(column_at(where, t), B)
        columns[:, t * B:(t + 1) * B] = panel[:, at]
    early[...] = dot(low[...], columns[:2048, :])


def first_density(where, keep_d, its, columns, early, square, out):
    x, y, core, z = where[0], where[1], where[2], where[3]
    value = 3.0 * square[...] - 2.0 * (early[...] + dot(its[...], columns[2048:, :]))
    for t in range(2):
        for u in range(4):
            keep = keep_d[1, (x * 4 + y) * 2 + t, z * 8 + u * 2 + core].astype(jnp.float32)
            piece = value[t * B:(t + 1) * B, u * B:(u + 1) * B] * keep
            out[t * B:(t + 1) * B, u * B:(u + 1) * B] = piece.astype(jnp.bfloat16)


def parts_times_panel(parts, z, panel):
    total = None
    for ref, d, kind in parts:
        rows = [panel[aligned(((z + d) & 3) * 8 + t * 2 + kind, B), :] for t in range(4)]
        term = dot(ref[...], jnp.concatenate(rows, axis=0))
        total = term if total is None else total + term
    return total


def early_cube(where, *refs):
    own, other, panel, out = refs[:4], refs[4], refs[5], refs[6]
    core, z = where[2], where[3]
    parts = [(own[d], d, core) for d in range(4)] + [(other, 0, 1 - core)]
    out[...] = parts_times_panel(parts, z, panel)


def late_cube(where, others, early, panel):
    core, z = where[2], where[3]
    parts = [(others[d - 1], d, 1 - core) for d in (1, 2, 3)]
    return early[...] + parts_times_panel(parts, z, panel)


def chips_times(where, line, chips, panel, sems):
    x, y, core = where[0], where[1], where[2]
    copies, left, right = [], [], []
    for n, (ref, offset, first, second) in enumerate(chips):
        px, py = place(x, y, core, first, second)
        copies.append(pltpu.make_async_copy(
            ref.at[pl.ds(offset, ROWS)], panel.at[aligned(px * 4 + py, ROWS)], sems.at[n]))
        copies[-1].start()
        left.append(line[:, aligned(px * 4 + py, ROWS)])
        right.append(ref[offset:offset + ROWS, :])
    total = None
    for n in range(0, len(chips), 4):
        term = dot(jnp.concatenate(left[n:n + 4], axis=1), jnp.concatenate(right[n:n + 4], axis=0))
        total = term if total is None else total + term
    return total, copies


def early_square(where, *refs):
    both, parts, (early, line, panel), (sems,) = refs[:4], refs[4:7], refs[7:10], refs[10:]
    core, z = where[2], where[3]
    for d in range(4):
        for half, kind in enumerate((core, 1 - core)):
            for t in range(4):
                line[:, aligned(((z + d) & 3) * 8 + t * 2 + kind, B)] = (
                    both[d][half * ROWS:(half + 1) * ROWS, t * B:(t + 1) * B])
    chips = [(parts[n], i * ROWS, i, EARLY[n]) for n in range(3) for i in range(4)]
    value, copies = chips_times(where, line, chips, panel, sems)
    early[...] = value
    for copy in copies:
        copy.wait()


def second_square(where, keep_s, two, early, line, _, square, low, panel, sems):
    x, y, core, z = where[0], where[1], where[2], where[3]
    value, copies = chips_times(where, line, [(two, i * ROWS, i, 2) for i in range(4)], panel, sems)
    value = early[...] + value
    for t in range(2):
        for u in range(4):
            keep = keep_s[1, (x * 4 + y) * 2 + t, z * 8 + u * 2 + core].astype(jnp.float32)
            piece = value[t * B:(t + 1) * B, u * B:(u + 1) * B] * keep
            square[t * B:(t + 1) * B, u * B:(u + 1) * B] = piece
            low[t * B:(t + 1) * B, u * B:(u + 1) * B] = piece.astype(jnp.bfloat16)
    for copy in copies:
        copy.wait()


def second_density(where, *refs):
    others, (early, square, panel, stay, leave) = refs[:3], refs[3:]
    value = 3.0 * square[...] - 2.0 * late_cube(where, others, early, panel)
    first = where[2] == 0
    stay[...] = jnp.where(first, value[:B], value[B:])
    leave[...] = jnp.where(first, value[B:], value[:B])


def join(where, stay, come, out):
    first = where[2] == 0
    for t in range(4):
        mine, its = stay[:, t * B:(t + 1) * B], come[:, t * B:(t + 1) * B]
        out[:, 2 * t * B:(2 * t + 1) * B] = jnp.where(first, mine, its)
        out[:, (2 * t + 1) * B:(2 * t + 2) * B] = jnp.where(first, its, mine)


SMEM = pl.BlockSpec(memory_space=pltpu.SMEM)
VMEM = pl.BlockSpec(memory_space=pltpu.VMEM)


def call(kernel, n_smem, ins, outs, scratch, flops, moved, aliases={}):
    return pl.pallas_call(
        kernel,
        in_specs=[SMEM] * n_smem + [VMEM] * (len(ins) - n_smem),
        out_specs=[VMEM] * len(outs),
        out_shape=outs,
        scratch_shapes=scratch,
        input_output_aliases=aliases,
        cost_estimate=pl.CostEstimate(flops=flops, bytes_accessed=moved, transcendentals=0),
        compiler_params=pltpu.CompilerParams(vmem_limit_bytes=12 * MIB),
    )(*ins)


def body(coeffs, coef_pattern, keep_density, keep_square):
    r, z = lax.axis_index("row"), lax.axis_index("col")
    x, y, core = r // 8, (r // 2) % 4, r % 2
    where = jnp.stack([x, y, core, z]).astype(jnp.int32)
    low_block = jax.ShapeDtypeStruct((ROWS, COLS), jnp.bfloat16)
    full_block = jax.ShapeDtypeStruct((ROWS, COLS), jnp.float32)
    panel_shape = jax.ShapeDtypeStruct((N, COLS), jnp.bfloat16)
    line_shape = jax.ShapeDtypeStruct((ROWS, N), jnp.bfloat16)
    wide_shape = jax.ShapeDtypeStruct((N, N // 2), jnp.bfloat16)
    block_flops = 2 * ROWS * N * COLS
    pair_flops = 2 * 512 * 512 * K

    kept = jnp.concatenate(gather(coeffs, from_z), axis=1)
    pattern = lax.dynamic_slice(coef_pattern, (r, 0), (1, 8)).reshape(4, 2)
    pattern = jnp.concatenate([pattern, pattern], axis=0)
    pattern = lax.dynamic_slice(pattern, (z, 0), (4, 2)).reshape(1, 8)
    kept = kept * jnp.repeat(pattern, B, 1).astype(jnp.bfloat16)
    near = jnp.concatenate(gather(kept, from_first), axis=0)
    own0, own1, own2, own3 = gather(near, from_second)
    other0, other1, other3 = other_core(own0), other_core(own1), other_core(own3)
    panel, line = call(
        early_density, 2, [where, keep_density, own0, own1, own3, other0, other1, other3],
        [wide_shape, line_shape], [], 2 * pair_flops, 2 * MIB)
    panel, line, own2 = lax.optimization_barrier((panel, line, own2))
    other2 = other_core(own2)
    panel, line, low, square = call(
        first_square, 3,
        [where, keep_density, keep_square, own0, own1, own2, own3, other0, other1, other2, other3, panel, line],
        [wide_shape, line_shape, jax.ShapeDtypeStruct((ROWS, N // 2), jnp.bfloat16), full_block],
        [pltpu.VMEM((ROWS, N // 2), jnp.float32)],
        15 * pair_flops + 4 * block_flops, 40 * MIB, {11: 0, 12: 1})

    its = other_core(low)
    early, columns = call(
        early_first_cube, 1, [where, low, panel], [full_block, panel_shape], [], block_flops // 2, 12 * MIB)
    (current,) = call(
        first_density, 2, [where, keep_density, its, columns, early, square], [low_block], [],
        block_flops // 2, 4 * MIB)

    near = jnp.concatenate(gather(current, from_first), axis=0)
    part0, part1, part2, part3 = gather(near, from_second)
    both = gather(jnp.concatenate([current, other_core(current)], axis=0), from_z)
    early, line, panel = call(
        early_square, 1, [where, *both, part0, part1, part3], [full_block, line_shape, panel_shape],
        [pltpu.SemaphoreType.DMA((12,))], block_flops * 3 // 4, 12 * MIB)
    early, part2 = lax.optimization_barrier((early, part2))
    square, low, panel = call(
        second_square, 2, [where, keep_square, part2, early, line, panel],
        [full_block, low_block, panel_shape],
        [pltpu.SemaphoreType.DMA((4,))], block_flops // 4, 6 * MIB, {5: 2})

    own = gather(low, from_z)
    other = [other_core(part) for part in own]
    (early,) = call(
        early_cube, 1, [where, *own, other[0], panel], [full_block], [], block_flops * 5 // 8, 4 * MIB)
    half = jax.ShapeDtypeStruct((B, COLS), jnp.float32)
    stay, leave = call(
        second_density, 1, [where, *other[1:], early, square, panel], [half, half], [],
        block_flops * 3 // 8, 3 * MIB)
    come = other_core(leave)
    (out,) = call(
        join, 1, [where, stay, come], [jax.ShapeDtypeStruct((B, 2 * COLS), jnp.float32)], [], 0, MIB)
    return out


def solution(mesh):
    placed = (P("row", "col"), P(), P(), P())
    return jax.shard_map(
        body, mesh=mesh, in_specs=placed, out_specs=P("row", "col"), check_vma=False
    )
```

time: 178 us -> 152 us (0.85)
  the two profiles are of different devices: /device:TPU:1 before, /device:TPU:5 now
where the time goes in v5:
time: 152 us; the launch traced here: 151 us
  waiting for transfers between devices  63.7 us (42%)
  starting transfers between devices  42.8 us (28%)
  Pallas kernels  42.8 us (28%)
    pallas_call x9, Pallas kernels, call(): pl.pallas_call(kernel, in_specs=[SMEM] * n_smem + [VMEM] * (len(ins) - n_...  42.8 us
    ppermute x9, waiting for transfers between devices, from_z(): lax.ppermute(a, AXES, pairs(lambda x, y, core, z: (x, y, core, z - d)))  37.3 us
    ppermute x11, starting transfers between devices, other_core(): lax.ppermute(a, AXES, pairs(lambda x, y, core, z: (x, y, 1 - core, z)))  20.3 us
    ppermute x6, waiting for transfers between devices, from_first(): lax.ppermute(a, AXES, pairs(lambda x, y, core, z: (x - d, y, core, z) if...  11.8 us
    ppermute x6, starting transfers between devices, from_first(): lax.ppermute(a, AXES, pairs(lambda x, y, core, z: (x - d, y, core, z) if...  8.83 us
    ppermute x9, starting transfers between devices, from_z(): lax.ppermute(a, AXES, pairs(lambda x, y, core, z: (x, y, core, z - d)))  8.77 us
    ppermute x6, waiting for transfers between devices, from_second(): lax.ppermute(a, AXES, pairs(lambda x, y, core, z: (x, y - d, core, z) if...  7.53 us
    ppermute x11, waiting for transfers between devices, other_core(): lax.ppermute(a, AXES, pairs(lambda x, y, core, z: (x, y, 1 - core, z)))  7.12 us
  transfers between devices with their start and end apart: 32, of which 16 were waited for; matrix products, arithmetic and copies ran while one was open for 1% of the time, Pallas kernels for 13%

profile of v5, /device:TPU:5, one launch (start us, length us, event | category | flops | bytes accessed | tf_op | source)
XLA Modules:
  0.0 151.4 jit_solution(7630325177508709986)
XLA Ops:
  0.0 3.6 %collective-permute-start.1 = (bf16[128,256]{1,0:T(8,128)(2,1)}, bf16[128,256]{1,0:T(8,128)(2,1)S(1)}, u32[]{:S(2)}, u32[]{:S(2)}) collective-permute-start(bf16[128,256]{1,0:T(8,128)(2,1)} %param.4), channel_id=1, source_target_pairs={{0,2},{1,3},{2,0},{3,1},{4,6},{5,7},{6,4},{7,5},{8,10},{9,11},{10,... | collective-permute-start | bytes 196616 | tf_op jit(solution)/shard_map/ppermute | solution.py:33
  4.0 1.0 collective-permute-start.2
  5.9 1.4 collective-permute-done
  7.3 1.3 collective-permute-done.2
  8.6 0.9 maximum_multiply_fusion
  9.5 1.4 collective-permute-start.5
  10.8 2.6 %collective-permute-start.4 = (bf16[128,1024]{1,0:T(8,128)(2,1)S(1)}, bf16[128,1024]{1,0:T(8,128)(2,1)S(1)}, u32[]{:S(2)}, u32[]{:S(2)}) collective-permute-start(bf16[128,1024]{1,0:T(8,128)(2,1)S(1)} %maximum_multiply_fusion), channel_id=1, source_target_pairs={{0,64},{1,65},{2,66},{3,67},{4,20},{5,21},{6,22},{7,23},{8,72},{9,... | collective-permute-start | bytes 786440 | tf_op jit(solution)/shard_map/ppermute | solution.py:37
  13.5 1.1 collective-permute-start.3
  14.5 1.5 collective-permute-done.5
  16.0 4.0 %collective-permute-done.4 = bf16[128,1024]{1,0:T(8,128)(2,1)S(1)} collective-permute-done((bf16[128,1024]{1,0:T(8,128)(2,1)S(1)}, bf16[128,1024]{1,0:T(8,128)(2,1)S(1)}, u32[]{:S(2)}, u32[]{:S(2)}) %collective-permute-start.4) | collective-permute-done | bytes 262176 | tf_op jit(solution)/shard_map/ppermute | solution.py:37
  20.1 1.0 collective-permute-start.7
  21.1 0.5 collective-permute-start.6
  21.6 5.0 %collective-permute-start.8 = (bf16[512,1024]{1,0:T(8,128)(2,1)S(1)}, bf16[512,1024]{1,0:T(8,128)(2,1)}, u32[]{:S(2)}, u32[]{:S(2)}) collective-permute-start(bf16[512,1024]{1,0:T(8,128)(2,1)S(1)} %pad_maximum_fusion.own0.refs_0_), channel_id=1, source_target_pairs={{0,4},{1,5},{2,6},{3,7},{4,0},{5,1},{6,2},{7,3},{8,12},{9,13},{10,... | collective-permute-start | bytes 3145736 | tf_op jit(solution)/shard_map/ppermute | solution.py:29
  26.6 7.5 %collective-permute-done.7.own3.refs_3_ = bf16[512,1024]{1,0:T(8,128)(2,1)S(1)} collective-permute-done((bf16[512,1024]{1,0:T(8,128)(2,1)S(1)}, bf16[512,1024]{1,0:T(8,128)(2,1)S(1)}, u32[]{:S(2)}, u32[]{:S(2)}) %collective-permute-start.7) | collective-permute-done | bytes 1048608 | tf_op jit(solution)/shard_map/ppermute | solution.py:42
  34.1 5.3 %collective-permute-start.10 = (bf16[512,1024]{1,0:T(8,128)(2,1)S(1)}, bf16[512,1024]{1,0:T(8,128)(2,1)}, u32[]{:S(2)}, u32[]{:S(2)}) collective-permute-start(bf16[512,1024]{1,0:T(8,128)(2,1)S(1)} %collective-permute-done.7.own3.refs_3_), channel_id=1, source_target_pairs={{0,4},{1,5},{2,6},{3,7},{4,0},{5,1},{6,2},{7,3},{8,12},{9,13},{10,... | collective-permute-start | bytes 3145736 | tf_op jit(solution)/shard_map/ppermute | solution.py:29
  40.1 1.7 %collective-permute-done.10.other3.refs_7_ = bf16[512,1024]{1,0:T(8,128)(2,1)} collective-permute-done((bf16[512,1024]{1,0:T(8,128)(2,1)S(1)}, bf16[512,1024]{1,0:T(8,128)(2,1)}, u32[]{:S(2)}, u32[]{:S(2)}) %collective-permute-start.10) | collective-permute-done | bytes 1048608 | tf_op jit(solution)/shard_map/ppermute | solution.py:29
  41.8 1.5 collective-permute-done.9.other1.refs_5_
  43.3 13.5 %shard_map.46 = (bf16[4096,2048]{1,0:T(8,128)(2,1)S(1)}, bf16[256,4096]{1,0:T(8,128)(2,1)S(1)}) custom-call(s32[4]{0:T(128)S(1)} %pad_add_fusion.1.where, s32[2,32,32]{2,1,0:T(8,128)S(1)} %copy-done.1, bf16[512,1024]{1,0:T(8,128)(2,1)S(1)} %pad_maximum_fusion.own0.refs_0_, bf16[512,1024]{1,0:T(8,128)(2,1)S(1)} %collective-permute-done.6.own1.refs_1_, ...), custom_call_target="tpu_custom_call" | custom-call | flops 1073741824 | bytes 2097152 | tf_op jit(solution)/shard_map/pallas_call | solution.py:253
  56.8 0.7 collective-permute-start.12
  57.4 2.5 %collective-permute-done.12.refs_6_ = bf16[512,1024]{1,0:T(8,128)(2,1)S(1)} collective-permute-done((bf16[512,1024]{1,0:T(8,128)(2,1)}, bf16[512,1024]{1,0:T(8,128)(2,1)S(1)}, u32[]{:S(2)}, u32[]{:S(2)}) %collective-permute-start.12) | collective-permute-done | bytes 1048608 | tf_op jit(solution)/shard_map/ppermute | solution.py:29
  59.9 16.8 %shard_map.47 = (bf16[4096,2048]{1,0:T(8,128)(2,1)S(1)}, bf16[256,4096]{1,0:T(8,128)(2,1)S(1)}, bf16[256,2048]{1,0:T(8,128)(2,1)S(1)}, f32[256,512]{1,0:T(8,128)S(1)}) custom-call(s32[4]{0:T(128)S(1)} %pad_add_fusion.1.where, s32[2,32,32]{2,1,0:T(8,128)S(1)} %copy-done.1, ...), custom_call_target="tpu_custom_call", output_to_operand_aliasing={{0}: (11, {}), {1}: (12, {})} | custom-call | flops 12348030976 | bytes 41943040 | tf_op jit(solution)/shard_map/pallas_call | solution.py:253
  77.2 2.3 %shard_map.48 = (f32[256,512]{1,0:T(8,128)S(1)}, bf16[4096,512]{1,0:T(8,128)(2,1)S(1)}) custom-call(s32[4]{0:T(128)S(1)} %pad_add_fusion.1.where, bf16[256,2048]{1,0:T(8,128)(2,1)S(1)} %get-tuple-element.30.low, bf16[4096,2048]{1,0:T(8,128)(2,1)S(1)} %get-tuple-element.31.panel), custom_call_target="tpu_custom_call" | custom-call | flops 536870912 | bytes 12582912 | tf_op jit(solution)/shard_map/pallas_call | solution.py:253
  79.5 1.8 %shard_map.49 = bf16[256,512]{1,0:T(8,128)(2,1)S(1)} custom-call(s32[4]{0:T(128)S(1)} %pad_add_fusion.1.where, s32[2,32,32]{2,1,0:T(8,128)S(1)} %copy-done.1, bf16[256,2048]{1,0:T(8,128)(2,1)S(1)} %collective-permute-done.13.its, bf16[4096,512]{1,0:T(8,128)(2,1)S(1)} %get-tuple-element.32.columns, f32[256,512]{1,0:T(8,128)S(1)} %get-tuple-element.33.early, ...), custom_call_target="tpu_custom_call" | custom-call | flops 536870912 | bytes 4194304 | tf_op jit(solution)/shard_map/pallas_call | solution.py:253
  81.3 0.5 collective-permute-start.14
  81.9 2.5 %collective-permute-start.19 = (bf16[256,512]{1,0:T(8,128)(2,1)S(1)}, bf16[256,512]{1,0:T(8,128)(2,1)S(1)}, u32[]{:S(2)}, u32[]{:S(2)}) collective-permute-start(bf16[256,512]{1,0:T(8,128)(2,1)S(1)} %shard_map.49), channel_id=1, source_target_pairs={{0,64},{1,65},{2,66},{3,67},{4,20},{5,21},{6,22},{7,23},{8,72},{9,... | collective-permute-start | bytes 786440 | tf_op jit(solution)/shard_map/ppermute | solution.py:37
  84.4 1.1 collective-permute-start.18
  85.6 2.5 %collective-permute-done.20 = bf16[256,512]{1,0:T(8,128)(2,1)S(1)} collective-permute-done((bf16[256,512]{1,0:T(8,128)(2,1)S(1)}, bf16[256,512]{1,0:T(8,128)(2,1)S(1)}, u32[]{:S(2)}, u32[]{:S(2)}) %collective-permute-start.20) | collective-permute-done | bytes 262176 | tf_op jit(solution)/shard_map/ppermute | solution.py:37
  88.2 2.8 %collective-permute-done.19 = bf16[256,512]{1,0:T(8,128)(2,1)S(1)} collective-permute-done((bf16[256,512]{1,0:T(8,128)(2,1)S(1)}, bf16[256,512]{1,0:T(8,128)(2,1)S(1)}, u32[]{:S(2)}, u32[]{:S(2)}) %collective-permute-start.19) | collective-permute-done | bytes 262176 | tf_op jit(solution)/shard_map/ppermute | solution.py:37
  91.0 0.9 collective-permute-done.18
  92.0 0.8 collective-permute-start.22
  92.8 0.7 collective-permute-start.21
  93.5 1.5 %collective-permute-start.23 = (bf16[1024,512]{1,0:T(8,128)(2,1)S(1)}, bf16[1024,512]{1,0:T(8,128)(2,1)S(1)}, u32[]{:S(2)}, u32[]{:S(2)}) collective-permute-start(bf16[1024,512]{1,0:T(8,128)(2,1)S(1)} %pad_maximum_fusion.1.refs_4_), channel_id=1, source_target_pairs={{0,16},{1,17},{2,18},{3,19},{4,68},{5,69},{6,70},{7,71},{8,24},{9,... | collective-permute-start | bytes 3145736 | tf_op jit(solution)/shard_map/ppermute | solution.py:42
  95.0 0.9 collective-permute-start.16
  95.9 16.1 %collective-permute-done.17.refs_3_ = bf16[512,512]{1,0:T(8,128)(2,1)S(1)} collective-permute-done((bf16[512,512]{1,0:T(8,128)(2,1)S(1)}, bf16[512,512]{1,0:T(8,128)(2,1)S(1)}, u32[]{:S(2)}, u32[]{:S(2)}) %collective-permute-start.17) | collective-permute-done | bytes 524320 | tf_op jit(solution)/shard_map/ppermute | solution.py:33
  112.0 13.0 %collective-permute-done.15.refs_1_ = bf16[512,512]{1,0:T(8,128)(2,1)S(1)} collective-permute-done((bf16[512,512]{1,0:T(8,128)(2,1)S(1)}, bf16[512,512]{1,0:T(8,128)(2,1)S(1)}, u32[]{:S(2)}, u32[]{:S(2)}) %collective-permute-start.15) | collective-permute-done | bytes 524320 | tf_op jit(solution)/shard_map/ppermute | solution.py:33
  125.0 2.8 %shard_map.50 = (f32[256,512]{1,0:T(8,128)S(1)}, bf16[256,4096]{1,0:T(8,128)(2,1)S(1)}, bf16[4096,512]{1,0:T(8,128)(2,1)S(1)}) custom-call(s32[4]{0:T(128)S(1)} %pad_add_fusion.1.where, bf16[512,512]{1,0:T(8,128)(2,1)S(1)} %pad_maximum_fusion.2.refs_0_, bf16[512,512]{1,0:T(8,128)(2,1)S(1)} %collective-permute-done.15.refs_1_, ...), custom_call_target="tpu_custom_call" | custom-call | flops 805306368 | bytes 12582912 | tf_op jit(solution)/shard_map/pallas_call | solution.py:253
  127.8 1.7 %shard_map.51 = (f32[256,512]{1,0:T(8,128)S(1)}, bf16[256,512]{1,0:T(8,128)(2,1)S(1)}, bf16[4096,512]{1,0:T(8,128)(2,1)S(1)}) custom-call(s32[4]{0:T(128)S(1)} %pad_add_fusion.1.where, s32[2,32,32]{2,1,0:T(8,128)S(1)} %copy-done.2, bf16[1024,512]{1,0:T(8,128)(2,1)S(1)} %collective-permute-done.23.two, ...), custom_call_target="tpu_custom_call", output_to_operand_aliasing={{2}: (5, {})} | custom-call | flops 268435456 | bytes 6291456 | tf_op jit(solution)/shard_map/pallas_call | solution.py:253
  129.7 2.7 %collective-permute-start.26 = (bf16[256,512]{1,0:T(8,128)(2,1)S(1)}, bf16[256,512]{1,0:T(8,128)(2,1)S(1)}, u32[]{:S(2)}, u32[]{:S(2)}) collective-permute-start(bf16[256,512]{1,0:T(8,128)(2,1)S(1)} %get-tuple-element.40.refs_0_), channel_id=1, source_target_pairs={{0,2},{1,3},{2,0},{3,1},{4,6},{5,7},{6,4},{7,5},{8,10},{9,11},{10,... | collective-permute-start | bytes 786440 | tf_op jit(solution)/shard_map/ppermute | solution.py:33
  132.4 1.8 %collective-permute-start.30 = (bf16[256,512]{1,0:T(8,128)(2,1)S(1)}, bf16[256,512]{1,0:T(8,128)(2,1)S(1)}, u32[]{:S(2)}, u32[]{:S(2)}) collective-permute-start(bf16[256,512]{1,0:T(8,128)(2,1)S(1)} %get-tuple-element.40.refs_0_), channel_id=1, source_target_pairs={{0,4},{1,5},{2,6},{3,7},{4,0},{5,1},{6,2},{7,3},{8,12},{9,13},{10,... | collective-permute-start | bytes 786440 | tf_op jit(solution)/shard_map/ppermute | solution.py:29
  134.2 3.2 %collective-permute-done.28.refs_3_ = bf16[256,512]{1,0:T(8,128)(2,1)S(1)} collective-permute-done((bf16[256,512]{1,0:T(8,128)(2,1)S(1)}, bf16[256,512]{1,0:T(8,128)(2,1)S(1)}, u32[]{:S(2)}, u32[]{:S(2)}) %collective-permute-start.28) | collective-permute-done | bytes 262176 | tf_op jit(solution)/shard_map/ppermute | solution.py:33
  137.4 3.7 %collective-permute-start.29 = (bf16[256,512]{1,0:T(8,128)(2,1)S(1)}, bf16[256,512]{1,0:T(8,128)(2,1)S(1)}, u32[]{:S(2)}, u32[]{:S(2)}) collective-permute-start(bf16[256,512]{1,0:T(8,128)(2,1)S(1)} %collective-permute-done.28.refs_3_), channel_id=1, source_target_pairs={{0,4},{1,5},{2,6},{3,7},{4,0},{5,1},{6,2},{7,3},{8,12},{9,13},{10,... | collective-permute-start | bytes 786440 | tf_op jit(solution)/shard_map/ppermute | solution.py:29
  141.1 2.3 %collective-permute-done.26.refs_2_ = bf16[256,512]{1,0:T(8,128)(2,1)S(1)} collective-permute-done((bf16[256,512]{1,0:T(8,128)(2,1)S(1)}, bf16[256,512]{1,0:T(8,128)(2,1)S(1)}, u32[]{:S(2)}, u32[]{:S(2)}) %collective-permute-start.26) | collective-permute-done | bytes 262176 | tf_op jit(solution)/shard_map/ppermute | solution.py:33
  143.4 1.9 %collective-permute-start.27 = (bf16[256,512]{1,0:T(8,128)(2,1)S(1)}, bf16[256,512]{1,0:T(8,128)(2,1)S(1)}, u32[]{:S(2)}, u32[]{:S(2)}) collective-permute-start(bf16[256,512]{1,0:T(8,128)(2,1)S(1)} %collective-permute-done.26.refs_2_), channel_id=1, source_target_pairs={{0,4},{1,5},{2,6},{3,7},{4,0},{5,1},{6,2},{7,3},{8,12},{9,13},{10,... | collective-permute-start | bytes 786440 | tf_op jit(solution)/shard_map/ppermute | solution.py:29
  145.3 0.6 collective-permute-start.25
  145.8 1.4 shard_map.52.refs_3_
  147.3 1.2 shard_map.53
  148.6 1.4 collective-permute-done.31.come
  150.0 1.4 shard_map.54
  (44 shorter events, 3.2 us)
Async XLA Ops:
  0.0 5.1 %copy-start = (s32[32,8]{0,1:T(8,128)S(1)}, s32[32,8]{0,1:T(8,128)}, u32[]{:S(2)}) copy-start(s32[32,8]{0,1:T(8,128)} %param.5) | copy-start | bytes 3076
  0.0 43.3 %copy-start.1 = (s32[2,32,32]{2,1,0:T(8,128)S(1)}, s32[2,32,32]{2,1,0:T(8,128)}, u32[]{:S(2)}) copy-start(s32[2,32,32]{2,1,0:T(8,128)} %keep_d.5) | copy-start | bytes 24580
  0.0 5.9 %collective-permute-start.1 = (bf16[128,256]{1,0:T(8,128)(2,1)}, bf16[128,256]{1,0:T(8,128)(2,1)S(1)}, u32[]{:S(2)}, u32[]{:S(2)}) collective-permute-start(bf16[128,256]{1,0:T(8,128)(2,1)} %param.4), channel_id=1, source_target_pairs={{0,2},{1,3},{2,0},{3,1},{4,6},{5,7},{6,4},{7,5},{8,10},{9,11},{10,... | collective-permute-start | bytes 196616 | tf_op jit(solution)/shard_map/ppermute | solution.py:33
  3.6 3.7 %collective-permute-start = (bf16[128,256]{1,0:T(8,128)(2,1)}, bf16[128,256]{1,0:T(8,128)(2,1)S(1)}, u32[]{:S(2)}, u32[]{:S(2)}) collective-permute-start(bf16[128,256]{1,0:T(8,128)(2,1)} %param.4), channel_id=1, source_target_pairs={{0,3},{1,0},{2,1},{3,2},{4,7},{5,4},{6,5},{7,6},{8,11},{9,8},{10,9... | collective-permute-start | bytes 196616 | tf_op jit(solution)/shard_map/ppermute | solution.py:33
  4.0 4.5 %collective-permute-start.2 = (bf16[128,256]{1,0:T(8,128)(2,1)}, bf16[128,256]{1,0:T(8,128)(2,1)S(1)}, u32[]{:S(2)}, u32[]{:S(2)}) collective-permute-start(bf16[128,256]{1,0:T(8,128)(2,1)} %param.4), channel_id=1, source_target_pairs={{0,1},{1,2},{2,3},{3,0},{4,5},{5,6},{6,7},{7,4},{8,9},{9,10},{10,1... | collective-permute-start | bytes 196616 | tf_op jit(solution)/shard_map/ppermute | solution.py:33
  9.5 6.6 %collective-permute-start.5 = (bf16[128,1024]{1,0:T(8,128)(2,1)S(1)}, bf16[128,1024]{1,0:T(8,128)(2,1)S(1)}, u32[]{:S(2)}, u32[]{:S(2)}) collective-permute-start(bf16[128,1024]{1,0:T(8,128)(2,1)S(1)} %maximum_multiply_fusion), channel_id=1, source_target_pairs={{0,32},{1,33},{2,34},{3,35},{4,12},{5,13},{6,14},{7,15},{8,40},{9,... | collective-permute-start | bytes 786440 | tf_op jit(solution)/shard_map/ppermute | solution.py:37
  10.8 9.2 %collective-permute-start.4 = (bf16[128,1024]{1,0:T(8,128)(2,1)S(1)}, bf16[128,1024]{1,0:T(8,128)(2,1)S(1)}, u32[]{:S(2)}, u32[]{:S(2)}) collective-permute-start(bf16[128,1024]{1,0:T(8,128)(2,1)S(1)} %maximum_multiply_fusion), channel_id=1, source_target_pairs={{0,64},{1,65},{2,66},{3,67},{4,20},{5,21},{6,22},{7,23},{8,72},{9,... | collective-permute-start | bytes 786440 | tf_op jit(solution)/shard_map/ppermute | solution.py:37
  13.5 6.6 %collective-permute-start.3 = (bf16[128,1024]{1,0:T(8,128)(2,1)S(1)}, bf16[128,1024]{1,0:T(8,128)(2,1)S(1)}, u32[]{:S(2)}, u32[]{:S(2)}) collective-permute-start(bf16[128,1024]{1,0:T(8,128)(2,1)S(1)} %maximum_multiply_fusion), channel_id=1, source_target_pairs={{0,96},{1,97},{2,98},{3,99},{4,28},{5,29},{6,30},{7,31},{8,104},{9... | collective-permute-start | bytes 786440 | tf_op jit(solution)/shard_map/ppermute | solution.py:37
  20.1 14.0 %collective-permute-start.7 = (bf16[512,1024]{1,0:T(8,128)(2,1)S(1)}, bf16[512,1024]{1,0:T(8,128)(2,1)S(1)}, u32[]{:S(2)}, u32[]{:S(2)}) collective-permute-start(bf16[512,1024]{1,0:T(8,128)(2,1)S(1)} %pad_maximum_fusion.own0.refs_0_), channel_id=1, source_target_pairs={{0,8},{1,9},{2,10},{3,11},{4,36},{5,37},{6,38},{7,39},{8,16},{9,17... | collective-permute-start | bytes 3145736 | tf_op jit(solution)/shard_map/ppermute | solution.py:42
  21.1 18.3 %collective-permute-start.6 = (bf16[512,1024]{1,0:T(8,128)(2,1)S(1)}, bf16[512,1024]{1,0:T(8,128)(2,1)S(1)}, u32[]{:S(2)}, u32[]{:S(2)}) collective-permute-start(bf16[512,1024]{1,0:T(8,128)(2,1)S(1)} %pad_maximum_fusion.own0.refs_0_), channel_id=1, source_target_pairs={{0,24},{1,25},{2,26},{3,27},{4,100},{5,101},{6,102},{7,103},{8,0},... | collective-permute-start | bytes 3145736 | tf_op jit(solution)/shard_map/ppermute | solution.py:42
  21.6 18.5 %collective-permute-start.8 = (bf16[512,1024]{1,0:T(8,128)(2,1)S(1)}, bf16[512,1024]{1,0:T(8,128)(2,1)}, u32[]{:S(2)}, u32[]{:S(2)}) collective-permute-start(bf16[512,1024]{1,0:T(8,128)(2,1)S(1)} %pad_maximum_fusion.own0.refs_0_), channel_id=1, source_target_pairs={{0,4},{1,5},{2,6},{3,7},{4,0},{5,1},{6,2},{7,3},{8,12},{9,13},{10,... | collective-permute-start | bytes 3145736 | tf_op jit(solution)/shard_map/ppermute | solution.py:29
  34.1 7.7 %collective-permute-start.10 = (bf16[512,1024]{1,0:T(8,128)(2,1)S(1)}, bf16[512,1024]{1,0:T(8,128)(2,1)}, u32[]{:S(2)}, u32[]{:S(2)}) collective-permute-start(bf16[512,1024]{1,0:T(8,128)(2,1)S(1)} %collective-permute-done.7.own3.refs_3_), channel_id=1, source_target_pairs={{0,4},{1,5},{2,6},{3,7},{4,0},{5,1},{6,2},{7,3},{8,12},{9,13},{10,... | collective-permute-start | bytes 3145736 | tf_op jit(solution)/shard_map/ppermute | solution.py:29
  39.4 3.9 %collective-permute-start.9 = (bf16[512,1024]{1,0:T(8,128)(2,1)S(1)}, bf16[512,1024]{1,0:T(8,128)(2,1)}, u32[]{:S(2)}, u32[]{:S(2)}) collective-permute-start(bf16[512,1024]{1,0:T(8,128)(2,1)S(1)} %collective-permute-done.6.own1.refs_1_), channel_id=1, source_target_pairs={{0,4},{1,5},{2,6},{3,7},{4,0},{5,1},{6,2},{7,3},{8,12},{9,13},{10,... | collective-permute-start | bytes 3145736 | tf_op jit(solution)/shard_map/ppermute | solution.py:29
  39.7 17.0 %collective-permute-start.11 = (bf16[512,1024]{1,0:T(8,128)(2,1)S(1)}, bf16[512,1024]{1,0:T(8,128)(2,1)}, u32[]{:S(2)}, u32[]{:S(2)}) collective-permute-start(bf16[512,1024]{1,0:T(8,128)(2,1)S(1)} %pad_maximum_fusion.own0.refs_0_), channel_id=1, source_target_pairs={{0,16},{1,17},{2,18},{3,19},{4,68},{5,69},{6,70},{7,71},{8,24},{9,... | collective-permute-start | bytes 3145736 | tf_op jit(solution)/shard_map/ppermute | solution.py:42
  40.1 19.8 %copy-start.2 = (s32[2,32,32]{2,1,0:T(8,128)S(1)}, s32[2,32,32]{2,1,0:T(8,128)}, u32[]{:S(2)}) copy-start(s32[2,32,32]{2,1,0:T(8,128)} %keep_s.3) | copy-start | bytes 24580
  56.8 3.2 %collective-permute-start.12 = (bf16[512,1024]{1,0:T(8,128)(2,1)}, bf16[512,1024]{1,0:T(8,128)(2,1)S(1)}, u32[]{:S(2)}, u32[]{:S(2)}) collective-permute-start(bf16[512,1024]{1,0:T(8,128)(2,1)} %collective-permute-done.11.refs_2_), channel_id=1, source_target_pairs={{0,4},{1,5},{2,6},{3,7},{4,0},{5,1},{6,2},{7,3},{8,12},{9,13},{10,... | collective-permute-start | bytes 3145736 | tf_op jit(solution)/shard_map/ppermute | solution.py:29
  76.7 2.7 %collective-permute-start.13 = (bf16[256,2048]{1,0:T(8,128)(2,1)S(1)}, bf16[256,2048]{1,0:T(8,128)(2,1)S(1)}, u32[]{:S(2)}, u32[]{:S(2)}) collective-permute-start(bf16[256,2048]{1,0:T(8,128)(2,1)S(1)} %get-tuple-element.30.low), channel_id=1, source_target_pairs={{0,4},{1,5},{2,6},{3,7},{4,0},{5,1},{6,2},{7,3},{8,12},{9,13},{10,... | collective-permute-start | bytes 3145736 | tf_op jit(solution)/shard_map/ppermute | solution.py:29
  81.3 4.2 %collective-permute-start.14 = (bf16[256,512]{1,0:T(8,128)(2,1)S(1)}, bf16[256,512]{1,0:T(8,128)(2,1)S(1)}, u32[]{:S(2)}, u32[]{:S(2)}) collective-permute-start(bf16[256,512]{1,0:T(8,128)(2,1)S(1)} %shard_map.49), channel_id=1, source_target_pairs={{0,4},{1,5},{2,6},{3,7},{4,0},{5,1},{6,2},{7,3},{8,12},{9,13},{10,... | collective-permute-start | bytes 786440 | tf_op jit(solution)/shard_map/ppermute | solution.py:29
  81.7 6.4 %collective-permute-start.20 = (bf16[256,512]{1,0:T(8,128)(2,1)S(1)}, bf16[256,512]{1,0:T(8,128)(2,1)S(1)}, u32[]{:S(2)}, u32[]{:S(2)}) collective-permute-start(bf16[256,512]{1,0:T(8,128)(2,1)S(1)} %shard_map.49), channel_id=1, source_target_pairs={{0,32},{1,33},{2,34},{3,35},{4,12},{5,13},{6,14},{7,15},{8,40},{9,... | collective-permute-start | bytes 786440 | tf_op jit(solution)/shard_map/ppermute | solution.py:37
  81.9 9.1 %collective-permute-start.19 = (bf16[256,512]{1,0:T(8,128)(2,1)S(1)}, bf16[256,512]{1,0:T(8,128)(2,1)S(1)}, u32[]{:S(2)}, u32[]{:S(2)}) collective-permute-start(bf16[256,512]{1,0:T(8,128)(2,1)S(1)} %shard_map.49), channel_id=1, source_target_pairs={{0,64},{1,65},{2,66},{3,67},{4,20},{5,21},{6,22},{7,23},{8,72},{9,... | collective-permute-start | bytes 786440 | tf_op jit(solution)/shard_map/ppermute | solution.py:37
  84.4 7.5 %collective-permute-start.18 = (bf16[256,512]{1,0:T(8,128)(2,1)S(1)}, bf16[256,512]{1,0:T(8,128)(2,1)S(1)}, u32[]{:S(2)}, u32[]{:S(2)}) collective-permute-start(bf16[256,512]{1,0:T(8,128)(2,1)S(1)} %shard_map.49), channel_id=1, source_target_pairs={{0,96},{1,97},{2,98},{3,99},{4,28},{5,29},{6,30},{7,31},{8,104},{9... | collective-permute-start | bytes 786440 | tf_op jit(solution)/shard_map/ppermute | solution.py:37
  85.6 26.4 %collective-permute-start.17 = (bf16[512,512]{1,0:T(8,128)(2,1)S(1)}, bf16[512,512]{1,0:T(8,128)(2,1)S(1)}, u32[]{:S(2)}, u32[]{:S(2)}) collective-permute-start(bf16[512,512]{1,0:T(8,128)(2,1)S(1)} %pad_maximum_fusion.2.refs_0_), channel_id=1, source_target_pairs={{0,1},{1,2},{2,3},{3,0},{4,5},{5,6},{6,7},{7,4},{8,9},{9,10},{10,1... | collective-permute-start | bytes 1572872 | tf_op jit(solution)/shard_map/ppermute | solution.py:33
  92.0 33.1 %collective-permute-start.22 = (bf16[1024,512]{1,0:T(8,128)(2,1)S(1)}, bf16[1024,512]{1,0:T(8,128)(2,1)S(1)}, u32[]{:S(2)}, u32[]{:S(2)}) collective-permute-start(bf16[1024,512]{1,0:T(8,128)(2,1)S(1)} %pad_maximum_fusion.1.refs_4_), channel_id=1, source_target_pairs={{0,8},{1,9},{2,10},{3,11},{4,36},{5,37},{6,38},{7,39},{8,16},{9,17... | collective-permute-start | bytes 3145736 | tf_op jit(solution)/shard_map/ppermute | solution.py:42
  92.8 32.2 %collective-permute-start.21 = (bf16[1024,512]{1,0:T(8,128)(2,1)S(1)}, bf16[1024,512]{1,0:T(8,128)(2,1)S(1)}, u32[]{:S(2)}, u32[]{:S(2)}) collective-permute-start(bf16[1024,512]{1,0:T(8,128)(2,1)S(1)} %pad_maximum_fusion.1.refs_4_), channel_id=1, source_target_pairs={{0,24},{1,25},{2,26},{3,27},{4,100},{5,101},{6,102},{7,103},{8,0},... | collective-permute-start | bytes 3145736 | tf_op jit(solution)/shard_map/ppermute | solution.py:42
  93.5 34.3 %collective-permute-start.23 = (bf16[1024,512]{1,0:T(8,128)(2,1)S(1)}, bf16[1024,512]{1,0:T(8,128)(2,1)S(1)}, u32[]{:S(2)}, u32[]{:S(2)}) collective-permute-start(bf16[1024,512]{1,0:T(8,128)(2,1)S(1)} %pad_maximum_fusion.1.refs_4_), channel_id=1, source_target_pairs={{0,16},{1,17},{2,18},{3,19},{4,68},{5,69},{6,70},{7,71},{8,24},{9,... | collective-permute-start | bytes 3145736 | tf_op jit(solution)/shard_map/ppermute | solution.py:42
  95.0 16.9 %collective-permute-start.16 = (bf16[512,512]{1,0:T(8,128)(2,1)S(1)}, bf16[512,512]{1,0:T(8,128)(2,1)S(1)}, u32[]{:S(2)}, u32[]{:S(2)}) collective-permute-start(bf16[512,512]{1,0:T(8,128)(2,1)S(1)} %pad_maximum_fusion.2.refs_0_), channel_id=1, source_target_pairs={{0,2},{1,3},{2,0},{3,1},{4,6},{5,7},{6,4},{7,5},{8,10},{9,11},{10,... | collective-permute-start | bytes 1572872 | tf_op jit(solution)/shard_map/ppermute | solution.py:33
  112.0 13.1 %collective-permute-start.15 = (bf16[512,512]{1,0:T(8,128)(2,1)S(1)}, bf16[512,512]{1,0:T(8,128)(2,1)S(1)}, u32[]{:S(2)}, u32[]{:S(2)}) collective-permute-start(bf16[512,512]{1,0:T(8,128)(2,1)S(1)} %pad_maximum_fusion.2.refs_0_), channel_id=1, source_target_pairs={{0,3},{1,0},{2,1},{3,2},{4,7},{5,4},{6,5},{7,6},{8,11},{9,8},{10,9... | collective-permute-start | bytes 1572872 | tf_op jit(solution)/shard_map/ppermute | solution.py:33
  129.6 7.8 %collective-permute-start.28 = (bf16[256,512]{1,0:T(8,128)(2,1)S(1)}, bf16[256,512]{1,0:T(8,128)(2,1)S(1)}, u32[]{:S(2)}, u32[]{:S(2)}) collective-permute-start(bf16[256,512]{1,0:T(8,128)(2,1)S(1)} %get-tuple-element.40.refs_0_), channel_id=1, source_target_pairs={{0,1},{1,2},{2,3},{3,0},{4,5},{5,6},{6,7},{7,4},{8,9},{9,10},{10,1... | collective-permute-start | bytes 786440 | tf_op jit(solution)/shard_map/ppermute | solution.py:33
  129.7 13.7 %collective-permute-start.26 = (bf16[256,512]{1,0:T(8,128)(2,1)S(1)}, bf16[256,512]{1,0:T(8,128)(2,1)S(1)}, u32[]{:S(2)}, u32[]{:S(2)}) collective-permute-start(bf16[256,512]{1,0:T(8,128)(2,1)S(1)} %get-tuple-element.40.refs_0_), channel_id=1, source_target_pairs={{0,2},{1,3},{2,0},{3,1},{4,6},{5,7},{6,4},{7,5},{8,10},{9,11},{10,... | collective-permute-start | bytes 786440 | tf_op jit(solution)/shard_map/ppermute | solution.py:33
  132.4 12.9 %collective-permute-start.24 = (bf16[256,512]{1,0:T(8,128)(2,1)S(1)}, bf16[256,512]{1,0:T(8,128)(2,1)S(1)}, u32[]{:S(2)}, u32[]{:S(2)}) collective-permute-start(bf16[256,512]{1,0:T(8,128)(2,1)S(1)} %get-tuple-element.40.refs_0_), channel_id=1, source_target_pairs={{0,3},{1,0},{2,1},{3,2},{4,7},{5,4},{6,5},{7,6},{8,11},{9,8},{10,9... | collective-permute-start | bytes 786440 | tf_op jit(solution)/shard_map/ppermute | solution.py:33
  132.4 13.5 %collective-permute-start.30 = (bf16[256,512]{1,0:T(8,128)(2,1)S(1)}, bf16[256,512]{1,0:T(8,128)(2,1)S(1)}, u32[]{:S(2)}, u32[]{:S(2)}) collective-permute-start(bf16[256,512]{1,0:T(8,128)(2,1)S(1)} %get-tuple-element.40.refs_0_), channel_id=1, source_target_pairs={{0,4},{1,5},{2,6},{3,7},{4,0},{5,1},{6,2},{7,3},{8,12},{9,13},{10,... | collective-permute-start | bytes 786440 | tf_op jit(solution)/shard_map/ppermute | solution.py:29
  137.4 9.9 %collective-permute-start.29 = (bf16[256,512]{1,0:T(8,128)(2,1)S(1)}, bf16[256,512]{1,0:T(8,128)(2,1)S(1)}, u32[]{:S(2)}, u32[]{:S(2)}) collective-permute-start(bf16[256,512]{1,0:T(8,128)(2,1)S(1)} %collective-permute-done.28.refs_3_), channel_id=1, source_target_pairs={{0,4},{1,5},{2,6},{3,7},{4,0},{5,1},{6,2},{7,3},{8,12},{9,13},{10,... | collective-permute-start | bytes 786440 | tf_op jit(solution)/shard_map/ppermute | solution.py:29
  143.4 3.9 %collective-permute-start.27 = (bf16[256,512]{1,0:T(8,128)(2,1)S(1)}, bf16[256,512]{1,0:T(8,128)(2,1)S(1)}, u32[]{:S(2)}, u32[]{:S(2)}) collective-permute-start(bf16[256,512]{1,0:T(8,128)(2,1)S(1)} %collective-permute-done.26.refs_2_), channel_id=1, source_target_pairs={{0,4},{1,5},{2,6},{3,7},{4,0},{5,1},{6,2},{7,3},{8,12},{9,13},{10,... | collective-permute-start | bytes 786440 | tf_op jit(solution)/shard_map/ppermute | solution.py:29
  145.3 2.0 %collective-permute-start.25 = (bf16[256,512]{1,0:T(8,128)(2,1)S(1)}, bf16[256,512]{1,0:T(8,128)(2,1)S(1)}, u32[]{:S(2)}, u32[]{:S(2)}) collective-permute-start(bf16[256,512]{1,0:T(8,128)(2,1)S(1)} %collective-permute-done.24.refs_1_), channel_id=1, source_target_pairs={{0,4},{1,5},{2,6},{3,7},{4,0},{5,1},{6,2},{7,3},{8,12},{9,13},{10,... | collective-permute-start | bytes 786440 | tf_op jit(solution)/shard_map/ppermute | solution.py:29
  148.4 1.6 %collective-permute-start.31 = (f32[128,512]{1,0:T(8,128)S(1)}, f32[128,512]{1,0:T(8,128)S(1)}, u32[]{:S(2)}, u32[]{:S(2)}) collective-permute-start(f32[128,512]{1,0:T(8,128)S(1)} %get-tuple-element.44), channel_id=1, source_target_pairs={{0,4},{1,5},{2,6},{3,7},{4,0},{5,1},{6,2},{7,3},{8,12},{9,13},{10,... | collective-permute-start | bytes 786440 | tf_op jit(solution)/shard_map/ppermute | solution.py:29

commit v6 on v5

--- a/solution.py
+++ b/solution.py
@@ -1,3 +1,5 @@
+import functools
+
 import jax
 import jax.numpy as jnp
 from jax import lax
@@ -71,69 +73,85 @@
     return px * 8 + py * 2 + kind
 
 
-def some_rows(where, keep_d, own, other, ns, line):
-    x, y, core = where[0], where[1], where[2]
-    mine, its = own[0][:B, :], other[0][:B, :]
-    rows = jnp.concatenate([jnp.where(core == 0, mine, its), jnp.where(core == 0, its, mine)], axis=0)
-    for half, (parts, kind) in enumerate(((own, core), (other, 1 - core))):
-        for n in ns:
-            value = dot_t(rows, parts[n][...])
-            for u in range(4):
-                block = block_at(x, y, kind, n * 4 + u)
-                at = (half * 16 + n * 4 + u) * B
-                for t in range(2):
-                    keep = keep_d[0, (x * 4 + y) * 2 + t, block].astype(jnp.float32)
-                    piece = value[t * B:(t + 1) * B, u * B:(u + 1) * B] * keep
-                    line[t * B:(t + 1) * B, at:at + B] = piece.astype(jnp.bfloat16)
-
-
-def some_columns(where, keep_d, parts, half, n, m, column, panel):
+def some_rows(where, keep_d, rows, half, parts, line):
     x, y, core = where[0], where[1], where[2]
     kind = core if half == 0 else 1 - core
-    value = dot_t(parts[n][...], column[...])
-    for i in range(4):
-        row_block = block_at(x, y, kind, n * 4 + i)
-        at = (half * 16 + n * 4 + i) * B
+    for n, part in parts.items():
+        value = dot_t(rows[...], part[...])
         for u in range(4):
-            keep = keep_d[0, row_block, block_at(x, y, core, m * 4 + u)].astype(jnp.float32)
-            piece = value[i * B:(i + 1) * B, u * B:(u + 1) * B] * keep
-            to = (m * 4 + u) * B
-            panel[at:at + B, to:to + B] = piece.astype(jnp.bfloat16)
+            block = block_at(x, y, kind, n * 4 + u)
+            at = (half * 16 + n * 4 + u) * B
+            for t in range(2):
+                keep = keep_d[0, (x * 4 + y) * 2 + t, block].astype(jnp.float32)
+                piece = value[t * B:(t + 1) * B, u * B:(u + 1) * B] * keep
+                line[t * B:(t + 1) * B, at:at + B] = piece.astype(jnp.bfloat16)
+
+
+def some_columns(where, keep_d, half, parts, columns, panel, skip=()):
+    x, y, core = where[0], where[1], where[2]
+    kind = core if half == 0 else 1 - core
+    for n, part in parts.items():
+        for m, column in columns.items():
+            if (n, m) in skip:
+                continue
+            value = dot_t(part[...], column[...])
+            for i in range(4):
+                row_block = block_at(x, y, kind, n * 4 + i)
+                at = (half * 16 + n * 4 + i) * B
+                for u in range(4):
+                    keep = keep_d[0, row_block, block_at(x, y, core, m * 4 + u)].astype(jnp.float32)
+                    piece = value[i * B:(i + 1) * B, u * B:(u + 1) * B] * keep
+                    to = (m * 4 + u) * B
+                    panel[at:at + B, to:to + B] = piece.astype(jnp.bfloat16)
 
 
 EARLY = (0, 1, 3)
 
 
-def early_density(where, keep_d, own0, own1, own3, other0, other1, other3, panel, line):
-    own, other = {0: own0, 1: own1, 3: own3}, {0: other0, 1: other1, 3: other3}
-    some_rows(where, keep_d, own, other, EARLY, line)
-    for half, parts in enumerate((own, other)):
-        for n in EARLY:
-            for m in EARLY:
-                some_columns(where, keep_d, parts, half, n, m, own[m], panel)
-
-
-def first_square(where, keep_d, keep_s, *refs):
-    own, other, (panel, line, low, square, total) = refs[:4], refs[4:8], refs[10:]
+def density_0(where, keep_d, own0, other0, panel, line, rows):
+    first = where[2] == 0
+    mine, its = own0[:B, :], other0[:B, :]
+    rows[:B, :] = jnp.where(first, mine, its)
+    rows[B:, :] = jnp.where(first, its, mine)
+    for half, part in enumerate((own0, other0)):
+        some_rows(where, keep_d, rows, half, {0: part}, line)
+        some_columns(where, keep_d, half, {0: part}, {0: own0}, panel)
+
+
+def density_1(where, keep_d, own0, own1, own3, other0, rows, _, __, panel, line):
+    own = {0: own0, 1: own1, 3: own3}
+    some_rows(where, keep_d, rows, 0, {1: own1, 3: own3}, line)
+    some_columns(where, keep_d, 0, own, own, panel, ((0, 0),))
+    some_columns(where, keep_d, 1, {0: other0}, {1: own1, 3: own3}, panel)
+
+
+def density_2(where, keep_d, own0, own1, own2, own3, other0, rows, _, __, panel, line):
+    some_rows(where, keep_d, rows, 0, {2: own2}, line)
+    some_columns(where, keep_d, 0, {2: own2}, {0: own0, 1: own1, 2: own2, 3: own3}, panel)
+    some_columns(where, keep_d, 0, {0: own0, 1: own1, 3: own3}, {2: own2}, panel)
+    some_columns(where, keep_d, 1, {0: other0}, {2: own2}, panel)
+
+
+def density_3(where, keep_d, own0, own1, own2, own3, other1, other3, rows, _, __, panel, line):
+    other = {1: other1, 3: other3}
+    some_rows(where, keep_d, rows, 1, other, line)
+    some_columns(where, keep_d, 1, other, {0: own0, 1: own1, 2: own2, 3: own3}, panel)
+
+
+def first_square(where, keep_d, keep_s, own0, own1, own2, own3, other2, rows, _, __, panel, line, low, square, total):
     x, y, core, z = where[0], where[1], where[2], where[3]
-    some_rows(where, keep_d, own, other, (2,), line)
-    for half, parts in enumerate((own, other)):
-        for n in range(4):
-            for m in range(4):
-                if n == 2 or m == 2:
-                    some_columns(where, keep_d, parts, half, n, m, own[m], panel)
-
-    @pl.loop(0, 8)
-    def _(part):
-        at = aligned(part, 256)
-        value = dot(line[...], panel[:, at])
+    some_rows(where, keep_d, rows, 1, {2: other2}, line)
+    some_columns(where, keep_d, 1, {2: other2}, {0: own0, 1: own1, 2: own2, 3: own3}, panel)
+    for half in range(2):
+        value = dot(line[...], panel[:, half * 1024:(half + 1) * 1024])
         for t in range(2):
-            for u in range(2):
-                block = block_at(x, y, core, part * 2 + u)
+            for u in range(8):
+                block = block_at(x, y, core, half * 8 + u)
                 keep = keep_s[0, (x * 4 + y) * 2 + t, block].astype(jnp.float32)
                 piece = value[t * B:(t + 1) * B, u * B:(u + 1) * B] * keep
-                total[t * B:(t + 1) * B, aligned(part * 2 + u, B)] = piece
-                low[t * B:(t + 1) * B, aligned(part * 2 + u, B)] = piece.astype(jnp.bfloat16)
+                at = (half * 8 + u) * B
+                total[t * B:(t + 1) * B, at:at + B] = piece
+                low[t * B:(t + 1) * B, at:at + B] = piece.astype(jnp.bfloat16)
     for t in range(4):
         square[:, t * B:(t + 1) * B] = total[:, aligned(column_at(where, t), B)]
 
@@ -175,12 +193,6 @@
     core, z = where[2], where[3]
     parts = [(own[d], d, core) for d in range(4)] + [(other, 0, 1 - core)]
     out[...] = parts_times_panel(parts, z, panel)
-
-
-def late_cube(where, others, early, panel):
-    core, z = where[2], where[3]
-    parts = [(others[d - 1], d, 1 - core) for d in (1, 2, 3)]
-    return early[...] + parts_times_panel(parts, z, panel)
 
 
 def chips_times(where, line, chips, panel, sems):
@@ -201,23 +213,24 @@
 
 
 def early_square(where, *refs):
-    both, parts, (early, line, panel), (sems,) = refs[:4], refs[4:7], refs[7:10], refs[10:]
+    own, other, near, far, (early, line, panel), (sems,) = (
+        refs[:4], refs[4:8], refs[8], refs[9:13], refs[13:16], refs[16:])
     core, z = where[2], where[3]
     for d in range(4):
-        for half, kind in enumerate((core, 1 - core)):
+        for ref, kind in ((own[d], core), (other[d], 1 - core)):
             for t in range(4):
-                line[:, aligned(((z + d) & 3) * 8 + t * 2 + kind, B)] = (
-                    both[d][half * ROWS:(half + 1) * ROWS, t * B:(t + 1) * B])
-    chips = [(parts[n], i * ROWS, i, EARLY[n]) for n in range(3) for i in range(4)]
+                line[:, aligned(((z + d) & 3) * 8 + t * 2 + kind, B)] = ref[:, t * B:(t + 1) * B]
+    chips = [(near, i * ROWS, i, 0) for i in range(4)] + [(far[i], 0, i, 2) for i in range(4)]
     value, copies = chips_times(where, line, chips, panel, sems)
     early[...] = value
     for copy in copies:
         copy.wait()
 
 
-def second_square(where, keep_s, two, early, line, _, square, low, panel, sems):
+def second_square(where, keep_s, one, three, early, line, _, square, low, panel, sems):
     x, y, core, z = where[0], where[1], where[2], where[3]
-    value, copies = chips_times(where, line, [(two, i * ROWS, i, 2) for i in range(4)], panel, sems)
+    chips = [(ref, i * ROWS, i, j) for ref, j in ((one, 1), (three, 3)) for i in range(4)]
+    value, copies = chips_times(where, line, chips, panel, sems)
     value = early[...] + value
     for t in range(2):
         for u in range(4):
@@ -229,18 +242,21 @@
         copy.wait()
 
 
-def second_density(where, *refs):
-    others, (early, square, panel, stay, leave) = refs[:3], refs[3:]
-    value = 3.0 * square[...] - 2.0 * late_cube(where, others, early, panel)
-    first = where[2] == 0
-    stay[...] = jnp.where(first, value[:B], value[B:])
-    leave[...] = jnp.where(first, value[B:], value[:B])
-
-
-def join(where, stay, come, out):
-    first = where[2] == 0
+def second_density(leave, where, *refs):
+    others, (early, square, panel), (come, out) = refs[:3], refs[3:6], (refs[6:] if not leave else (None,) + refs[6:])
+    core, z = where[2], where[3]
+    at = aligned(1 - core if leave else core, B)
+    total = early[at, :]
+    for d in (1, 2, 3):
+        rows = [panel[aligned(((z + d) & 3) * 8 + t * 2 + 1 - core, B), :] for t in range(4)]
+        total = total + dot(others[d - 1][at, :], jnp.concatenate(rows, axis=0))
+    value = 3.0 * square[at, :] - 2.0 * total
+    if leave:
+        out[...] = value
+        return
+    first = core == 0
     for t in range(4):
-        mine, its = stay[:, t * B:(t + 1) * B], come[:, t * B:(t + 1) * B]
+        mine, its = value[:, t * B:(t + 1) * B], come[:, t * B:(t + 1) * B]
         out[:, 2 * t * B:(2 * t + 1) * B] = jnp.where(first, mine, its)
         out[:, (2 * t + 1) * B:(2 * t + 2) * B] = jnp.where(first, its, mine)
 
@@ -281,18 +297,30 @@
     kept = kept * jnp.repeat(pattern, B, 1).astype(jnp.bfloat16)
     near = jnp.concatenate(gather(kept, from_first), axis=0)
     own0, own1, own2, own3 = gather(near, from_second)
-    other0, other1, other3 = other_core(own0), other_core(own1), other_core(own3)
+    other0 = other_core(own0)
+    rows_shape = jax.ShapeDtypeStruct((ROWS, K), jnp.bfloat16)
+    out_shapes = [wide_shape, line_shape]
+    panel, line, rows = call(
+        density_0, 2, [where, keep_density, own0, other0], out_shapes + [rows_shape], [], pair_flops // 8, MIB)
+    panel, line, own1, own3 = lax.optimization_barrier((panel, line, own1, own3))
+    other1, other3 = other_core(own1), other_core(own3)
     panel, line = call(
-        early_density, 2, [where, keep_density, own0, own1, own3, other0, other1, other3],
-        [wide_shape, line_shape], [], 2 * pair_flops, 2 * MIB)
+        density_1, 2, [where, keep_density, own0, own1, own3, other0, rows, panel, line],
+        out_shapes, [], pair_flops // 8, MIB, {7: 0, 8: 1})
     panel, line, own2 = lax.optimization_barrier((panel, line, own2))
     other2 = other_core(own2)
+    panel, line = call(
+        density_2, 2, [where, keep_density, own0, own1, own2, own3, other0, rows, panel, line],
+        out_shapes, [], 9 * pair_flops, 8 * MIB, {8: 0, 9: 1})
+    panel, line = call(
+        density_3, 2, [where, keep_density, own0, own1, own2, own3, other1, other3, rows, panel, line],
+        out_shapes, [], 9 * pair_flops, 8 * MIB, {9: 0, 10: 1})
     panel, line, low, square = call(
         first_square, 3,
-        [where, keep_density, keep_square, own0, own1, own2, own3, other0, other1, other2, other3, panel, line],
-        [wide_shape, line_shape, jax.ShapeDtypeStruct((ROWS, N // 2), jnp.bfloat16), full_block],
+        [where, keep_density, keep_square, own0, own1, own2, own3, other2, rows, panel, line],
+        out_shapes + [jax.ShapeDtypeStruct((ROWS, N // 2), jnp.bfloat16), full_block],
         [pltpu.VMEM((ROWS, N // 2), jnp.float32)],
-        15 * pair_flops + 4 * block_flops, 40 * MIB, {11: 0, 12: 1})
+        4 * pair_flops + 4 * block_flops, 20 * MIB, {9: 0, 10: 1})
 
     its = other_core(low)
     early, columns = call(
@@ -301,29 +329,34 @@
         first_density, 2, [where, keep_density, its, columns, early, square], [low_block], [],
         block_flops // 2, 4 * MIB)
 
-    near = jnp.concatenate(gather(current, from_first), axis=0)
-    part0, part1, part2, part3 = gather(near, from_second)
-    both = gather(jnp.concatenate([current, other_core(current)], axis=0), from_z)
+    near = gather(current, from_first)
+    far = from_second(current, 2)
+    own = gather(current, from_z)
+    current, far, own1, own2, own3 = lax.optimization_barrier((current, far, *own[1:]))
+    near = jnp.concatenate(near, axis=0)
+    one, three = from_second(near, 1), from_second(near, 3)
+    far = gather(far, from_first)
+    own = [current, own1, own2, own3]
+    other = [other_core(part) for part in own]
     early, line, panel = call(
-        early_square, 1, [where, *both, part0, part1, part3], [full_block, line_shape, panel_shape],
-        [pltpu.SemaphoreType.DMA((12,))], block_flops * 3 // 4, 12 * MIB)
-    early, part2 = lax.optimization_barrier((early, part2))
+        early_square, 1, [where, *own, *other, near, *far], [full_block, line_shape, panel_shape],
+        [pltpu.SemaphoreType.DMA((8,))], block_flops // 2, 10 * MIB)
     square, low, panel = call(
-        second_square, 2, [where, keep_square, part2, early, line, panel],
+        second_square, 2, [where, keep_square, one, three, early, line, panel],
         [full_block, low_block, panel_shape],
-        [pltpu.SemaphoreType.DMA((4,))], block_flops // 4, 6 * MIB, {5: 2})
+        [pltpu.SemaphoreType.DMA((8,))], block_flops // 2, 8 * MIB, {6: 2})
 
     own = gather(low, from_z)
     other = [other_core(part) for part in own]
     (early,) = call(
         early_cube, 1, [where, *own, other[0], panel], [full_block], [], block_flops * 5 // 8, 4 * MIB)
-    half = jax.ShapeDtypeStruct((B, COLS), jnp.float32)
-    stay, leave = call(
-        second_density, 1, [where, *other[1:], early, square, panel], [half, half], [],
-        block_flops * 3 // 8, 3 * MIB)
-    come = other_core(leave)
+    last = [*other[1:], early, square, panel]
+    (leave,) = call(
+        functools.partial(second_density, True), 1, [where, *last],
+        [jax.ShapeDtypeStruct((B, COLS), jnp.float32)], [], block_flops * 3 // 16, 3 * MIB)
     (out,) = call(
-        join, 1, [where, stay, come], [jax.ShapeDtypeStruct((B, 2 * COLS), jnp.float32)], [], 0, MIB)
+        functools.partial(second_density, False), 1, [where, *last, other_core(leave)],
+        [jax.ShapeDtypeStruct((B, 2 * COLS), jnp.float32)], [], block_flops * 3 // 16, 3 * MIB)
     return out
 
 

time: 152 us -> 167 us (1.099)
  the two profiles are of different devices: /device:TPU:5 before, /device:TPU:1 now
where the time goes in v6:
time: 167 us; the launch traced here: 164 us
  waiting for transfers between devices  73.4 us (44%)
  Pallas kernels  54.9 us (33%)
  starting transfers between devices  33.3 us (20%)
    pallas_call x12, Pallas kernels, call(): pl.pallas_call(kernel, in_specs=[SMEM] * n_smem + [VMEM] * (len(ins) - n_...  54.9 us
    ppermute x9, waiting for transfers between devices, from_first(): lax.ppermute(a, AXES, pairs(lambda x, y, core, z: (x - d, y, core, z) if...  27.5 us
    ppermute x6, waiting for transfers between devices, from_second(): lax.ppermute(a, AXES, pairs(lambda x, y, core, z: (x, y - d, core, z) if...  21.3 us
    ppermute x9, waiting for transfers between devices, from_z(): lax.ppermute(a, AXES, pairs(lambda x, y, core, z: (x, y, core, z - d)))  20.7 us
    ppermute x14, starting transfers between devices, other_core(): lax.ppermute(a, AXES, pairs(lambda x, y, core, z: (x, y, 1 - core, z)))  13.9 us
    ppermute x9, starting transfers between devices, from_z(): lax.ppermute(a, AXES, pairs(lambda x, y, core, z: (x, y, core, z - d)))  9.48 us
    ppermute x9, starting transfers between devices, from_first(): lax.ppermute(a, AXES, pairs(lambda x, y, core, z: (x - d, y, core, z) if...  5.86 us
    ppermute x6, starting transfers between devices, from_second(): lax.ppermute(a, AXES, pairs(lambda x, y, core, z: (x, y - d, core, z) if...  4.03 us
  transfers between devices with their start and end apart: 38, of which 22 were waited for; matrix products, arithmetic and copies ran while one was open for 1% of the time, Pallas kernels for 18%

profile of v6, /device:TPU:1, one launch (start us, length us, event | category | flops | bytes accessed | tf_op | source)
XLA Modules:
  0.0 163.9 jit_solution(14563548815488305214)
XLA Ops:
  0.0 4.6 %collective-permute-start = (bf16[128,256]{1,0:T(8,128)(2,1)}, bf16[128,256]{1,0:T(8,128)(2,1)S(1)}, u32[]{:S(2)}, u32[]{:S(2)}) collective-permute-start(bf16[128,256]{1,0:T(8,128)(2,1)} %param.4), channel_id=1, source_target_pairs={{0,3},{1,0},{2,1},{3,2},{4,7},{5,4},{6,5},{7,6},{8,11},{9,8},{10,9... | collective-permute-start | bytes 196616 | tf_op jit(solution)/shard_map/ppermute | solution.py:35
  4.6 0.7 collective-permute-start.2
  6.1 0.8 collective-permute-done
  6.9 2.7 %collective-permute-done.1 = bf16[128,256]{1,0:T(8,128)(2,1)S(1)} collective-permute-done((bf16[128,256]{1,0:T(8,128)(2,1)}, bf16[128,256]{1,0:T(8,128)(2,1)S(1)}, u32[]{:S(2)}, u32[]{:S(2)}) %collective-permute-start.1) | collective-permute-done | bytes 65568 | tf_op jit(solution)/shard_map/ppermute | solution.py:35
  9.8 0.9 maximum_multiply_fusion
  10.7 2.8 %collective-permute-start.3 = (bf16[128,1024]{1,0:T(8,128)(2,1)S(1)}, bf16[128,1024]{1,0:T(8,128)(2,1)S(1)}, u32[]{:S(2)}, u32[]{:S(2)}) collective-permute-start(bf16[128,1024]{1,0:T(8,128)(2,1)S(1)} %maximum_multiply_fusion), channel_id=1, source_target_pairs={{0,96},{1,97},{2,98},{3,99},{4,28},{5,29},{6,30},{7,31},{8,104},{9... | collective-permute-start | bytes 786440 | tf_op jit(solution)/shard_map/ppermute | solution.py:39
  13.9 0.7 collective-permute-start.5
  14.6 5.1 %collective-permute-done.3 = bf16[128,1024]{1,0:T(8,128)(2,1)S(1)} collective-permute-done((bf16[128,1024]{1,0:T(8,128)(2,1)S(1)}, bf16[128,1024]{1,0:T(8,128)(2,1)S(1)}, u32[]{:S(2)}, u32[]{:S(2)}) %collective-permute-start.3) | collective-permute-done | bytes 262176 | tf_op jit(solution)/shard_map/ppermute | solution.py:39
  19.7 0.9 collective-permute-done.4
  20.6 2.8 %collective-permute-done.5 = bf16[128,1024]{1,0:T(8,128)(2,1)S(1)} collective-permute-done((bf16[128,1024]{1,0:T(8,128)(2,1)S(1)}, bf16[128,1024]{1,0:T(8,128)(2,1)S(1)}, u32[]{:S(2)}, u32[]{:S(2)}) %collective-permute-start.5) | collective-permute-done | bytes 262176 | tf_op jit(solution)/shard_map/ppermute | solution.py:39
  23.4 3.1 %collective-permute-start.6 = (bf16[512,1024]{1,0:T(8,128)(2,1)S(1)}, bf16[512,1024]{1,0:T(8,128)(2,1)}, u32[]{:S(2)}, u32[]{:S(2)}) collective-permute-start(bf16[512,1024]{1,0:T(8,128)(2,1)S(1)} %pad_maximum_fusion.own0), channel_id=1, source_target_pairs={{0,4},{1,5},{2,6},{3,7},{4,0},{5,1},{6,2},{7,3},{8,12},{9,13},{10,... | collective-permute-start | bytes 3145736 | tf_op jit(solution)/shard_map/ppermute | solution.py:31
  26.8 1.1 collective-permute-start.8
  28.9 3.1 %shard_map.46 = (bf16[4096,2048]{1,0:T(8,128)(2,1)S(1)}, bf16[256,4096]{1,0:T(8,128)(2,1)S(1)}, bf16[256,1024]{1,0:T(8,128)(2,1)S(1)}) custom-call(s32[4]{0:T(128)S(1)} %pad_add_fusion.1.where, s32[2,32,32]{2,1,0:T(8,128)S(1)} %copy-done.1, bf16[512,1024]{1,0:T(8,128)(2,1)S(1)} %pad_maximum_fusion.own0, bf16[512,1024]{1,0:T(8,128)(2,1)} %collective-permute-done.6.other0), custom_call_target="tpu_custom_call" | custom-call | flops 67108864 | bytes 1048576 | tf_op jit(solution)/shard_map/pallas_call | solution.py:269
  32.0 8.4 %collective-permute-done.7.own1 = bf16[512,1024]{1,0:T(8,128)(2,1)S(1)} collective-permute-done((bf16[512,1024]{1,0:T(8,128)(2,1)S(1)}, bf16[512,1024]{1,0:T(8,128)(2,1)S(1)}, u32[]{:S(2)}, u32[]{:S(2)}) %collective-permute-start.7) | collective-permute-done | bytes 1048608 | tf_op jit(solution)/shard_map/ppermute | solution.py:44
  40.4 12.9 %collective-permute-done.8.own3 = bf16[512,1024]{1,0:T(8,128)(2,1)S(1)} collective-permute-done((bf16[512,1024]{1,0:T(8,128)(2,1)S(1)}, bf16[512,1024]{1,0:T(8,128)(2,1)S(1)}, u32[]{:S(2)}, u32[]{:S(2)}) %collective-permute-start.8) | collective-permute-done | bytes 1048608 | tf_op jit(solution)/shard_map/ppermute | solution.py:44
  53.3 3.5 %collective-permute-start.11 = (bf16[512,1024]{1,0:T(8,128)(2,1)S(1)}, bf16[512,1024]{1,0:T(8,128)(2,1)S(1)}, u32[]{:S(2)}, u32[]{:S(2)}) collective-permute-start(bf16[512,1024]{1,0:T(8,128)(2,1)S(1)} %collective-permute-done.7.own1), channel_id=1, source_target_pairs={{0,4},{1,5},{2,6},{3,7},{4,0},{5,1},{6,2},{7,3},{8,12},{9,13},{10,... | collective-permute-start | bytes 3145736 | tf_op jit(solution)/shard_map/ppermute | solution.py:31
  56.8 7.4 %shard_map.47 = (bf16[4096,2048]{1,0:T(8,128)(2,1)S(1)}, bf16[256,4096]{1,0:T(8,128)(2,1)S(1)}) custom-call(s32[4]{0:T(128)S(1)} %pad_add_fusion.1.where, s32[2,32,32]{2,1,0:T(8,128)S(1)} %copy-done.1, bf16[512,1024]{1,0:T(8,128)(2,1)S(1)} %pad_maximum_fusion.own0, ...), custom_call_target="tpu_custom_call", output_to_operand_aliasing={{0}: (7, {}), {1}: (8, {})} | custom-call | flops 67108864 | bytes 1048576 | tf_op jit(solution)/shard_map/pallas_call | solution.py:269
  64.3 0.8 collective-permute-start.10
  65.1 6.4 %shard_map.48 = (bf16[4096,2048]{1,0:T(8,128)(2,1)S(1)}, bf16[256,4096]{1,0:T(8,128)(2,1)S(1)}) custom-call(s32[4]{0:T(128)S(1)} %pad_add_fusion.1.where, s32[2,32,32]{2,1,0:T(8,128)S(1)} %copy-done.1, bf16[512,1024]{1,0:T(8,128)(2,1)S(1)} %pad_maximum_fusion.own0, ...), custom_call_target="tpu_custom_call", output_to_operand_aliasing={{0}: (8, {}), {1}: (9, {})} | custom-call | flops 4831838208 | bytes 8388608 | tf_op jit(solution)/shard_map/pallas_call | solution.py:269
  71.5 6.3 %shard_map.49 = (bf16[4096,2048]{1,0:T(8,128)(2,1)S(1)}, bf16[256,4096]{1,0:T(8,128)(2,1)S(1)}) custom-call(s32[4]{0:T(128)S(1)} %pad_add_fusion.1.where, s32[2,32,32]{2,1,0:T(8,128)S(1)} %copy-done.1, bf16[512,1024]{1,0:T(8,128)(2,1)S(1)} %pad_maximum_fusion.own0, ...), custom_call_target="tpu_custom_call", output_to_operand_aliasing={{0}: (9, {}), {1}: (10, {})} | custom-call | flops 4831838208 | bytes 8388608 | tf_op jit(solution)/shard_map/pallas_call | solution.py:269
  77.9 19.0 %shard_map.50 = (bf16[4096,2048]{1,0:T(8,128)(2,1)S(1)}, bf16[256,4096]{1,0:T(8,128)(2,1)S(1)}, bf16[256,2048]{1,0:T(8,128)(2,1)S(1)}, f32[256,512]{1,0:T(8,128)S(1)}) custom-call(s32[4]{0:T(128)S(1)} %pad_add_fusion.1.where, s32[2,32,32]{2,1,0:T(8,128)S(1)} %copy-done.1, s32[2,32,32]{2,1,0:T(8,128)S(1)} %copy-done.2, ...), custom_call_target="tpu_custom_call", output_to_operand_aliasing={{0}: (9, {}), {1}: (10, {})} | custom-call | flops 6442450944 | bytes 20971520 | tf_op jit(solution)/shard_map/pallas_call | solution.py:269
  97.0 2.3 %shard_map.51 = (f32[256,512]{1,0:T(8,128)S(1)}, bf16[4096,512]{1,0:T(8,128)(2,1)S(1)}) custom-call(s32[4]{0:T(128)S(1)} %pad_add_fusion.1.where, bf16[256,2048]{1,0:T(8,128)(2,1)S(1)} %get-tuple-element.53.low, bf16[4096,2048]{1,0:T(8,128)(2,1)S(1)} %get-tuple-element.54.panel), custom_call_target="tpu_custom_call" | custom-call | flops 536870912 | bytes 12582912 | tf_op jit(solution)/shard_map/pallas_call | solution.py:269
  99.7 1.8 %shard_map.52.refs_0_ = bf16[256,512]{1,0:T(8,128)(2,1)S(1)} custom-call(s32[4]{0:T(128)S(1)} %pad_add_fusion.1.where, s32[2,32,32]{2,1,0:T(8,128)S(1)} %copy-done.1, bf16[256,2048]{1,0:T(8,128)(2,1)S(1)} %collective-permute-done.13.its, bf16[4096,512]{1,0:T(8,128)(2,1)S(1)} %get-tuple-element.55.columns, f32[256,512]{1,0:T(8,128)S(1)} %get-tuple-element.56.early, ...), custom_call_target="tpu_custom_call" | custom-call | flops 536870912 | bytes 4194304 | tf_op jit(solution)/shard_map/pallas_call | solution.py:269
  101.7 1.4 collective-permute-start.16
  104.1 4.0 %collective-permute-done.14 = bf16[256,512]{1,0:T(8,128)(2,1)S(1)} collective-permute-done((bf16[256,512]{1,0:T(8,128)(2,1)S(1)}, bf16[256,512]{1,0:T(8,128)(2,1)S(1)}, u32[]{:S(2)}, u32[]{:S(2)}) %collective-permute-start.14) | collective-permute-done | bytes 262176 | tf_op jit(solution)/shard_map/ppermute | solution.py:39
  108.1 1.3 collective-permute-start.21
  109.5 4.8 %collective-permute-done.16 = bf16[256,512]{1,0:T(8,128)(2,1)S(1)} collective-permute-done((bf16[256,512]{1,0:T(8,128)(2,1)S(1)}, bf16[256,512]{1,0:T(8,128)(2,1)S(1)}, u32[]{:S(2)}, u32[]{:S(2)}) %collective-permute-start.16) | collective-permute-done | bytes 262176 | tf_op jit(solution)/shard_map/ppermute | solution.py:39
  114.4 1.4 collective-permute-start.18
  115.9 6.5 %collective-permute-done.22.refs_3_ = bf16[256,512]{1,0:T(8,128)(2,1)S(1)} collective-permute-done((bf16[256,512]{1,0:T(8,128)(2,1)S(1)}, bf16[256,512]{1,0:T(8,128)(2,1)S(1)}, u32[]{:S(2)}, u32[]{:S(2)}) %collective-permute-start.22) | collective-permute-done | bytes 262176 | tf_op jit(solution)/shard_map/ppermute | solution.py:35
  122.4 1.5 collective-permute-start.23
  124.5 0.7 collective-permute-done.23.refs_4_
  125.9 0.8 collective-permute-done.26.refs_7_
  127.1 6.1 %collective-permute-done.27.refs_10_ = bf16[256,512]{1,0:T(8,128)(2,1)S(1)} collective-permute-done((bf16[256,512]{1,0:T(8,128)(2,1)S(1)}, bf16[256,512]{1,0:T(8,128)(2,1)S(1)}, u32[]{:S(2)}, u32[]{:S(2)}) %collective-permute-start.27) | collective-permute-done | bytes 262176 | tf_op jit(solution)/shard_map/ppermute | solution.py:39
  133.1 3.8 %collective-permute-done.29.refs_12_ = bf16[256,512]{1,0:T(8,128)(2,1)S(1)} collective-permute-done((bf16[256,512]{1,0:T(8,128)(2,1)S(1)}, bf16[256,512]{1,0:T(8,128)(2,1)S(1)}, u32[]{:S(2)}, u32[]{:S(2)}) %collective-permute-start.29) | collective-permute-done | bytes 262176 | tf_op jit(solution)/shard_map/ppermute | solution.py:39
  137.0 2.3 %shard_map.53 = (f32[256,512]{1,0:T(8,128)S(1)}, bf16[256,4096]{1,0:T(8,128)(2,1)S(1)}, bf16[4096,512]{1,0:T(8,128)(2,1)S(1)}) custom-call(s32[4]{0:T(128)S(1)} %pad_add_fusion.1.where, bf16[256,512]{1,0:T(8,128)(2,1)S(1)} %shard_map.52.refs_0_, bf16[256,512]{1,0:T(8,128)(2,1)S(1)} %collective-permute-done.20.refs_1_, ...), custom_call_target="tpu_custom_call" | custom-call | flops 536870912 | bytes 10485760 | tf_op jit(solution)/shard_map/pallas_call | solution.py:269
  139.3 2.3 %shard_map.54 = (f32[256,512]{1,0:T(8,128)S(1)}, bf16[256,512]{1,0:T(8,128)(2,1)S(1)}, bf16[4096,512]{1,0:T(8,128)(2,1)S(1)}) custom-call(s32[4]{0:T(128)S(1)} %pad_add_fusion.1.where, s32[2,32,32]{2,1,0:T(8,128)S(1)} %copy-done.2, bf16[1024,512]{1,0:T(8,128)(2,1)S(1)} %collective-permute-done.17.one, ...), custom_call_target="tpu_custom_call", output_to_operand_aliasing={{2}: (6, {})} | custom-call | flops 536870912 | bytes 8388608 | tf_op jit(solution)/shard_map/pallas_call | solution.py:269
  142.2 0.9 collective-permute-start.32
  143.0 0.8 collective-permute-start.34
  143.8 0.8 collective-permute-start.36
  144.7 4.9 %collective-permute-done.30.refs_1_ = bf16[256,512]{1,0:T(8,128)(2,1)S(1)} collective-permute-done((bf16[256,512]{1,0:T(8,128)(2,1)S(1)}, bf16[256,512]{1,0:T(8,128)(2,1)S(1)}, u32[]{:S(2)}, u32[]{:S(2)}) %collective-permute-start.30) | collective-permute-done | bytes 262176 | tf_op jit(solution)/shard_map/ppermute | solution.py:35
  149.5 1.2 collective-permute-start.31
  150.7 0.9 collective-permute-done.32.refs_2_
  151.6 1.2 collective-permute-start.33
  152.9 4.7 %collective-permute-done.34.refs_3_ = bf16[256,512]{1,0:T(8,128)(2,1)S(1)} collective-permute-done((bf16[256,512]{1,0:T(8,128)(2,1)S(1)}, bf16[256,512]{1,0:T(8,128)(2,1)S(1)}, u32[]{:S(2)}, u32[]{:S(2)}) %collective-permute-start.34) | collective-permute-done | bytes 262176 | tf_op jit(solution)/shard_map/ppermute | solution.py:35
  158.0 1.4 shard_map.55.refs_3_
  159.4 0.9 shard_map.56
  160.6 1.4 collective-permute-done.37.refs_6_
  162.0 1.7 %shard_map.57 = f32[128,1024]{1,0:T(8,128)} custom-call(s32[4]{0:T(128)S(1)} %pad_add_fusion.1.where, bf16[256,512]{1,0:T(8,128)(2,1)S(1)} %collective-permute-done.31.refs_0_, bf16[256,512]{1,0:T(8,128)(2,1)S(1)} %collective-permute-done.33.refs_1_, bf16[256,512]{1,0:T(8,128)(2,1)S(1)} %collective-permute-done.35.refs_2_, ...), custom_call_target="tpu_custom_call" | custom-call | flops 201326592 | bytes 3145728 | tf_op jit(solution)/shard_map/pallas_call | solution.py:269
  (58 shorter events, 7.7 us)
Async XLA Ops:
  0.0 5.3 %copy-start = (s32[32,8]{0,1:T(8,128)S(1)}, s32[32,8]{0,1:T(8,128)}, u32[]{:S(2)}) copy-start(s32[32,8]{0,1:T(8,128)} %param.5) | copy-start | bytes 3076
  0.0 28.9 %copy-start.1 = (s32[2,32,32]{2,1,0:T(8,128)S(1)}, s32[2,32,32]{2,1,0:T(8,128)}, u32[]{:S(2)}) copy-start(s32[2,32,32]{2,1,0:T(8,128)} %keep_d.11) | copy-start | bytes 24580
  0.0 6.8 %collective-permute-start = (bf16[128,256]{1,0:T(8,128)(2,1)}, bf16[128,256]{1,0:T(8,128)(2,1)S(1)}, u32[]{:S(2)}, u32[]{:S(2)}) collective-permute-start(bf16[128,256]{1,0:T(8,128)(2,1)} %param.4), channel_id=1, source_target_pairs={{0,3},{1,0},{2,1},{3,2},{4,7},{5,4},{6,5},{7,6},{8,11},{9,8},{10,9... | collective-permute-start | bytes 196616 | tf_op jit(solution)/shard_map/ppermute | solution.py:35
  4.6 4.9 %collective-permute-start.1 = (bf16[128,256]{1,0:T(8,128)(2,1)}, bf16[128,256]{1,0:T(8,128)(2,1)S(1)}, u32[]{:S(2)}, u32[]{:S(2)}) collective-permute-start(bf16[128,256]{1,0:T(8,128)(2,1)} %param.4), channel_id=1, source_target_pairs={{0,2},{1,3},{2,0},{3,1},{4,6},{5,7},{6,4},{7,5},{8,10},{9,11},{10,... | collective-permute-start | bytes 196616 | tf_op jit(solution)/shard_map/ppermute | solution.py:35
  4.6 5.2 %collective-permute-start.2 = (bf16[128,256]{1,0:T(8,128)(2,1)}, bf16[128,256]{1,0:T(8,128)(2,1)S(1)}, u32[]{:S(2)}, u32[]{:S(2)}) collective-permute-start(bf16[128,256]{1,0:T(8,128)(2,1)} %param.4), channel_id=1, source_target_pairs={{0,1},{1,2},{2,3},{3,0},{4,5},{5,6},{6,7},{7,4},{8,9},{9,10},{10,1... | collective-permute-start | bytes 196616 | tf_op jit(solution)/shard_map/ppermute | solution.py:35
  10.7 8.9 %collective-permute-start.3 = (bf16[128,1024]{1,0:T(8,128)(2,1)S(1)}, bf16[128,1024]{1,0:T(8,128)(2,1)S(1)}, u32[]{:S(2)}, u32[]{:S(2)}) collective-permute-start(bf16[128,1024]{1,0:T(8,128)(2,1)S(1)} %maximum_multiply_fusion), channel_id=1, source_target_pairs={{0,96},{1,97},{2,98},{3,99},{4,28},{5,29},{6,30},{7,31},{8,104},{9... | collective-permute-start | bytes 786440 | tf_op jit(solution)/shard_map/ppermute | solution.py:39
  13.5 7.1 %collective-permute-start.4 = (bf16[128,1024]{1,0:T(8,128)(2,1)S(1)}, bf16[128,1024]{1,0:T(8,128)(2,1)S(1)}, u32[]{:S(2)}, u32[]{:S(2)}) collective-permute-start(bf16[128,1024]{1,0:T(8,128)(2,1)S(1)} %maximum_multiply_fusion), channel_id=1, source_target_pairs={{0,64},{1,65},{2,66},{3,67},{4,20},{5,21},{6,22},{7,23},{8,72},{9,... | collective-permute-start | bytes 786440 | tf_op jit(solution)/shard_map/ppermute | solution.py:39
  13.9 9.5 %collective-permute-start.5 = (bf16[128,1024]{1,0:T(8,128)(2,1)S(1)}, bf16[128,1024]{1,0:T(8,128)(2,1)S(1)}, u32[]{:S(2)}, u32[]{:S(2)}) collective-permute-start(bf16[128,1024]{1,0:T(8,128)(2,1)S(1)} %maximum_multiply_fusion), channel_id=1, source_target_pairs={{0,32},{1,33},{2,34},{3,35},{4,12},{5,13},{6,14},{7,15},{8,40},{9,... | collective-permute-start | bytes 786440 | tf_op jit(solution)/shard_map/ppermute | solution.py:39
  23.4 5.5 %collective-permute-start.6 = (bf16[512,1024]{1,0:T(8,128)(2,1)S(1)}, bf16[512,1024]{1,0:T(8,128)(2,1)}, u32[]{:S(2)}, u32[]{:S(2)}) collective-permute-start(bf16[512,1024]{1,0:T(8,128)(2,1)S(1)} %pad_maximum_fusion.own0), channel_id=1, source_target_pairs={{0,4},{1,5},{2,6},{3,7},{4,0},{5,1},{6,2},{7,3},{8,12},{9,13},{10,... | collective-permute-start | bytes 3145736 | tf_op jit(solution)/shard_map/ppermute | solution.py:31
  26.5 13.9 %collective-permute-start.7 = (bf16[512,1024]{1,0:T(8,128)(2,1)S(1)}, bf16[512,1024]{1,0:T(8,128)(2,1)S(1)}, u32[]{:S(2)}, u32[]{:S(2)}) collective-permute-start(bf16[512,1024]{1,0:T(8,128)(2,1)S(1)} %pad_maximum_fusion.own0), channel_id=1, source_target_pairs={{0,24},{1,25},{2,26},{3,27},{4,100},{5,101},{6,102},{7,103},{8,0},... | collective-permute-start | bytes 3145736 | tf_op jit(solution)/shard_map/ppermute | solution.py:44
  26.8 26.5 %collective-permute-start.8 = (bf16[512,1024]{1,0:T(8,128)(2,1)S(1)}, bf16[512,1024]{1,0:T(8,128)(2,1)S(1)}, u32[]{:S(2)}, u32[]{:S(2)}) collective-permute-start(bf16[512,1024]{1,0:T(8,128)(2,1)S(1)} %pad_maximum_fusion.own0), channel_id=1, source_target_pairs={{0,8},{1,9},{2,10},{3,11},{4,36},{5,37},{6,38},{7,39},{8,16},{9,17... | collective-permute-start | bytes 3145736 | tf_op jit(solution)/shard_map/ppermute | solution.py:44
  28.0 36.3 %collective-permute-start.9 = (bf16[512,1024]{1,0:T(8,128)(2,1)S(1)}, bf16[512,1024]{1,0:T(8,128)(2,1)}, u32[]{:S(2)}, u32[]{:S(2)}) collective-permute-start(bf16[512,1024]{1,0:T(8,128)(2,1)S(1)} %pad_maximum_fusion.own0), channel_id=1, source_target_pairs={{0,16},{1,17},{2,18},{3,19},{4,68},{5,69},{6,70},{7,71},{8,24},{9,... | collective-permute-start | bytes 3145736 | tf_op jit(solution)/shard_map/ppermute | solution.py:44
  53.3 18.2 %collective-permute-start.11 = (bf16[512,1024]{1,0:T(8,128)(2,1)S(1)}, bf16[512,1024]{1,0:T(8,128)(2,1)S(1)}, u32[]{:S(2)}, u32[]{:S(2)}) collective-permute-start(bf16[512,1024]{1,0:T(8,128)(2,1)S(1)} %collective-permute-done.7.own1), channel_id=1, source_target_pairs={{0,4},{1,5},{2,6},{3,7},{4,0},{5,1},{6,2},{7,3},{8,12},{9,13},{10,... | collective-permute-start | bytes 3145736 | tf_op jit(solution)/shard_map/ppermute | solution.py:31
  56.8 14.7 %collective-permute-start.12 = (bf16[512,1024]{1,0:T(8,128)(2,1)S(1)}, bf16[512,1024]{1,0:T(8,128)(2,1)S(1)}, u32[]{:S(2)}, u32[]{:S(2)}) collective-permute-start(bf16[512,1024]{1,0:T(8,128)(2,1)S(1)} %collective-permute-done.8.own3), channel_id=1, source_target_pairs={{0,4},{1,5},{2,6},{3,7},{4,0},{5,1},{6,2},{7,3},{8,12},{9,13},{10,... | collective-permute-start | bytes 3145736 | tf_op jit(solution)/shard_map/ppermute | solution.py:31
  64.3 13.6 %collective-permute-start.10 = (bf16[512,1024]{1,0:T(8,128)(2,1)}, bf16[512,1024]{1,0:T(8,128)(2,1)S(1)}, u32[]{:S(2)}, u32[]{:S(2)}) collective-permute-start(bf16[512,1024]{1,0:T(8,128)(2,1)} %collective-permute-done.9.own2), channel_id=1, source_target_pairs={{0,4},{1,5},{2,6},{3,7},{4,0},{5,1},{6,2},{7,3},{8,12},{9,13},{10,... | collective-permute-start | bytes 3145736 | tf_op jit(solution)/shard_map/ppermute | solution.py:31
  71.5 6.4 %copy-start.2 = (s32[2,32,32]{2,1,0:T(8,128)S(1)}, s32[2,32,32]{2,1,0:T(8,128)}, u32[]{:S(2)}) copy-start(s32[2,32,32]{2,1,0:T(8,128)} %keep_s.3) | copy-start | bytes 24580
  96.9 2.7 %collective-permute-start.13 = (bf16[256,2048]{1,0:T(8,128)(2,1)S(1)}, bf16[256,2048]{1,0:T(8,128)(2,1)S(1)}, u32[]{:S(2)}, u32[]{:S(2)}) collective-permute-start(bf16[256,2048]{1,0:T(8,128)(2,1)S(1)} %get-tuple-element.53.low), channel_id=1, source_target_pairs={{0,4},{1,5},{2,6},{3,7},{4,0},{5,1},{6,2},{7,3},{8,12},{9,13},{10,... | collective-permute-start | bytes 3145736 | tf_op jit(solution)/shard_map/ppermute | solution.py:31
  101.5 6.7 %collective-permute-start.14 = (bf16[256,512]{1,0:T(8,128)(2,1)S(1)}, bf16[256,512]{1,0:T(8,128)(2,1)S(1)}, u32[]{:S(2)}, u32[]{:S(2)}) collective-permute-start(bf16[256,512]{1,0:T(8,128)(2,1)S(1)} %shard_map.52.refs_0_), channel_id=1, source_target_pairs={{0,96},{1,97},{2,98},{3,99},{4,28},{5,29},{6,30},{7,31},{8,104},{9... | collective-permute-start | bytes 786440 | tf_op jit(solution)/shard_map/ppermute | solution.py:39
  101.6 7.9 %collective-permute-start.15 = (bf16[256,512]{1,0:T(8,128)(2,1)S(1)}, bf16[256,512]{1,0:T(8,128)(2,1)S(1)}, u32[]{:S(2)}, u32[]{:S(2)}) collective-permute-start(bf16[256,512]{1,0:T(8,128)(2,1)S(1)} %shard_map.52.refs_0_), channel_id=1, source_target_pairs={{0,64},{1,65},{2,66},{3,67},{4,20},{5,21},{6,22},{7,23},{8,72},{9,... | collective-permute-start | bytes 786440 | tf_op jit(solution)/shard_map/ppermute | solution.py:39
  101.7 12.6 %collective-permute-start.16 = (bf16[256,512]{1,0:T(8,128)(2,1)S(1)}, bf16[256,512]{1,0:T(8,128)(2,1)S(1)}, u32[]{:S(2)}, u32[]{:S(2)}) collective-permute-start(bf16[256,512]{1,0:T(8,128)(2,1)S(1)} %shard_map.52.refs_0_), channel_id=1, source_target_pairs={{0,32},{1,33},{2,34},{3,35},{4,12},{5,13},{6,14},{7,15},{8,40},{9,... | collective-permute-start | bytes 786440 | tf_op jit(solution)/shard_map/ppermute | solution.py:39
  103.0 11.4 %collective-permute-start.19 = (bf16[256,512]{1,0:T(8,128)(2,1)S(1)}, bf16[256,512]{1,0:T(8,128)(2,1)S(1)}, u32[]{:S(2)}, u32[]{:S(2)}) collective-permute-start(bf16[256,512]{1,0:T(8,128)(2,1)S(1)} %shard_map.52.refs_0_), channel_id=1, source_target_pairs={{0,16},{1,17},{2,18},{3,19},{4,68},{5,69},{6,70},{7,71},{8,24},{9,... | collective-permute-start | bytes 786440 | tf_op jit(solution)/shard_map/ppermute | solution.py:44
  103.5 12.4 %collective-permute-start.20 = (bf16[256,512]{1,0:T(8,128)(2,1)S(1)}, bf16[256,512]{1,0:T(8,128)(2,1)S(1)}, u32[]{:S(2)}, u32[]{:S(2)}) collective-permute-start(bf16[256,512]{1,0:T(8,128)(2,1)S(1)} %shard_map.52.refs_0_), channel_id=1, source_target_pairs={{0,3},{1,0},{2,1},{3,2},{4,7},{5,4},{6,5},{7,6},{8,11},{9,8},{10,9... | collective-permute-start | bytes 786440 | tf_op jit(solution)/shard_map/ppermute | solution.py:35
  108.1 7.8 %collective-permute-start.21 = (bf16[256,512]{1,0:T(8,128)(2,1)S(1)}, bf16[256,512]{1,0:T(8,128)(2,1)S(1)}, u32[]{:S(2)}, u32[]{:S(2)}) collective-permute-start(bf16[256,512]{1,0:T(8,128)(2,1)S(1)} %shard_map.52.refs_0_), channel_id=1, source_target_pairs={{0,2},{1,3},{2,0},{3,1},{4,6},{5,7},{6,4},{7,5},{8,10},{9,11},{10,... | collective-permute-start | bytes 786440 | tf_op jit(solution)/shard_map/ppermute | solution.py:35
  109.5 13.0 %collective-permute-start.22 = (bf16[256,512]{1,0:T(8,128)(2,1)S(1)}, bf16[256,512]{1,0:T(8,128)(2,1)S(1)}, u32[]{:S(2)}, u32[]{:S(2)}) collective-permute-start(bf16[256,512]{1,0:T(8,128)(2,1)S(1)} %shard_map.52.refs_0_), channel_id=1, source_target_pairs={{0,1},{1,2},{2,3},{3,0},{4,5},{5,6},{6,7},{7,4},{8,9},{9,10},{10,1... | collective-permute-start | bytes 786440 | tf_op jit(solution)/shard_map/ppermute | solution.py:35
  114.4 24.9 %collective-permute-start.17 = (bf16[1024,512]{1,0:T(8,128)(2,1)S(1)}, bf16[1024,512]{1,0:T(8,128)(2,1)S(1)}, u32[]{:S(2)}, u32[]{:S(2)}) collective-permute-start(bf16[1024,512]{1,0:T(8,128)(2,1)S(1)} %pad_maximum_fusion.1.refs_8_), channel_id=1, source_target_pairs={{0,24},{1,25},{2,26},{3,27},{4,100},{5,101},{6,102},{7,103},{8,0},... | collective-permute-start | bytes 3145736 | tf_op jit(solution)/shard_map/ppermute | solution.py:44
  114.4 24.8 %collective-permute-start.18 = (bf16[1024,512]{1,0:T(8,128)(2,1)S(1)}, bf16[1024,512]{1,0:T(8,128)(2,1)S(1)}, u32[]{:S(2)}, u32[]{:S(2)}) collective-permute-start(bf16[1024,512]{1,0:T(8,128)(2,1)S(1)} %pad_maximum_fusion.1.refs_8_), channel_id=1, source_target_pairs={{0,8},{1,9},{2,10},{3,11},{4,36},{5,37},{6,38},{7,39},{8,16},{9,17... | collective-permute-start | bytes 3145736 | tf_op jit(solution)/shard_map/ppermute | solution.py:44
  122.4 2.7 %collective-permute-start.23 = (bf16[256,512]{1,0:T(8,128)(2,1)S(1)}, bf16[256,512]{1,0:T(8,128)(2,1)S(1)}, u32[]{:S(2)}, u32[]{:S(2)}) collective-permute-start(bf16[256,512]{1,0:T(8,128)(2,1)S(1)} %shard_map.52.refs_0_), channel_id=1, source_target_pairs={{0,4},{1,5},{2,6},{3,7},{4,0},{5,1},{6,2},{7,3},{8,12},{9,13},{10,... | collective-permute-start | bytes 786440 | tf_op jit(solution)/shard_map/ppermute | solution.py:31
  124.0 1.5 collective-permute-start.24
  124.0 1.9 %collective-permute-start.25 = (bf16[256,512]{1,0:T(8,128)(2,1)S(1)}, bf16[256,512]{1,0:T(8,128)(2,1)S(1)}, u32[]{:S(2)}, u32[]{:S(2)}) collective-permute-start(bf16[256,512]{1,0:T(8,128)(2,1)S(1)} %collective-permute-done.21.refs_2_), channel_id=1, source_target_pairs={{0,4},{1,5},{2,6},{3,7},{4,0},{5,1},{6,2},{7,3},{8,12},{9,13},{10,... | collective-permute-start | bytes 786440 | tf_op jit(solution)/shard_map/ppermute | solution.py:31
  125.1 1.5 collective-permute-start.26
  125.5 7.6 %collective-permute-start.27 = (bf16[256,512]{1,0:T(8,128)(2,1)S(1)}, bf16[256,512]{1,0:T(8,128)(2,1)S(1)}, u32[]{:S(2)}, u32[]{:S(2)}) collective-permute-start(bf16[256,512]{1,0:T(8,128)(2,1)S(1)} %collective-permute-done.19.refs_9_), channel_id=1, source_target_pairs={{0,96},{1,97},{2,98},{3,99},{4,28},{5,29},{6,30},{7,31},{8,104},{9... | collective-permute-start | bytes 786440 | tf_op jit(solution)/shard_map/ppermute | solution.py:39
  125.9 7.3 %collective-permute-start.28 = (bf16[256,512]{1,0:T(8,128)(2,1)S(1)}, bf16[256,512]{1,0:T(8,128)(2,1)S(1)}, u32[]{:S(2)}, u32[]{:S(2)}) collective-permute-start(bf16[256,512]{1,0:T(8,128)(2,1)S(1)} %collective-permute-done.19.refs_9_), channel_id=1, source_target_pairs={{0,64},{1,65},{2,66},{3,67},{4,20},{5,21},{6,22},{7,23},{8,72},{9,... | collective-permute-start | bytes 786440 | tf_op jit(solution)/shard_map/ppermute | solution.py:39
  126.7 10.3 %collective-permute-start.29 = (bf16[256,512]{1,0:T(8,128)(2,1)S(1)}, bf16[256,512]{1,0:T(8,128)(2,1)S(1)}, u32[]{:S(2)}, u32[]{:S(2)}) collective-permute-start(bf16[256,512]{1,0:T(8,128)(2,1)S(1)} %collective-permute-done.19.refs_9_), channel_id=1, source_target_pairs={{0,32},{1,33},{2,34},{3,35},{4,12},{5,13},{6,14},{7,15},{8,40},{9,... | collective-permute-start | bytes 786440 | tf_op jit(solution)/shard_map/ppermute | solution.py:39
  141.5 8.0 %collective-permute-start.30 = (bf16[256,512]{1,0:T(8,128)(2,1)S(1)}, bf16[256,512]{1,0:T(8,128)(2,1)S(1)}, u32[]{:S(2)}, u32[]{:S(2)}) collective-permute-start(bf16[256,512]{1,0:T(8,128)(2,1)S(1)} %get-tuple-element.66.refs_0_), channel_id=1, source_target_pairs={{0,3},{1,0},{2,1},{3,2},{4,7},{5,4},{6,5},{7,6},{8,11},{9,8},{10,9... | collective-permute-start | bytes 786440 | tf_op jit(solution)/shard_map/ppermute | solution.py:35
  142.2 9.5 %collective-permute-start.32 = (bf16[256,512]{1,0:T(8,128)(2,1)S(1)}, bf16[256,512]{1,0:T(8,128)(2,1)S(1)}, u32[]{:S(2)}, u32[]{:S(2)}) collective-permute-start(bf16[256,512]{1,0:T(8,128)(2,1)S(1)} %get-tuple-element.66.refs_0_), channel_id=1, source_target_pairs={{0,2},{1,3},{2,0},{3,1},{4,6},{5,7},{6,4},{7,5},{8,10},{9,11},{10,... | collective-permute-start | bytes 786440 | tf_op jit(solution)/shard_map/ppermute | solution.py:35
  143.0 14.5 %collective-permute-start.34 = (bf16[256,512]{1,0:T(8,128)(2,1)S(1)}, bf16[256,512]{1,0:T(8,128)(2,1)S(1)}, u32[]{:S(2)}, u32[]{:S(2)}) collective-permute-start(bf16[256,512]{1,0:T(8,128)(2,1)S(1)} %get-tuple-element.66.refs_0_), channel_id=1, source_target_pairs={{0,1},{1,2},{2,3},{3,0},{4,5},{5,6},{6,7},{7,4},{8,9},{9,10},{10,1... | collective-permute-start | bytes 786440 | tf_op jit(solution)/shard_map/ppermute | solution.py:35
  143.8 14.2 %collective-permute-start.36 = (bf16[256,512]{1,0:T(8,128)(2,1)S(1)}, bf16[256,512]{1,0:T(8,128)(2,1)S(1)}, u32[]{:S(2)}, u32[]{:S(2)}) collective-permute-start(bf16[256,512]{1,0:T(8,128)(2,1)S(1)} %get-tuple-element.66.refs_0_), channel_id=1, source_target_pairs={{0,4},{1,5},{2,6},{3,7},{4,0},{5,1},{6,2},{7,3},{8,12},{9,13},{10,... | collective-permute-start | bytes 786440 | tf_op jit(solution)/shard_map/ppermute | solution.py:31
  149.5 9.9 %collective-permute-start.31 = (bf16[256,512]{1,0:T(8,128)(2,1)S(1)}, bf16[256,512]{1,0:T(8,128)(2,1)S(1)}, u32[]{:S(2)}, u32[]{:S(2)}) collective-permute-start(bf16[256,512]{1,0:T(8,128)(2,1)S(1)} %collective-permute-done.30.refs_1_), channel_id=1, source_target_pairs={{0,4},{1,5},{2,6},{3,7},{4,0},{5,1},{6,2},{7,3},{8,12},{9,13},{10,... | collective-permute-start | bytes 786440 | tf_op jit(solution)/shard_map/ppermute | solution.py:31
  151.6 7.8 %collective-permute-start.33 = (bf16[256,512]{1,0:T(8,128)(2,1)S(1)}, bf16[256,512]{1,0:T(8,128)(2,1)S(1)}, u32[]{:S(2)}, u32[]{:S(2)}) collective-permute-start(bf16[256,512]{1,0:T(8,128)(2,1)S(1)} %collective-permute-done.32.refs_2_), channel_id=1, source_target_pairs={{0,4},{1,5},{2,6},{3,7},{4,0},{5,1},{6,2},{7,3},{8,12},{9,13},{10,... | collective-permute-start | bytes 786440 | tf_op jit(solution)/shard_map/ppermute | solution.py:31
  157.5 1.9 %collective-permute-start.35 = (bf16[256,512]{1,0:T(8,128)(2,1)S(1)}, bf16[256,512]{1,0:T(8,128)(2,1)S(1)}, u32[]{:S(2)}, u32[]{:S(2)}) collective-permute-start(bf16[256,512]{1,0:T(8,128)(2,1)S(1)} %collective-permute-done.34.refs_3_), channel_id=1, source_target_pairs={{0,4},{1,5},{2,6},{3,7},{4,0},{5,1},{6,2},{7,3},{8,12},{9,13},{10,... | collective-permute-start | bytes 786440 | tf_op jit(solution)/shard_map/ppermute | solution.py:31
  160.4 1.6 collective-permute-start.37
